TPU v7x, 32 devices: a whole 2x2x4 slice. The times are simulated.
32 devices in a mesh: img: 4 (over y, x), tile: 8 (over z, core).
Axes of the slice: x: 2, y: 2, z: 4, core: 2. Of those that a mesh axis runs over, the one named last changes fastest.
Arguments:
- patches: bfloat16 [32, 32, 32, 768], P(('img', 'tile')), may hold values from -6 to 6
- norm_gain: float32 [768], replicated, may hold values from 0.1 to 1.9
- norm_bias: float32 [768], replicated, may hold values from -3 to 3
- up_weight: bfloat16 [768, 3072], replicated, may hold values from -0.21875 to 0.21875
- up_bias: float32 [3072], replicated, may hold values from -3 to 3
- down_weight: bfloat16 [3072, 768], replicated, may hold values from -0.109375 to 0.109375
- down_bias: float32 [768], replicated, may hold values from -3 to 3
- final_gain: float32 [768], replicated, may hold values from 0.1 to 1.9
- final_bias: float32 [768], replicated, may hold values from -3 to 3
- head_weight: bfloat16 [768, 512], replicated, may hold values from -0.21875 to 0.21875
- gauss_rows: bfloat16 [65536, 512], P(('img', 'tile')), may hold values from -48 to 48
- tile_lists: int32 [32, 32, 128], P('img', 'tile'), may hold values from 0 to 65535, as said below
- alphas: float32 [32, 32, 32, 128], P('img', 'tile'), may hold values from 0.002 to 0.05
Outputs:
- rendered: bfloat16 [32, 32, 32, 512], P('img', 'tile')
- feature_grad: float32 [65536, 512], P(('img', 'tile'))
Inputs may be any that keep to these rules, and one draw needn't show every extreme that they name: `tile_lists`: among the 4096 entries of the tiles held by one device (one index of img and of tile), at most 256 name Gaussians held by any one device, the holder of id g being index g // 2048 of img+tile.
All inputs are finite; a program needn't handle non-finite values.
Results may differ from a plain program's by a relative error of at most 0.0049.
Values may be sent and summed in bfloat16 or wider, within the bound.
No kernel may reach another device: no remote copies, remote signals or barrier semaphores. Data moves between devices by JAX's collectives and lax.ppermute only.
A program may use at most 128 MiB of HBM per device.

v0:
```python
import math

import jax
import jax.numpy as jnp
from jax import lax
from jax.sharding import PartitionSpec as P


def layer_norm(rows, gain, bias):
    mean = jnp.mean(rows, axis=-1, keepdims=True)
    centred = rows - mean
    var = jnp.mean(centred * centred, axis=-1, keepdims=True)
    return centred * lax.rsqrt(var + 1e-05) * gain + bias


def slot_ranks(owner, peers):
    entries = owner.shape[0]
    block = math.gcd(entries, 512)
    nblocks = entries // block
    onehot = (owner[:, None] == jnp.arange(peers, dtype=jnp.int32)[None, :]).astype(jnp.bfloat16)
    onehot = onehot.reshape(nblocks, block, peers)
    rowpos = lax.broadcasted_iota(jnp.int32, (block, block), 0)
    colpos = lax.broadcasted_iota(jnp.int32, (block, block), 1)
    lower = (rowpos > colpos).astype(jnp.bfloat16)
    within = jnp.einsum("ij,bjp->bip", lower, onehot, preferred_element_type=jnp.float32)
    totals = jnp.sum(onehot.astype(jnp.float32), axis=1)
    offsets = jnp.cumsum(totals, axis=0) - totals
    counted = jnp.sum((within + offsets[:, None, :]) * onehot.astype(jnp.float32), axis=-1)
    return counted.reshape(entries).astype(jnp.int32)


def on_device(
    patches,
    norm_gain,
    norm_bias,
    up_weight,
    up_bias,
    down_weight,
    down_bias,
    final_gain,
    final_bias,
    head_weight,
    gauss_rows,
    tile_lists,
    alphas,
):
    view_count, tiles_view, cells, width = patches.shape
    feat_width = head_weight.shape[1]
    wide = patches.reshape(-1, width).astype(jnp.float32)
    normed = layer_norm(wide, norm_gain, norm_bias).astype(jnp.bfloat16)
    inner = jnp.dot(normed, up_weight, preferred_element_type=jnp.float32) + up_bias
    act = (inner * jax.nn.sigmoid(1.702 * inner)).astype(jnp.bfloat16)
    block_out = wide + jnp.dot(act, down_weight, preferred_element_type=jnp.float32) + down_bias
    final = layer_norm(block_out, final_gain, final_bias).astype(jnp.bfloat16)
    embed = jnp.dot(final, head_weight, preferred_element_type=jnp.float32)
    scale = lax.rsqrt(jnp.mean(embed * embed, axis=-1, keepdims=True) + 1e-06)
    target = (embed * scale).astype(jnp.bfloat16).reshape(view_count, tiles_view, cells, feat_width)
    target = lax.all_to_all(target, "tile", split_axis=1, concat_axis=0, tiled=True)
    n_img = lax.axis_size("img")
    n_tile = lax.axis_size("tile")
    peers = n_img * n_tile
    rows_held = gauss_rows.shape[0]
    group_views, strip_tiles, list_len = tile_lists.shape
    entries = group_views * strip_tiles * list_len
    capacity = 2 * entries // peers
    slot_total = peers * capacity
    flat_ids = tile_lists.reshape(-1)
    owner = flat_ids // rows_held
    local_row = flat_ids - owner * rows_held
    place = owner * capacity + slot_ranks(owner, peers)
    slot_entry = (
        jnp.full((slot_total,), -1, jnp.int32).at[place].set(jnp.arange(entries, dtype=jnp.int32))
    )
    filled = slot_entry >= 0
    source = jnp.maximum(slot_entry, 0)
    request = jnp.where(filled, local_row[source], 0).reshape(peers, capacity)
    asked = lax.all_to_all(request, ("img", "tile"), split_axis=0, concat_axis=0, tiled=True)
    looked = gauss_rows[asked]
    returned = lax.all_to_all(looked, ("img", "tile"), split_axis=0, concat_axis=0, tiled=True)
    fetched_rows = returned
    fetched_rows = fetched_rows.reshape(slot_total, feat_width)
    entry_rows = fetched_rows[place].reshape(group_views, strip_tiles, list_len, feat_width)
    logs = jnp.log1p(-alphas)
    trans = jnp.exp(jnp.cumsum(logs, axis=-1) - logs)
    weight = (alphas * trans).astype(jnp.bfloat16)
    color = jnp.einsum("vtpl,vtlf->vtpf", weight, entry_rows, preferred_element_type=jnp.float32)
    rendered = color.astype(jnp.bfloat16)
    diff = (color - target.astype(jnp.float32)).astype(jnp.bfloat16)
    term = jnp.einsum("vtpl,vtpf->vtlf", weight, diff, preferred_element_type=jnp.float32).astype(
        jnp.bfloat16
    )
    term_flat = term.reshape(entries, feat_width)
    outgoing = jnp.where(filled[:, None], term_flat[source], jnp.zeros((), jnp.bfloat16))
    incoming = lax.all_to_all(
        outgoing.reshape(peers, capacity, feat_width),
        ("img", "tile"),
        split_axis=0,
        concat_axis=0,
        tiled=True,
    )
    incoming = incoming.reshape(slot_total, feat_width)
    target_rows = asked.reshape(-1)
    row_block = math.gcd(rows_held, 256)

    def add_block(first):
        local_ids = first + jnp.arange(row_block, dtype=jnp.int32)
        select = (local_ids[:, None] == target_rows[None, :]).astype(jnp.bfloat16)
        return jnp.dot(select, incoming, preferred_element_type=jnp.float32)

    starts = jnp.arange(rows_held // row_block, dtype=jnp.int32) * row_block
    feature_grad = lax.map(add_block, starts).reshape(rows_held, feat_width)
    return (rendered, feature_grad)


def solution(mesh):
    placed = (
        P(("img", "tile"), None, None, None),
        P(),
        P(),
        P(),
        P(),
        P(),
        P(),
        P(),
        P(),
        P(),
        P(("img", "tile"), None),
        P("img", "tile", None),
        P("img", "tile", None, None),
    )
    return jax.shard_map(
        on_device,
        mesh=mesh,
        in_specs=placed,
        out_specs=(P("img", "tile", None, None), P(("img", "tile"), None)),
        check_vma=False,
    )
```

profile of v0, /device:TPU:0, one launch (start us, length us, event | category | flops | bytes accessed | tf_op | source)
XLA Modules:
  0.0 642.3 jit_solution(15487832787106695686)
XLA Ops:
  0.6 0.0 copy-start
  0.6 0.9 add_select_fusion.1
  1.5 0.1 convert_reduce_fusion.1
  1.7 0.4 fusion.24
  2.1 0.8 compare_select_fusion.1
  2.9 15.5 %scatter_custom_fusion = s32[8192]{0:T(1024)S(1)} fusion(s32[4096]{0:T(1024)S(1)} %bitcast.98, s32[4096]{0:T(1024)S(1)} %iota.34, s32[]{:T(128)} %constant.25.clone.1), kind=kCustom, calls=%fused_computation.77 | custom fusion | bytes 32772 | tf_op jit(solution)/shard_map/scatter | solution.py:72
  18.5 0.7 fusion.33
  19.3 45.5 %gather_fusion = s32[8192]{0:T(1024)S(1)} fusion(s32[4096]{0:T(1024)S(1)} %fusion.33, s32[8192]{0:T(1024)S(1)} %maximum_clamp_fusion), kind=kCustom, calls=%fused_computation | custom fusion | bytes 98304 | tf_op jit(solution)/shard_map/gather | solution.py:76
  64.8 14.3 %all_to_all.34 = s32[32,1,256]{2,1,0:T(1,128)S(1)} all-to-all(s32[32,1,256]{2,1,0:T(1,128)S(1)} %bitcast.96), channel_id=1, replica_groups=mesh['img'=4,'tile'=8] {'img','tile'}, dimensions={0} | all-to-all | bytes 65536 | tf_op jit(solution)/shard_map/all_to_all | solution.py:77
  79.2 33.6 %gather_fusion.1 = bf16[8192,512]{1,0:T(8,128)(2,1)} fusion(bf16[2048,512]{1,0:T(8,128)(2,1)S(1)} %copy-done, s32[8192]{0:T(1024)S(1)} %broadcast_clamp_fusion), kind=kCustom, calls=%fused_computation.1 | custom fusion | bytes 16809984 | tf_op jit(solution)/shard_map/gather | solution.py:78
  112.8 3.8 all-to-all-start.1
  116.6 0.0 copy-start.4
  116.6 0.0 copy-start.5
  116.6 0.0 copy-start.6
  116.6 0.0 copy-start.7
  116.7 2.1 copy.17
  118.8 0.3 convert_reduce_fusion
  119.1 0.1 div.64
  119.1 0.6 multiply_reduce_fusion.1
  119.7 0.1 rsqrt.28
  119.8 0.0 copy-start.3
  119.8 0.0 copy-start.8
  119.9 16.8 %fusion.42 = (f32[1024]{0:T(1024)S(1)}, f32[1024,768]{0,1:T(8,128)}) fusion(f32[768]{0:T(1024)S(1)} %copy-done.5, f32[1024,768]{0,1:T(8,128)} %copy.17, bf16[3072,768]{1,0:T(8,128)(2,1)} %param.20, f32[3072]{0:T(1024)S(1)} %copy-done.4, bf16[768,3072]{1,0:T(8,128)(2,1)} %param.18, f32[768]{0:T(1024)S(1)} %copy-done.6, f32[768]{0:T(1024)S(1)} %copy-done.7, ...), kind=kOutput, calls=%fused_computation.90 | convolution fusion | flops 9692773376 | bytes 17335296 | tf_op jit(solution)/shard_map/dot_general | solution.py:53
  136.7 2.3 multiply_reduce_fusion
  139.0 3.4 multiply_reduce_fusion.2
  142.4 1.2 multiply_convert_fusion.2
  143.6 157.9 %all-to-all-done.1 = bf16[32,256,512]{2,1,0:T(8,128)(2,1)} async-done(((bf16[32,256,512]{2,1,0:T(8,128)(2,1)}), bf16[32,256,512]{2,1,0:T(8,128)(2,1)}, u32[]{:S(2)}, u32[]{:S(2)}) %all-to-all-start.1) | async-done | bytes 8388640 | tf_op jit(solution)/shard_map/all_to_all | solution.py:79
  301.5 3.6 all-to-all-start.2
  305.1 1.2 negate_log-plus-one_fusion
  306.3 9.2 %reduce_window_sum.22 = f32[8,4,32,128]{3,2,1,0:T(8,128)S(1)} reduce-window(f32[8,4,32,128]{3,2,1,0:T(8,128)S(1)} %negate_log-plus-one_fusion, f32[]{:T(128)} %constant.22.clone.1), window={size=1x1x1x128 pad=0_0x0_0x0_0x127_0}, to_apply=%region_0.0 | reduce-window | flops 16646144 | bytes 1048580 | tf_op jit(solution)/shard_map/jit(cumsum)/reduce_window_sum | solution.py:84
  315.6 1.3 multiply_convert_fusion.5
  316.9 21.9 %gather_fusion.2 = bf16[4096,512]{1,0:T(8,128)(2,1)} fusion(bf16[8192,512]{1,0:T(8,128)(2,1)} %bitcast.11, s32[4096]{0:T(1024)S(1)} %broadcast_clamp_fusion.1), kind=kCustom, calls=%fused_computation.2 | custom fusion | bytes 8404992 | tf_op jit(solution)/shard_map/gather | solution.py:82
  338.8 3.8 fusion.41
  342.6 3.3 convolution_convert_fusion
  345.9 36.5 %gather_fusion.3 = bf16[8192,512]{1,0:T(8,128)(2,1)} fusion(bf16[4096,512]{1,0:T(8,128)(2,1)} %bitcast.83, s32[8192]{0:T(1024)S(1)} %maximum_clamp_fusion), kind=kCustom, calls=%fused_computation.3 | custom fusion | bytes 16809984 | tf_op jit(solution)/shard_map/gather | solution.py:93
  382.4 7.4 %broadcast_select_fusion = bf16[32,256,512]{2,1,0:T(8,128)(2,1)} fusion(bf16[32,256,512]{2,1,0:T(8,128)(2,1)} %bitcast.85, pred[32,256]{1,0:T(8,128)(4,1)S(1)} %broadcast_in_dim.24), kind=kLoop, calls=%fused_computation.13 | loop fusion | flops 4194304 | bytes 16785408 | tf_op jit(solution)/shard_map/jit(_where)/select_n | solution.py:93
  389.9 4.2 all-to-all-start.3
  394.1 184.9 %all-to-all-done.3 = bf16[32,256,512]{2,1,0:T(8,128)(2,1)} async-done(((bf16[32,256,512]{2,1,0:T(8,128)(2,1)}), bf16[32,256,512]{2,1,0:T(8,128)(2,1)}, u32[]{:S(2)}, u32[]{:S(2)}) %all-to-all-start.3) | async-done | bytes 8388640 | tf_op jit(solution)/shard_map/all_to_all | solution.py:94
  579.0 61.7 %while.10 = (s32[]{:T(128)}, f32[8,256,512]{2,1,0:T(8,128)}, s32[8]{0:T(128)S(1)}, s32[32,256]{1,0:T(8,128)S(1)}, bf16[8192,512]{1,0:T(8,128)(2,1)}, /*index=5*/s32[]{:T(128)}) while((s32[]{:T(128)}, f32[8,256,512]{2,1,0:T(8,128)}, s32[8]{0:T(128)S(1)}, s32[32,256]{1,0:T(8,128)S(1)}, bf16[8192,512]{1,0:T(8,128)(2,1)}, ...), condition=%wide.region_11.12_spmd, body=%wide.region_10.11_spmd.sunk | while | flops 2149581056 | bytes 9013845 | solution.py:111
  579.0 0.6 dynamic_slice.5
  579.6 0.6 iota_add_fusion.2
  580.2 6.6 %fusion.60 = f32[8,256,512]{2,1,0:T(8,128)} fusion(f32[8,256,512]{2,1,0:T(8,128)} %get-tuple-element.86, s32[]{:T(128)} %get-tuple-element.85, bf16[8192,512]{1,0:T(8,128)(2,1)} %get-tuple-element.95, s32[8192]{0:T(1024)S(1)} %bitcast.92, s32[256]{0:T(256)S(1)} %iota_add_fusion.2), kind=kOutput, calls=%fused_computation.10.clone.1 | convolution fusion | flops 2149580800 | bytes 8947200 | tf_op jit(solution)/shard_map/while/body/eval_jaxpr/dot_general | solution.py:108
  586.7 0.6 dynamic_slice.5
  587.3 0.6 iota_add_fusion.2
  587.9 6.5 %fusion.60 = f32[8,256,512]{2,1,0:T(8,128)} fusion(f32[8,256,512]{2,1,0:T(8,128)} %get-tuple-element.86, s32[]{:T(128)} %get-tuple-element.85, bf16[8192,512]{1,0:T(8,128)(2,1)} %get-tuple-element.95, s32[8192]{0:T(1024)S(1)} %bitcast.92, s32[256]{0:T(256)S(1)} %iota_add_fusion.2), kind=kOutput, calls=%fused_computation.10.clone.1 | convolution fusion | flops 2149580800 | bytes 8947200 | tf_op jit(solution)/shard_map/while/body/eval_jaxpr/dot_general | solution.py:108
  594.4 0.6 dynamic_slice.5
  595.0 0.6 iota_add_fusion.2
  595.6 6.6 %fusion.60 = f32[8,256,512]{2,1,0:T(8,128)} fusion(f32[8,256,512]{2,1,0:T(8,128)} %get-tuple-element.86, s32[]{:T(128)} %get-tuple-element.85, bf16[8192,512]{1,0:T(8,128)(2,1)} %get-tuple-element.95, s32[8192]{0:T(1024)S(1)} %bitcast.92, s32[256]{0:T(256)S(1)} %iota_add_fusion.2), kind=kOutput, calls=%fused_computation.10.clone.1 | convolution fusion | flops 2149580800 | bytes 8947200 | tf_op jit(solution)/shard_map/while/body/eval_jaxpr/dot_general | solution.py:108
  602.1 0.6 dynamic_slice.5
  602.7 0.6 iota_add_fusion.2
  603.3 6.5 %fusion.60 = f32[8,256,512]{2,1,0:T(8,128)} fusion(f32[8,256,512]{2,1,0:T(8,128)} %get-tuple-element.86, s32[]{:T(128)} %get-tuple-element.85, bf16[8192,512]{1,0:T(8,128)(2,1)} %get-tuple-element.95, s32[8192]{0:T(1024)S(1)} %bitcast.92, s32[256]{0:T(256)S(1)} %iota_add_fusion.2), kind=kOutput, calls=%fused_computation.10.clone.1 | convolution fusion | flops 2149580800 | bytes 8947200 | tf_op jit(solution)/shard_map/while/body/eval_jaxpr/dot_general | solution.py:108
  609.9 0.6 dynamic_slice.5
  610.4 0.6 iota_add_fusion.2
  611.0 6.5 %fusion.60 = f32[8,256,512]{2,1,0:T(8,128)} fusion(f32[8,256,512]{2,1,0:T(8,128)} %get-tuple-element.86, s32[]{:T(128)} %get-tuple-element.85, bf16[8192,512]{1,0:T(8,128)(2,1)} %get-tuple-element.95, s32[8192]{0:T(1024)S(1)} %bitcast.92, s32[256]{0:T(256)S(1)} %iota_add_fusion.2), kind=kOutput, calls=%fused_computation.10.clone.1 | convolution fusion | flops 2149580800 | bytes 8947200 | tf_op jit(solution)/shard_map/while/body/eval_jaxpr/dot_general | solution.py:108
  617.6 0.6 dynamic_slice.5
  618.1 0.6 iota_add_fusion.2
  618.7 6.5 %fusion.60 = f32[8,256,512]{2,1,0:T(8,128)} fusion(f32[8,256,512]{2,1,0:T(8,128)} %get-tuple-element.86, s32[]{:T(128)} %get-tuple-element.85, bf16[8192,512]{1,0:T(8,128)(2,1)} %get-tuple-element.95, s32[8192]{0:T(1024)S(1)} %bitcast.92, s32[256]{0:T(256)S(1)} %iota_add_fusion.2), kind=kOutput, calls=%fused_computation.10.clone.1 | convolution fusion | flops 2149580800 | bytes 8947200 | tf_op jit(solution)/shard_map/while/body/eval_jaxpr/dot_general | solution.py:108
  625.3 0.6 dynamic_slice.5
  625.8 0.6 iota_add_fusion.2
  626.4 6.6 %fusion.60 = f32[8,256,512]{2,1,0:T(8,128)} fusion(f32[8,256,512]{2,1,0:T(8,128)} %get-tuple-element.86, s32[]{:T(128)} %get-tuple-element.85, bf16[8192,512]{1,0:T(8,128)(2,1)} %get-tuple-element.95, s32[8192]{0:T(1024)S(1)} %bitcast.92, s32[256]{0:T(256)S(1)} %iota_add_fusion.2), kind=kOutput, calls=%fused_computation.10.clone.1 | convolution fusion | flops 2149580800 | bytes 8947200 | tf_op jit(solution)/shard_map/while/body/eval_jaxpr/dot_general | solution.py:108
  633.0 0.6 dynamic_slice.5
  633.5 0.6 iota_add_fusion.2
  634.1 6.5 %fusion.60 = f32[8,256,512]{2,1,0:T(8,128)} fusion(f32[8,256,512]{2,1,0:T(8,128)} %get-tuple-element.86, s32[]{:T(128)} %get-tuple-element.85, bf16[8192,512]{1,0:T(8,128)(2,1)} %get-tuple-element.95, s32[8192]{0:T(1024)S(1)} %bitcast.92, s32[256]{0:T(256)S(1)} %iota_add_fusion.2), kind=kOutput, calls=%fused_computation.10.clone.1 | convolution fusion | flops 2149580800 | bytes 8947200 | tf_op jit(solution)/shard_map/while/body/eval_jaxpr/dot_general | solution.py:108
  640.7 1.6 copy-done.1
  (40 shorter events, 0.4 us)
Async XLA Ops:
  0.6 78.6 %copy-start = (bf16[2048,512]{1,0:T(8,128)(2,1)S(1)}, bf16[2048,512]{1,0:T(8,128)(2,1)}, u32[]{:S(2)}) copy-start(bf16[2048,512]{1,0:T(8,128)(2,1)} %param.25) | copy-start | bytes 6291460
  112.8 3.9 copy-start.2
  112.8 188.7 %all-to-all-start.1 = ((bf16[32,256,512]{2,1,0:T(8,128)(2,1)}), bf16[32,256,512]{2,1,0:T(8,128)(2,1)}, u32[]{:S(2)}, u32[]{:S(2)}) async-start(bf16[32,256,512]{2,1,0:T(8,128)(2,1)} %bitcast.84), calls=%async_computation.1 | async-start | bytes 16777216 | tf_op jit(solution)/shard_map/all_to_all | solution.py:79
  116.6 3.2 copy-start.4
  116.6 3.2 copy-start.5
  116.6 3.2 copy-start.6
  116.6 3.2 copy-start.7
  119.8 19.1 %copy-start.3 = (bf16[768,512]{1,0:T(8,128)(2,1)S(1)}, bf16[768,512]{1,0:T(8,128)(2,1)}, u32[]{:S(2)}) copy-start(bf16[768,512]{1,0:T(8,128)(2,1)} %param.24) | copy-start | bytes 2359300
  119.8 19.1 %copy-start.8 = (f32[768]{0:T(1024)S(1)}, f32[768]{0:T(1024)}, u32[]{:S(2)}) copy-start(f32[768]{0:T(1024)} %param.23) | copy-start | bytes 9220
  119.8 19.1 %copy-start.9 = (f32[768]{0:T(1024)S(1)}, f32[768]{0:T(1024)}, u32[]{:S(2)}) copy-start(f32[768]{0:T(1024)} %param.22) | copy-start | bytes 9220
  301.5 41.1 %all-to-all-start.2 = ((bf16[1,32,32,512]{3,2,0,1:T(8,128)(2,1)}), bf16[1,32,32,512]{3,2,0,1:T(8,128)(2,1)S(1)}, u32[]{:S(2)}, u32[]{:S(2)}) async-start(bf16[1,32,32,512]{3,2,0,1:T(8,128)(2,1)} %bitcast.15), calls=%async_computation.2 | async-start | bytes 2097152 | tf_op jit(solution)/shard_map/all_to_all | solution.py:58
  389.9 189.2 %all-to-all-start.3 = ((bf16[32,256,512]{2,1,0:T(8,128)(2,1)}), bf16[32,256,512]{2,1,0:T(8,128)(2,1)}, u32[]{:S(2)}, u32[]{:S(2)}) async-start(bf16[32,256,512]{2,1,0:T(8,128)(2,1)} %broadcast_select_fusion), calls=%async_computation.3 | async-start | bytes 16777216 | tf_op jit(solution)/shard_map/all_to_all | solution.py:94
  640.7 1.6 copy-start.1
where the time goes:
time: 643 us; the launch traced here: 642 us
  waiting for transfers between devices  343 us (53%)
  local copies, waits for them, and re-layouts  162 us (25%)
  matrix products  80.1 us (12%)
  other arithmetic  30.7 us (5%)
  blocking collectives  14.3 us (2%)
  starting transfers between devices  11.6 us (2%)
    all_to_all x1, waiting for transfers between devices, on_device(): lax.all_to_all(outgoing.reshape(peers, capacity, feat_width), ('img', 'ti...  185 us
    all_to_all x1, waiting for transfers between devices, on_device(): lax.all_to_all(looked, ('img', 'tile'), split_axis=0, concat_axis=0, tile...  158 us
    dot_general x8, matrix products, add_block(): return jnp.dot(select, incoming, preferred_element_type=jnp.float32)  52.4 us
    gather x1, local copies, waits for them, and re-layouts, on_device(): request = jnp.where(filled, local_row[source], 0).reshape(peers, capacity)  45.5 us
    gather x1, local copies, waits for them, and re-layouts, on_device(): term_flat[source]  36.5 us
    gather x1, local copies, waits for them, and re-layouts, on_device(): looked = gauss_rows[asked]  33.6 us
    gather x1, local copies, waits for them, and re-layouts, on_device(): fetched_rows[place].reshape(group_views, strip_tiles, list_len, feat_width)  21.9 us
    dot_general x1, matrix products, on_device(): jnp.dot(act, down_weight, preferred_element_type=jnp.float32)  16.8 us
  transfers between devices with their start and end apart: 3, of which 2 were waited for; matrix products, arithmetic and copies ran while one was open for 10% of the time, Pallas kernels for 0%

commit v1 on v0

v1 whole, which is shorter than its diff:
```python
import functools

import jax
import jax.numpy as jnp
from jax import lax
from jax.experimental import pallas as pl
from jax.experimental.pallas import tpu as pltpu
from jax.sharding import PartitionSpec as P

F32 = jnp.float32
BF16 = jnp.bfloat16
I32 = jnp.int32
VMEM_BYTES = 50 * 1024 * 1024
LANES = (((1,), (1,)), ((), ()))
ROWS = (((0,), (0,)), ((), ()))


def params():
    return pltpu.CompilerParams(vmem_limit_bytes=VMEM_BYTES)


def index_kernel(peers, cap, rows_held, ids_ref, req_ref, own_ref, rank_ref):
    tiles, length = ids_ref.shape
    earlier = lax.broadcasted_iota(I32, (length, length), 0)
    later = lax.broadcasted_iota(I32, (length, length), 1)
    upper = (earlier < later).astype(BF16)
    every = jnp.ones((length, length), BF16)
    peer_id = lax.broadcasted_iota(I32, (peers, length), 0)
    slot_id = lax.broadcasted_iota(I32, (cap, length), 0)
    hots = []
    for t in range(tiles):
        owner = ids_ref[t : t + 1, :] // rows_held
        own_ref[t : t + 1, :] = owner
        hots.append((jnp.broadcast_to(owner, (peers, length)) == peer_id).astype(F32))
    stack = jnp.concatenate(hots, 0).astype(BF16)
    within = jnp.dot(stack, upper, preferred_element_type=F32)
    totals = jnp.dot(stack, every, preferred_element_type=F32)
    offset = jnp.zeros((peers, length), F32)
    found = jnp.zeros((2 * peers, cap), F32)
    for t in range(tiles):
        own_rows = slice(t * peers, (t + 1) * peers)
        rank = jnp.sum(hots[t] * (within[own_rows] + offset), axis=0, keepdims=True).astype(I32)
        offset = offset + totals[own_rows]
        rank_ref[t : t + 1, :] = rank
        ids = ids_ref[t : t + 1, :]
        row = ids - (ids // rows_held) * rows_held + 1
        high = (row >> 6).astype(F32)
        low = (row & 63).astype(F32)
        digits = jnp.concatenate([hots[t] * high, hots[t] * low], 0).astype(BF16)
        slots = (jnp.broadcast_to(rank, (cap, length)) == slot_id).astype(F32).astype(BF16)
        found = found + lax.dot_general(digits, slots, LANES, preferred_element_type=F32)
    req_ref[...] = (found[:peers] * 64.0 + found[peers:]).astype(I32) - 1


def index(ids, peers, cap, rows_held):
    like = jax.ShapeDtypeStruct(ids.shape, I32)
    return pl.pallas_call(
        functools.partial(index_kernel, peers, cap, rows_held),
        out_shape=(jax.ShapeDtypeStruct((peers, cap), I32), like, like),
        compiler_params=params(),
        cost_estimate=pl.CostEstimate(flops=10**9, bytes_accessed=10**7, transcendentals=0),
        name="index",
    )(ids)


def weights_kernel(alpha_ref, out_ref):
    alpha = alpha_ref[...]
    length = alpha.shape[1]
    logs = jnp.log1p(-alpha)
    earlier = lax.broadcasted_iota(I32, (length, length), 0)
    later = lax.broadcasted_iota(I32, (length, length), 1)
    upper = (earlier < later).astype(F32)
    before = jnp.dot(logs, upper, preferred_element_type=F32, precision=lax.Precision.HIGHEST)
    out_ref[...] = (alpha * jnp.exp(before)).astype(BF16)


def weights(alphas):
    return pl.pallas_call(
        weights_kernel,
        out_shape=jax.ShapeDtypeStruct(alphas.shape, BF16),
        compiler_params=params(),
        cost_estimate=pl.CostEstimate(flops=10**9, bytes_accessed=10**7, transcendentals=0),
        name="weights",
    )(alphas)


def spread_kernel(near, cap, own_ref, rank_ref, weight_ref, out_ref):
    t = pl.program_id(0)
    own = own_ref[pl.ds(t, 1), :]
    rank = rank_ref[pl.ds(t, 1), :]
    weight = weight_ref[...].astype(F32)
    cells, length = weight.shape
    by_owner = jnp.concatenate([jnp.where(own == o, weight, 0.0) for o in range(near)], 0).astype(BF16)
    slot_id = lax.broadcasted_iota(I32, (cap, length), 0)
    slots = (jnp.broadcast_to(rank, (cap, length)) == slot_id).astype(F32).astype(BF16)
    moved = lax.dot_general(by_owner, slots, LANES, preferred_element_type=F32).astype(BF16)
    if cap % 128 == 0:
        for o in range(near):
            out_ref[:, o * cap : (o + 1) * cap] = moved[o * cells : (o + 1) * cells]
    else:
        out_ref[...] = jnp.concatenate([moved[o * cells : (o + 1) * cells] for o in range(near)], 1)


def spread(own, rank, weight, near, cap):
    tiles, length = own.shape
    cells = weight.shape[0] // tiles
    whole = pl.BlockSpec((tiles, length), lambda t: (0, 0))
    return pl.pallas_call(
        functools.partial(spread_kernel, near, cap),
        grid=(tiles,),
        in_specs=[whole, whole, pl.BlockSpec((cells, length), lambda t: (t, 0))],
        out_specs=pl.BlockSpec((cells, near * cap), lambda t: (t, 0)),
        out_shape=jax.ShapeDtypeStruct((weight.shape[0], near * cap), BF16),
        compiler_params=params(),
        cost_estimate=pl.CostEstimate(flops=15 * 10**9, bytes_accessed=10**7, transcendentals=0),
        name="spread",
    )(own, rank, weight)


def gather_kernel(group, cap, asked_ref, rows_ref, out_ref):
    first = pl.program_id(0) * group
    asked = asked_ref[...]
    peer = lax.broadcasted_iota(I32, asked.shape, 1)
    held = rows_ref.shape[0]
    row_id = lax.broadcasted_iota(I32, (cap, held), 1)
    picks = []
    for q in range(group):
        column = jnp.sum(jnp.where(peer == first + q, asked, 0), axis=1, keepdims=True)
        picks.append((jnp.broadcast_to(column, (cap, held)) == row_id).astype(F32).astype(BF16))
    pick = jnp.concatenate(picks, 0)
    out_ref[...] = jnp.dot(pick, rows_ref[...], preferred_element_type=F32).astype(BF16)


def gather(asked, rows):
    near, cap = asked.shape
    held, feat = rows.shape
    group = max(1, min(near, 1024 // cap))
    return pl.pallas_call(
        functools.partial(gather_kernel, group, cap),
        grid=(near // group,),
        in_specs=[pl.BlockSpec((cap, near), lambda i: (0, 0)), pl.BlockSpec((held, feat), lambda i: (0, 0))],
        out_specs=pl.BlockSpec((group * cap, feat), lambda i: (i, 0)),
        out_shape=jax.ShapeDtypeStruct((near * cap, feat), BF16),
        compiler_params=params(),
        cost_estimate=pl.CostEstimate(flops=10**10, bytes_accessed=10**7, transcendentals=0),
        name="gather",
    )(asked.T, rows)


def blend_kernel(weight_ref, rows_ref, out_ref):
    out_ref[...] = jnp.dot(weight_ref[...], rows_ref[...], preferred_element_type=F32).astype(BF16)


def blend_rest_kernel(weight_ref, rows_ref, part_ref, target_ref, color_ref, diff_ref):
    color = jnp.dot(weight_ref[...], rows_ref[...], preferred_element_type=F32) + part_ref[...].astype(F32)
    color_ref[...] = color.astype(BF16)
    diff_ref[...] = (color - target_ref[...].astype(F32)).astype(BF16)


def blend(weight, rows, part=None, target=None):
    cells, slots = weight.shape
    feat = rows.shape[1]
    block = min(cells, 512)
    cell_block = pl.BlockSpec((block, feat), lambda i: (i, 0))
    out = jax.ShapeDtypeStruct((cells, feat), BF16)
    in_specs = [pl.BlockSpec((block, slots), lambda i: (i, 0)), pl.BlockSpec((slots, feat), lambda i: (0, 0))]
    rest = part is not None
    return pl.pallas_call(
        blend_rest_kernel if rest else blend_kernel,
        grid=(cells // block,),
        in_specs=in_specs + [cell_block] * (2 * rest),
        out_specs=(cell_block, cell_block) if rest else cell_block,
        out_shape=(out, out) if rest else out,
        compiler_params=params(),
        cost_estimate=pl.CostEstimate(flops=8 * 10**9, bytes_accessed=10**7, transcendentals=0),
        name="blend",
    )(weight, rows, *((part, target) if rest else ()))


def terms_kernel(weight_ref, diff_ref, out_ref):
    out_ref[...] = lax.dot_general(weight_ref[...], diff_ref[...], ROWS, preferred_element_type=F32).astype(BF16)


def terms(weight, diff):
    cells, slots = weight.shape
    feat = diff.shape[1]
    block = min(slots, 1024)
    return pl.pallas_call(
        terms_kernel,
        grid=(slots // block,),
        in_specs=[pl.BlockSpec((cells, block), lambda i: (0, i)), pl.BlockSpec((cells, feat), lambda i: (0, 0))],
        out_specs=pl.BlockSpec((block, feat), lambda i: (i, 0)),
        out_shape=jax.ShapeDtypeStruct((slots, feat), BF16),
        compiler_params=params(),
        cost_estimate=pl.CostEstimate(flops=8 * 10**9, bytes_accessed=10**7, transcendentals=0),
        name="terms",
    )(weight, diff)


def add_rows_kernel(asked_ref, terms_ref, *rest):
    out_ref = rest[-1]
    block = out_ref.shape[0]
    near, cap = asked_ref.shape
    row_id = lax.broadcasted_iota(I32, (block, cap), 0) + pl.program_id(0) * block
    picks = []
    for o in range(near):
        asked = jnp.broadcast_to(asked_ref[o : o + 1, :], (block, cap))
        picks.append((asked == row_id).astype(F32).astype(BF16))
    total = jnp.dot(jnp.concatenate(picks, 1), terms_ref[...], preferred_element_type=F32)
    out_ref[...] = total if len(rest) == 1 else total + rest[0][...]


def add_rows(asked, arrived, held, before=None):
    near, cap = asked.shape
    feat = arrived.shape[1]
    block = min(held, 512)
    row_block = pl.BlockSpec((block, feat), lambda i: (i, 0))
    more = before is not None
    in_specs = [pl.BlockSpec((near, cap), lambda i: (0, 0)), pl.BlockSpec((near * cap, feat), lambda i: (0, 0))]
    return pl.pallas_call(
        add_rows_kernel,
        grid=(held // block,),
        in_specs=in_specs + [row_block] * more,
        out_specs=row_block,
        out_shape=jax.ShapeDtypeStruct((held, feat), F32),
        compiler_params=params(),
        cost_estimate=pl.CostEstimate(flops=10**10, bytes_accessed=10**7, transcendentals=0),
        name="add_rows",
    )(asked, arrived, *((before,) if more else ()))


def layer_norm(rows, gain, bias):
    mean = jnp.mean(rows, axis=-1, keepdims=True)
    centred = rows - mean
    var = jnp.mean(centred * centred, axis=-1, keepdims=True)
    return centred * lax.rsqrt(var + 1e-05) * gain + bias


def on_device(
    patches,
    norm_gain,
    norm_bias,
    up_weight,
    up_bias,
    down_weight,
    down_bias,
    final_gain,
    final_bias,
    head_weight,
    gauss_rows,
    tile_lists,
    alphas,
):
    view_count, tiles_view, cells, width = patches.shape
    feat = head_weight.shape[1]
    n_img = lax.axis_size("img")
    n_tile = lax.axis_size("tile")
    peers = n_img * n_tile
    both = ("img", "tile")
    held = gauss_rows.shape[0]
    group_views, strip_tiles, list_len = tile_lists.shape
    tiles = group_views * strip_tiles
    cap = 2 * tiles * list_len // peers

    n_half = n_tile // 2
    near = n_img * n_half
    half = lax.axis_index("tile") // n_half
    mirror_of = [(n_half // 2 - 1 - k // 2) * 2 + k % 2 for k in range(n_half)] if n_half % 2 == 0 else list(range(n_half))
    groups = [[i * n_tile + h * n_half + k for i in range(n_img) for k in range(n_half)] for h in range(2)]
    crossing = [
        (i * n_tile + h * n_half + k, i * n_tile + (1 - h) * n_half + mirror_of[k])
        for i in range(n_img)
        for h in range(2)
        for k in range(n_half)
    ]

    def cross(x):
        return lax.ppermute(x, both, crossing)

    def exchange(x):
        return lax.all_to_all(x, both, split_axis=0, concat_axis=0, axis_index_groups=groups, tiled=True)

    def near_owner(own):
        img = own // n_tile
        tile = own - img * n_tile
        place = tile - half * n_half
        return jnp.where((place >= 0) & (place < n_half), img * n_half + place, -1)

    request, own, rank = index(tile_lists.reshape(tiles, list_len), peers, cap, held)
    asked = lax.all_to_all(request, both, split_axis=0, concat_axis=0, tiled=True)
    weight = weights(alphas.reshape(tiles * cells, list_len))
    code_far = cross(own * cap + rank)
    weight_far = cross(weight)

    wide = patches.reshape(-1, width).astype(F32)
    normed = layer_norm(wide, norm_gain, norm_bias).astype(BF16)
    inner = jnp.dot(normed, up_weight, preferred_element_type=F32) + up_bias
    act = (inner * jax.nn.sigmoid(1.702 * inner)).astype(BF16)
    block_out = wide + jnp.dot(act, down_weight, preferred_element_type=F32) + down_bias
    final = layer_norm(block_out, final_gain, final_bias).astype(BF16)
    embed = jnp.dot(final, head_weight, preferred_element_type=F32)
    scale = lax.rsqrt(jnp.mean(embed * embed, axis=-1, keepdims=True) + 1e-06)
    target = (embed * scale).astype(BF16).reshape(view_count, tiles_view, cells, feat)
    target = lax.all_to_all(target, "tile", split_axis=1, concat_axis=0, tiled=True)
    target = target.reshape(tiles * cells, feat)

    asked = asked.reshape(n_img, 2, n_half, cap)
    asked_near = lax.dynamic_index_in_dim(asked, half, 1, keepdims=False).reshape(near, cap)
    asked_far = lax.dynamic_index_in_dim(asked, 1 - half, 1, keepdims=False)
    asked_far = jnp.stack([asked_far[:, mirror_of[k]] for k in range(n_half)], 1).reshape(near, cap)

    rows_far = exchange(gather(asked_far, gauss_rows))
    spread_far = spread(near_owner(code_far // cap), code_far % cap, weight_far, near, cap)
    part = cross(blend(spread_far, rows_far))
    looked = gather(asked_near, gauss_rows)
    looked, rows_far = lax.optimization_barrier((looked, rows_far))
    rows_near = exchange(looked)
    spread_near = spread(near_owner(own), rank, weight, near, cap)
    color, diff = blend(spread_near, rows_near, part, target)

    diff_far = cross(diff)
    back_near = exchange(terms(spread_near, diff))
    term_far = terms(spread_far, diff_far)
    term_far, back_near = lax.optimization_barrier((term_far, back_near))
    back_far = exchange(term_far)
    grad = add_rows(asked_near, back_near, held)
    grad = add_rows(asked_far, back_far, held, grad)
    return (color.reshape(group_views, strip_tiles, cells, feat), grad)


def solution(mesh):
    placed = (
        P(("img", "tile"), None, None, None),
        P(),
        P(),
        P(),
        P(),
        P(),
        P(),
        P(),
        P(),
        P(),
        P(("img", "tile"), None),
        P("img", "tile", None),
        P("img", "tile", None, None),
    )
    return jax.shard_map(
        on_device,
        mesh=mesh,
        in_specs=placed,
        out_specs=(P("img", "tile", None, None), P(("img", "tile"), None)),
        check_vma=False,
    )
```

time: 643 us -> 410 us (0.64)
  local copies, waits for them, and re-layouts: 162 us -> 5.42 us
  waiting for transfers between devices: 343 us -> 224 us
  Pallas kernels: 0 us -> 113 us
  matrix products: 80.1 us -> 18.6 us
  starting transfers between devices: 11.6 us -> 38.1 us
  other arithmetic: 30.7 us -> 7.46 us
  blocking collectives: 14.3 us -> 0 us
    all_to_all x2 -> x5, waiting for transfers between devices: 343 us -> 69 us  [the longest x4 61.8 us: exchange(): lax.all_to_all(x, both, split_axis=0, concat_axis=0, axis_index_groups=gr...]
    ppermute x0 -> x4, waiting for transfers between devices: none -> 140 us  [cross(): return lax.ppermute(x, both, crossing)]
    gather x4 -> x0, local copies, waits for them, and re-layouts: 138 us -> none  [the longest x1 45.5 us: on_device(): request = jnp.where(filled, local_row[source], 0).reshape(peers, capacity)]
    pallas_call x0 -> x12, Pallas kernels: none -> 113 us  [the longest x2 30.6 us: spread(): pl.pallas_call(functools.partial(spread_kernel, near, cap), grid=(tiles,)...]
    dot_general x13 -> x2, matrix products: 80.1 us -> 18.6 us  [the longest x1 17.2 us: on_device(): jnp.dot(act, down_weight, preferred_element_type=F32)]
    all_to_all x2 -> x5, starting transfers between devices: 8.05 us -> 26.7 us  [the longest x4 19.4 us: exchange(): lax.all_to_all(x, both, split_axis=0, concat_axis=0, axis_index_groups=gr...]
    all_to_all x1, waiting for transfers between devices: 0.01 us -> 15.9 us  [on_device(): lax.all_to_all(target, 'tile', split_axis=1, concat_axis=0, tiled=True)]
    scatter x1 -> x0, local copies, waits for them, and re-layouts: 15.5 us -> none  [on_device(): jnp.full((slot_total,), -1, jnp.int32).at[place]]
  transfers between devices with their start and end apart: 3 -> 10, of which waited for: 2 -> 7; matrix products, arithmetic and copies ran while one was open for 10% -> 7% of each run, Pallas kernels for 0% -> 17%
where the time goes in v1:
time: 410 us; the launch traced here: 409 us
  waiting for transfers between devices  224 us (55%)
  Pallas kernels  113 us (28%)
  starting transfers between devices  38.1 us (9%)
  matrix products  18.6 us (5%)
  other arithmetic  7.46 us (2%)
  local copies, waits for them, and re-layouts  5.42 us (1%)
    ppermute x4, waiting for transfers between devices, cross(): return lax.ppermute(x, both, crossing)  140 us
    all_to_all x4, waiting for transfers between devices, exchange(): lax.all_to_all(x, both, split_axis=0, concat_axis=0, axis_index_groups=gr...  61.8 us
    pallas_call x2, Pallas kernels, spread(): pl.pallas_call(functools.partial(spread_kernel, near, cap), grid=(tiles,)...  30.6 us
    pallas_call x2, Pallas kernels, add_rows(): pl.pallas_call(add_rows_kernel, grid=(held // block,), in_specs=in_specs...  25.5 us
    pallas_call x2, Pallas kernels, gather(): pl.pallas_call(functools.partial(gather_kernel, group, cap), grid=(near /...  21.2 us
    all_to_all x4, starting transfers between devices, exchange(): lax.all_to_all(x, both, split_axis=0, concat_axis=0, axis_index_groups=gr...  19.4 us
    dot_general x1, matrix products, on_device(): jnp.dot(act, down_weight, preferred_element_type=F32)  17.2 us
    pallas_call x2, Pallas kernels, blend(): pl.pallas_call(blend_rest_kernel if rest else blend_kernel, grid=(cells /...  17.2 us
  transfers between devices with their start and end apart: 10, of which 7 were waited for; matrix products, arithmetic and copies ran while one was open for 7% of the time, Pallas kernels for 17%

profile of v1, /device:TPU:0, one launch (start us, length us, event | category | flops | bytes accessed | tf_op | source)
XLA Modules:
  0.0 408.6 jit_solution(59444334411787166)
XLA Ops:
  0.6 0.0 copy-start
  0.6 0.0 copy-start.2
  0.7 0.0 copy-start.4
  0.7 0.9 copy-done.4
  1.5 1.2 index.1
  2.8 0.6 copy.23
  3.4 7.3 %all-to-all-start = ((s32[32,1,256]{2,1,0:T(1,128)}), s32[32,1,256]{2,1,0:T(1,128)S(1)}, u32[]{:S(2)}, u32[]{:S(2)}) async-start(s32[32,1,256]{2,1,0:T(1,128)} %copy.23), calls=%async_computation | async-start | bytes 65536 | tf_op jit(solution)/shard_map/all_to_all | solution.py:290
  10.8 7.2 %all-to-all-done = s32[32,1,256]{2,1,0:T(1,128)S(1)} async-done(((s32[32,1,256]{2,1,0:T(1,128)}), s32[32,1,256]{2,1,0:T(1,128)S(1)}, u32[]{:S(2)}, u32[]{:S(2)}) %all-to-all-start) | async-done | bytes 32800 | tf_op jit(solution)/shard_map/all_to_all | solution.py:290
  18.0 0.1 reduce.2
  18.1 0.1 copy.26.asked_ref
  18.2 0.0 copy-done.2
  18.3 10.6 %gather.3 = bf16[4096,512]{1,0:T(8,128)(2,1)} custom-call(s32[256,16]{1,0:T(8,128)S(1)} %copy.26.asked_ref, bf16[2048,512]{1,0:T(8,128)(2,1)S(1)} %copy-done.2), custom_call_target="tpu_custom_call" | custom-call | flops 10000000000 | bytes 10000000 | tf_op jit(solution)/shard_map/gather/pallas_call | solution.py:138
  28.9 4.6 %all-to-all-start.1 = ((bf16[16,256,512]{2,1,0:T(8,128)(2,1)}), bf16[16,256,512]{2,1,0:T(8,128)(2,1)}, u32[]{:S(2)}, u32[]{:S(2)}) async-start(bf16[16,256,512]{2,1,0:T(8,128)(2,1)} %bitcast.42), calls=%async_computation.1 | async-start | bytes 8388608 | tf_op jit(solution)/shard_map/all_to_all | solution.py:281
  33.4 1.7 convert_reduce_fusion
  35.1 0.1 div.73
  35.2 0.0 copy-start.6
  35.2 0.0 copy-start.7
  35.2 0.0 copy-start.8
  35.2 0.0 copy-start.9
  35.2 2.0 multiply_reduce_fusion.1
  37.3 0.1 rsqrt.28
  37.3 3.1 copy.27
  40.4 0.0 copy-done.6
  40.4 0.0 copy-done.7
  40.4 0.0 copy-done.8
  40.4 0.0 copy-done.9
  40.4 17.2 %fusion.20 = (f32[1024]{0:T(1024)S(1)}, f32[1024,768]{0,1:T(8,128)}) fusion(f32[768]{0:T(1024)S(1)} %copy-done.7, f32[1024,768]{0,1:T(8,128)} %copy.27, bf16[3072,768]{1,0:T(8,128)(2,1)} %param.18, f32[3072]{0:T(1024)S(1)} %copy-done.6, bf16[768,3072]{1,0:T(8,128)(2,1)} %param.16, f32[768]{0:T(1024)S(1)} %copy-done.8, f32[768]{0:T(1024)S(1)} %copy-done.9, ...), kind=kOutput, calls=%fused_computation.58 | convolution fusion | flops 9692773376 | bytes 17335296 | tf_op jit(solution)/shard_map/dot_general | solution.py:299
  57.6 2.4 multiply_reduce_fusion
  60.0 0.0 copy-done
  60.0 0.4 copy-done.5
  60.4 0.0 copy-done.10
  60.4 0.0 copy-done.11
  60.4 1.4 multiply_reduce_fusion.2
  62.1 1.2 multiply_convert_fusion.2
  63.2 22.3 %all-to-all-done.1 = bf16[16,256,512]{2,1,0:T(8,128)(2,1)} async-done(((bf16[16,256,512]{2,1,0:T(8,128)(2,1)}), bf16[16,256,512]{2,1,0:T(8,128)(2,1)}, u32[]{:S(2)}, u32[]{:S(2)}) %all-to-all-start.1) | async-done | bytes 4194336 | tf_op jit(solution)/shard_map/all_to_all | solution.py:281
  85.5 3.8 all-to-all-start.3
  89.3 0.1 copy.25.asked_ref
  89.4 10.6 %gather.2 = bf16[4096,512]{1,0:T(8,128)(2,1)} custom-call(s32[256,16]{1,0:T(8,128)S(1)} %copy.25.asked_ref, bf16[2048,512]{1,0:T(8,128)(2,1)S(1)} %copy-done.2), custom_call_target="tpu_custom_call" | custom-call | flops 10000000000 | bytes 10000000 | tf_op jit(solution)/shard_map/gather/pallas_call | solution.py:138
  99.9 15.9 %all-to-all-done.3 = bf16[1,32,32,512]{3,2,0,1:T(8,128)(2,1)S(1)} async-done(((bf16[1,32,32,512]{3,2,0,1:T(8,128)(2,1)}), bf16[1,32,32,512]{3,2,0,1:T(8,128)(2,1)S(1)}, u32[]{:S(2)}, u32[]{:S(2)}) %all-to-all-start.3) | async-done | bytes 1048608 | tf_op jit(solution)/shard_map/all_to_all | solution.py:304
  115.8 5.7 %all-to-all-start.2 = ((bf16[16,256,512]{2,1,0:T(8,128)(2,1)}), bf16[16,256,512]{2,1,0:T(8,128)(2,1)}, u32[]{:S(2)}, u32[]{:S(2)}) async-start(bf16[16,256,512]{2,1,0:T(8,128)(2,1)} %bitcast.41), calls=%async_computation.2 | async-start | bytes 8388608 | tf_op jit(solution)/shard_map/all_to_all | solution.py:281
  121.6 0.0 copy-done.3
  121.6 0.7 weights.1.weight_ref
  122.3 2.6 collective-permute-start.1
  124.9 1.3 collective-permute-start
  126.3 56.2 %collective-permute-done = s32[32,128]{1,0:T(8,128)S(1)} collective-permute-done((s32[32,128]{1,0:T(8,128)S(1)}, s32[32,128]{1,0:T(8,128)S(1)}, u32[]{:S(2)}, u32[]{:S(2)}) %collective-permute-start) | collective-permute-done | bytes 16416 | tf_op jit(solution)/shard_map/ppermute | solution.py:278
  182.5 0.0 collective-permute-done.1.weight_ref
  182.5 15.3 %spread.3.weight_ref = bf16[1024,4096]{1,0:T(8,128)(2,1)} custom-call(s32[32,128]{1,0:T(8,128)S(1)} %get-tuple-element.21.own_ref, s32[32,128]{1,0:T(8,128)S(1)} %get-tuple-element.20.rank_ref, bf16[1024,128]{1,0:T(8,128)(2,1)S(1)} %collective-permute-done.1.weight_ref), custom_call_target="tpu_custom_call" | custom-call | flops 15000000512 | bytes 10000000 | tf_op jit(solution)/shard_map/spread/pallas_call | solution.py:108
  197.8 8.1 %blend.2 = bf16[1024,512]{1,0:T(8,128)(2,1)S(1)} custom-call(bf16[1024,4096]{1,0:T(8,128)(2,1)} %spread.3.weight_ref, bf16[4096,512]{1,0:T(8,128)(2,1)} %bitcast.7.rows_ref), custom_call_target="tpu_custom_call" | custom-call | flops 8000000000 | bytes 10000000 | tf_op jit(solution)/shard_map/blend/pallas_call | solution.py:168
  205.9 1.8 collective-permute-start.2
  207.7 15.2 %spread.2.weight_ref = bf16[1024,4096]{1,0:T(8,128)(2,1)} custom-call(s32[32,128]{1,0:T(8,128)S(1)} %get-tuple-element.23.own_ref, s32[32,128]{1,0:T(8,128)S(1)} %get-tuple-element.11.rank_ref, bf16[1024,128]{1,0:T(8,128)(2,1)S(1)} %weights.1.weight_ref), custom_call_target="tpu_custom_call" | custom-call | flops 15000000512 | bytes 10000000 | tf_op jit(solution)/shard_map/spread/pallas_call | solution.py:108
  223.0 9.5 %collective-permute-done.2.part_ref = bf16[1024,512]{1,0:T(8,128)(2,1)S(1)} collective-permute-done((bf16[1024,512]{1,0:T(8,128)(2,1)S(1)}, bf16[1024,512]{1,0:T(8,128)(2,1)S(1)}, u32[]{:S(2)}, u32[]{:S(2)}) %collective-permute-start.2) | collective-permute-done | bytes 1048608 | tf_op jit(solution)/shard_map/ppermute | solution.py:278
  232.5 0.0 all-to-all-done.2
  232.5 9.0 %blend.3 = (bf16[1024,512]{1,0:T(8,128)(2,1)}, bf16[1024,512]{1,0:T(8,128)(2,1)S(1)}) custom-call(bf16[1024,4096]{1,0:T(8,128)(2,1)} %spread.2.weight_ref, bf16[4096,512]{1,0:T(8,128)(2,1)} %bitcast.9.rows_ref, bf16[1024,512]{1,0:T(8,128)(2,1)S(1)} %collective-permute-done.2.part_ref, bf16[1024,512]{1,0:T(8,128)(2,1)S(1)} %bitcast.33), custom_call_target="tpu_custom_call" | custom-call | flops 8000000000 | bytes 10000000 | tf_op jit(solution)/shard_map/blend/pallas_call | solution.py:168
  241.5 8.6 %terms.3 = bf16[4096,512]{1,0:T(8,128)(2,1)} custom-call(bf16[1024,4096]{1,0:T(8,128)(2,1)} %spread.2.weight_ref, bf16[1024,512]{1,0:T(8,128)(2,1)S(1)} %get-tuple-element.15.diff_ref), custom_call_target="tpu_custom_call" | custom-call | flops 8000000000 | bytes 10000000 | tf_op jit(solution)/shard_map/terms/pallas_call | solution.py:188
  250.1 4.6 %all-to-all-start.4 = ((bf16[16,256,512]{2,1,0:T(8,128)(2,1)}), bf16[16,256,512]{2,1,0:T(8,128)(2,1)}, u32[]{:S(2)}, u32[]{:S(2)}) async-start(bf16[16,256,512]{2,1,0:T(8,128)(2,1)} %bitcast.43), calls=%async_computation.4 | async-start | bytes 8388608 | tf_op jit(solution)/shard_map/all_to_all | solution.py:281
  254.7 1.9 collective-permute-start.3
  256.6 73.9 %collective-permute-done.3.diff_ref = bf16[1024,512]{1,0:T(8,128)(2,1)S(1)} collective-permute-done((bf16[1024,512]{1,0:T(8,128)(2,1)S(1)}, bf16[1024,512]{1,0:T(8,128)(2,1)S(1)}, u32[]{:S(2)}, u32[]{:S(2)}) %collective-permute-start.3) | collective-permute-done | bytes 1048608 | tf_op jit(solution)/shard_map/ppermute | solution.py:278
  330.5 8.6 %terms.2 = bf16[4096,512]{1,0:T(8,128)(2,1)} custom-call(bf16[1024,4096]{1,0:T(8,128)(2,1)} %spread.3.weight_ref, bf16[1024,512]{1,0:T(8,128)(2,1)S(1)} %collective-permute-done.3.diff_ref), custom_call_target="tpu_custom_call" | custom-call | flops 8000000000 | bytes 10000000 | tf_op jit(solution)/shard_map/terms/pallas_call | solution.py:188
  339.1 0.0 all-to-all-done.4
  339.1 4.6 %all-to-all-start.5 = ((bf16[16,256,512]{2,1,0:T(8,128)(2,1)}), bf16[16,256,512]{2,1,0:T(8,128)(2,1)}, u32[]{:S(2)}, u32[]{:S(2)}) async-start(bf16[16,256,512]{2,1,0:T(8,128)(2,1)} %bitcast.44), calls=%async_computation.5 | async-start | bytes 8388608 | tf_op jit(solution)/shard_map/all_to_all | solution.py:281
  343.6 12.6 %add_rows.2.rest_0_ = f32[2048,512]{1,0:T(8,128)} custom-call(s32[16,256]{1,0:T(8,128)S(1)} %reshape.110.asked_ref, bf16[4096,512]{1,0:T(8,128)(2,1)} %bitcast.16.terms_ref), custom_call_target="tpu_custom_call" | custom-call | flops 10000000000 | bytes 10000000 | tf_op jit(solution)/shard_map/add_rows/pallas_call | solution.py:220
  356.2 39.5 %all-to-all-done.5 = bf16[16,256,512]{2,1,0:T(8,128)(2,1)} async-done(((bf16[16,256,512]{2,1,0:T(8,128)(2,1)}), bf16[16,256,512]{2,1,0:T(8,128)(2,1)}, u32[]{:S(2)}, u32[]{:S(2)}) %all-to-all-start.5) | async-done | bytes 4194336 | tf_op jit(solution)/shard_map/all_to_all | solution.py:281
  395.7 12.9 %add_rows.3 = f32[2048,512]{1,0:T(8,128)} custom-call(s32[16,256]{1,0:T(8,128)S(1)} %reshape.111.asked_ref, bf16[4096,512]{1,0:T(8,128)(2,1)} %bitcast.18.terms_ref, f32[2048,512]{1,0:T(8,128)} %add_rows.2.rest_0_), custom_call_target="tpu_custom_call" | custom-call | flops 10000000000 | bytes 10000000 | tf_op jit(solution)/shard_map/add_rows/pallas_call | solution.py:220
  408.6 0.0 copy-done.1
  (18 shorter events, 0.2 us)
Async XLA Ops:
  0.6 59.4 %copy-start = (bf16[768,512]{1,0:T(8,128)(2,1)S(1)}, bf16[768,512]{1,0:T(8,128)(2,1)}, u32[]{:S(2)}) copy-start(bf16[768,512]{1,0:T(8,128)(2,1)} %param.22) | copy-start | bytes 2359300
  0.6 17.6 %copy-start.2 = (bf16[2048,512]{1,0:T(8,128)(2,1)S(1)}, bf16[2048,512]{1,0:T(8,128)(2,1)}, u32[]{:S(2)}) copy-start(bf16[2048,512]{1,0:T(8,128)(2,1)} %rows_ref.3) | copy-start | bytes 6291460
  0.7 0.9 copy-start.4
  3.4 14.5 %all-to-all-start = ((s32[32,1,256]{2,1,0:T(1,128)}), s32[32,1,256]{2,1,0:T(1,128)S(1)}, u32[]{:S(2)}, u32[]{:S(2)}) async-start(s32[32,1,256]{2,1,0:T(1,128)} %copy.23), calls=%async_computation | async-start | bytes 65536 | tf_op jit(solution)/shard_map/all_to_all | solution.py:290
  28.9 56.6 %all-to-all-start.1 = ((bf16[16,256,512]{2,1,0:T(8,128)(2,1)}), bf16[16,256,512]{2,1,0:T(8,128)(2,1)}, u32[]{:S(2)}, u32[]{:S(2)}) async-start(bf16[16,256,512]{2,1,0:T(8,128)(2,1)} %bitcast.42), calls=%async_computation.1 | async-start | bytes 8388608 | tf_op jit(solution)/shard_map/all_to_all | solution.py:281
  35.2 5.2 %copy-start.6 = (f32[3072]{0:T(1024)S(1)}, f32[3072]{0:T(1024)}, u32[]{:S(2)}) copy-start(f32[3072]{0:T(1024)} %param.17) | copy-start | bytes 36868
  35.2 5.2 %copy-start.7 = (f32[768]{0:T(1024)S(1)}, f32[768]{0:T(1024)}, u32[]{:S(2)}) copy-start(f32[768]{0:T(1024)} %param.19) | copy-start | bytes 9220
  35.2 5.2 %copy-start.8 = (f32[768]{0:T(1024)S(1)}, f32[768]{0:T(1024)}, u32[]{:S(2)}) copy-start(f32[768]{0:T(1024)} %param.15) | copy-start | bytes 9220
  35.2 5.2 %copy-start.9 = (f32[768]{0:T(1024)S(1)}, f32[768]{0:T(1024)}, u32[]{:S(2)}) copy-start(f32[768]{0:T(1024)} %param.14) | copy-start | bytes 9220
  57.6 2.8 copy-start.5
  57.6 2.8 copy-start.10
  57.6 2.8 copy-start.11
  85.5 30.4 %all-to-all-start.3 = ((bf16[1,32,32,512]{3,2,0,1:T(8,128)(2,1)}), bf16[1,32,32,512]{3,2,0,1:T(8,128)(2,1)S(1)}, u32[]{:S(2)}, u32[]{:S(2)}) async-start(bf16[1,32,32,512]{3,2,0,1:T(8,128)(2,1)} %bitcast.45), calls=%async_computation.3 | async-start | bytes 2097152 | tf_op jit(solution)/shard_map/all_to_all | solution.py:304
  115.8 5.7 %copy-start.3 = (f32[8,4,32,128]{3,2,1,0:T(8,128)S(1)}, f32[8,4,32,128]{3,2,1,0:T(8,128)}, u32[]{:S(2)}) copy-start(f32[8,4,32,128]{3,2,1,0:T(8,128)} %param.25) | copy-start | bytes 1572868
  115.8 116.6 %all-to-all-start.2 = ((bf16[16,256,512]{2,1,0:T(8,128)(2,1)}), bf16[16,256,512]{2,1,0:T(8,128)(2,1)}, u32[]{:S(2)}, u32[]{:S(2)}) async-start(bf16[16,256,512]{2,1,0:T(8,128)(2,1)} %bitcast.41), calls=%async_computation.2 | async-start | bytes 8388608 | tf_op jit(solution)/shard_map/all_to_all | solution.py:281
  122.3 60.2 %collective-permute-start.1 = (bf16[1024,128]{1,0:T(8,128)(2,1)S(1)}, bf16[1024,128]{1,0:T(8,128)(2,1)S(1)}, u32[]{:S(2)}, u32[]{:S(2)}) collective-permute-start(bf16[1024,128]{1,0:T(8,128)(2,1)S(1)} %weights.1.weight_ref), channel_id=1, source_target_pairs={{0,6},{1,7},{2,4},{3,5},{4,2},{5,3},{6,0},{7,1},{8,14},{9,15},{10,... | collective-permute-start | bytes 786440 | tf_op jit(solution)/shard_map/ppermute | solution.py:278
  124.9 57.5 %collective-permute-start = (s32[32,128]{1,0:T(8,128)S(1)}, s32[32,128]{1,0:T(8,128)S(1)}, u32[]{:S(2)}, u32[]{:S(2)}) collective-permute-start(s32[32,128]{1,0:T(8,128)S(1)} %get-tuple-element.22), channel_id=1, source_target_pairs={{0,6},{1,7},{2,4},{3,5},{4,2},{5,3},{6,0},{7,1},{8,14},{9,15},{10,... | collective-permute-start | bytes 49160 | tf_op jit(solution)/shard_map/ppermute | solution.py:278
  205.9 26.5 %collective-permute-start.2 = (bf16[1024,512]{1,0:T(8,128)(2,1)S(1)}, bf16[1024,512]{1,0:T(8,128)(2,1)S(1)}, u32[]{:S(2)}, u32[]{:S(2)}) collective-permute-start(bf16[1024,512]{1,0:T(8,128)(2,1)S(1)} %blend.2), channel_id=1, source_target_pairs={{0,6},{1,7},{2,4},{3,5},{4,2},{5,3},{6,0},{7,1},{8,14},{9,15},{10,... | collective-permute-start | bytes 3145736 | tf_op jit(solution)/shard_map/ppermute | solution.py:278
  250.1 89.0 %all-to-all-start.4 = ((bf16[16,256,512]{2,1,0:T(8,128)(2,1)}), bf16[16,256,512]{2,1,0:T(8,128)(2,1)}, u32[]{:S(2)}, u32[]{:S(2)}) async-start(bf16[16,256,512]{2,1,0:T(8,128)(2,1)} %bitcast.43), calls=%async_computation.4 | async-start | bytes 8388608 | tf_op jit(solution)/shard_map/all_to_all | solution.py:281
  254.7 75.8 %collective-permute-start.3 = (bf16[1024,512]{1,0:T(8,128)(2,1)S(1)}, bf16[1024,512]{1,0:T(8,128)(2,1)S(1)}, u32[]{:S(2)}, u32[]{:S(2)}) collective-permute-start(bf16[1024,512]{1,0:T(8,128)(2,1)S(1)} %get-tuple-element.15.diff_ref), channel_id=1, source_target_pairs={{0,6},{1,7},{2,4},{3,5},{4,2},{5,3},{6,0},{7,1},{8,14},{9,15},{10,... | collective-permute-start | bytes 3145736 | tf_op jit(solution)/shard_map/ppermute | solution.py:278
  339.1 56.6 %all-to-all-start.5 = ((bf16[16,256,512]{2,1,0:T(8,128)(2,1)}), bf16[16,256,512]{2,1,0:T(8,128)(2,1)}, u32[]{:S(2)}, u32[]{:S(2)}) async-start(bf16[16,256,512]{2,1,0:T(8,128)(2,1)} %bitcast.44), calls=%async_computation.5 | async-start | bytes 8388608 | tf_op jit(solution)/shard_map/all_to_all | solution.py:281
  395.7 12.9 %copy-start.1 = (bf16[768,512]{1,0:T(8,128)(2,1)S(1)}, bf16[768,512]{1,0:T(8,128)(2,1)}, u32[]{:S(2)}) copy-start(bf16[768,512]{1,0:T(8,128)(2,1)} %param.22) | copy-start | bytes 2359300

commit v2 on v1

--- a/solution.py
+++ b/solution.py
@@ -287,10 +287,21 @@
         return jnp.where((place >= 0) & (place < n_half), img * n_half + place, -1)
 
     request, own, rank = index(tile_lists.reshape(tiles, list_len), peers, cap, held)
+    weight = weights(alphas.reshape(tiles * cells, list_len))
+    request, code, weight = lax.optimization_barrier((request, own * cap + rank, weight))
+    code_far = cross(code)
+    weight_far = cross(weight)
     asked = lax.all_to_all(request, both, split_axis=0, concat_axis=0, tiled=True)
-    weight = weights(alphas.reshape(tiles * cells, list_len))
-    code_far = cross(own * cap + rank)
-    weight_far = cross(weight)
+    asked, code_far, weight_far = lax.optimization_barrier((asked, code_far, weight_far))
+
+    asked = asked.reshape(n_img, 2, n_half, cap)
+    asked_near = lax.dynamic_index_in_dim(asked, half, 1, keepdims=False).reshape(near, cap)
+    asked_far = lax.dynamic_index_in_dim(asked, 1 - half, 1, keepdims=False)
+    asked_far = jnp.stack([asked_far[:, mirror_of[k]] for k in range(n_half)], 1).reshape(near, cap)
+
+    looked_far = gather(asked_far, gauss_rows)
+    looked_far, patches = lax.optimization_barrier((looked_far, patches))
+    rows_far = exchange(looked_far)
 
     wide = patches.reshape(-1, width).astype(F32)
     normed = layer_norm(wide, norm_gain, norm_bias).astype(BF16)
@@ -301,21 +312,19 @@
     embed = jnp.dot(final, head_weight, preferred_element_type=F32)
     scale = lax.rsqrt(jnp.mean(embed * embed, axis=-1, keepdims=True) + 1e-06)
     target = (embed * scale).astype(BF16).reshape(view_count, tiles_view, cells, feat)
+    target, asked_near, code_far, weight_far = lax.optimization_barrier((target, asked_near, code_far, weight_far))
     target = lax.all_to_all(target, "tile", split_axis=1, concat_axis=0, tiled=True)
     target = target.reshape(tiles * cells, feat)
-
-    asked = asked.reshape(n_img, 2, n_half, cap)
-    asked_near = lax.dynamic_index_in_dim(asked, half, 1, keepdims=False).reshape(near, cap)
-    asked_far = lax.dynamic_index_in_dim(asked, 1 - half, 1, keepdims=False)
-    asked_far = jnp.stack([asked_far[:, mirror_of[k]] for k in range(n_half)], 1).reshape(near, cap)
-
-    rows_far = exchange(gather(asked_far, gauss_rows))
+    looked_near = gather(asked_near, gauss_rows)
     spread_far = spread(near_owner(code_far // cap), code_far % cap, weight_far, near, cap)
+
+    looked_near, rows_far, spread_far, target, own = lax.optimization_barrier(
+        (looked_near, rows_far, spread_far, target, own)
+    )
+    rows_near = exchange(looked_near)
     part = cross(blend(spread_far, rows_far))
-    looked = gather(asked_near, gauss_rows)
-    looked, rows_far = lax.optimization_barrier((looked, rows_far))
-    rows_near = exchange(looked)
     spread_near = spread(near_owner(own), rank, weight, near, cap)
+    part, rows_near, spread_near = lax.optimization_barrier((part, rows_near, spread_near))
     color, diff = blend(spread_near, rows_near, part, target)
 
     diff_far = cross(diff)

time: 410 us -> 410 us (level)
  blocking collectives: 0 us -> 30.2 us
  waiting for transfers between devices: 224 us -> 195 us
    all_to_all x0 -> x1, blocking collectives: none -> 30.2 us  [on_device(): lax.all_to_all(target, 'tile', split_axis=1, concat_axis=0, tiled=True)]
    all_to_all x1 -> x0, waiting for transfers between devices: 15.9 us -> none  [on_device(): lax.all_to_all(target, 'tile', split_axis=1, concat_axis=0, tiled=True)]
    ppermute x4, waiting for transfers between devices: 140 us -> 125 us  [cross(): return lax.ppermute(x, both, crossing)]
    ppermute x4, starting transfers between devices: 7.67 us -> 12.8 us  [cross(): return lax.ppermute(x, both, crossing)]
    all_to_all x1, starting transfers between devices: 7.3 us -> 2.81 us  [on_device(): lax.all_to_all(request, both, split_axis=0, concat_axis=0, tiled=True)]
  transfers between devices with their start and end apart: 10 -> 9, of which waited for: 7 -> 5; matrix products, arithmetic and copies ran while one was open for 7% -> 0% of each run, Pallas kernels for 17% -> 18%
where the time goes in v2:
time: 410 us; the launch traced here: 407 us
  waiting for transfers between devices  195 us (48%)
  Pallas kernels  117 us (29%)
  starting transfers between devices  35.3 us (9%)
  blocking collectives  30.2 us (7%)
  matrix products  18.6 us (5%)
  local copies, waits for them, and re-layouts  5.4 us (1%)
  other arithmetic  5.01 us (1%)
    ppermute x4, waiting for transfers between devices, cross(): return lax.ppermute(x, both, crossing)  125 us
    all_to_all x4, waiting for transfers between devices, exchange(): lax.all_to_all(x, both, split_axis=0, concat_axis=0, axis_index_groups=gr...  62.4 us
    pallas_call x2, Pallas kernels, spread(): pl.pallas_call(functools.partial(spread_kernel, near, cap), grid=(tiles,)...  33.6 us
    all_to_all x1, blocking collectives, on_device(): lax.all_to_all(target, 'tile', split_axis=1, concat_axis=0, tiled=True)  30.2 us
    pallas_call x2, Pallas kernels, add_rows(): pl.pallas_call(add_rows_kernel, grid=(held // block,), in_specs=in_specs...  25.5 us
    pallas_call x2, Pallas kernels, gather(): pl.pallas_call(functools.partial(gather_kernel, group, cap), grid=(near /...  21.2 us
    all_to_all x4, starting transfers between devices, exchange(): lax.all_to_all(x, both, split_axis=0, concat_axis=0, axis_index_groups=gr...  19.7 us
    pallas_call x2, Pallas kernels, blend(): pl.pallas_call(blend_rest_kernel if rest else blend_kernel, grid=(cells /...  17.2 us
  transfers between devices with their start and end apart: 9, of which 5 were waited for; matrix products, arithmetic and copies ran while one was open for 0% of the time, Pallas kernels for 18%

profile of v2, /device:TPU:0, one launch (start us, length us, event | category | flops | bytes accessed | tf_op | source)
XLA Modules:
  0.0 407.0 jit_solution(12152130019327263036)
XLA Ops:
  0.6 0.0 copy-start
  0.6 0.0 copy-start.3
  0.7 0.0 copy-start.6
  0.7 0.8 copy-done.6
  1.5 1.2 index.1
  2.7 0.0 copy-done.3
  2.7 0.7 weights.1.weight_ref
  3.4 0.0 copy-start.4
  3.5 5.1 %collective-permute-start.1 = (bf16[1024,128]{1,0:T(8,128)(2,1)S(1)}, bf16[1024,128]{1,0:T(8,128)(2,1)}, u32[]{:S(2)}, u32[]{:S(2)}) collective-permute-start(bf16[1024,128]{1,0:T(8,128)(2,1)S(1)} %weights.1.weight_ref), channel_id=1, source_target_pairs={{0,6},{1,7},{2,4},{3,5},{4,2},{5,3},{6,0},{7,1},{8,14},{9,15},{10,... | collective-permute-start | bytes 786440 | tf_op jit(solution)/shard_map/ppermute | solution.py:278
  8.6 0.6 copy.23
  9.2 2.8 all-to-all-start
  12.0 3.7 collective-permute-start
  15.7 6.9 %all-to-all-done = s32[32,1,256]{2,1,0:T(1,128)S(1)} async-done(((s32[32,1,256]{2,1,0:T(1,128)}), s32[32,1,256]{2,1,0:T(1,128)S(1)}, u32[]{:S(2)}, u32[]{:S(2)}) %all-to-all-start) | async-done | bytes 32800 | tf_op jit(solution)/shard_map/all_to_all | solution.py:294
  22.6 0.0 collective-permute-done
  22.6 0.0 collective-permute-done.1.weight_ref
  22.7 0.0 copy-done.4
  22.7 0.1 copy.24.asked_ref
  22.8 0.0 copy-done.2
  22.9 0.0 copy-start.7
  22.9 10.6 %gather.2 = bf16[4096,512]{1,0:T(8,128)(2,1)} custom-call(s32[256,16]{1,0:T(8,128)S(1)} %copy.24.asked_ref, bf16[2048,512]{1,0:T(8,128)(2,1)S(1)} %copy-done.2), custom_call_target="tpu_custom_call" | custom-call | flops 10000000000 | bytes 10000000 | tf_op jit(solution)/shard_map/gather/pallas_call | solution.py:138
  33.5 0.0 copy-done.7
  33.5 0.3 convert_reduce_fusion
  33.7 0.1 div.65
  33.8 2.0 multiply_reduce_fusion.1
  35.9 0.1 rsqrt.28
  36.0 3.1 copy.25
  39.0 0.0 copy-done.9
  39.0 0.0 copy-done.10
  39.0 0.0 copy-done.11
  39.0 0.0 copy-done.12
  39.1 17.2 %fusion.20 = (f32[1024]{0:T(1024)S(1)}, f32[1024,768]{0,1:T(8,128)}) fusion(f32[768]{0:T(1024)S(1)} %copy-done.10, f32[1024,768]{0,1:T(8,128)} %copy.25, bf16[3072,768]{1,0:T(8,128)(2,1)} %param.18, f32[3072]{0:T(1024)S(1)} %copy-done.9, bf16[768,3072]{1,0:T(8,128)(2,1)} %param.16, f32[768]{0:T(1024)S(1)} %copy-done.11, f32[768]{0:T(1024)S(1)} %copy-done.12, ...), kind=kOutput, calls=%fused_computation.59 | convolution fusion | flops 9692773376 | bytes 17335296 | tf_op jit(solution)/shard_map/dot_general | solution.py:310
  56.3 2.4 multiply_reduce_fusion
  58.7 0.0 copy-done
  58.7 0.4 copy-done.8
  59.1 0.0 copy-done.13
  59.1 0.0 copy-done.14
  59.1 1.4 multiply_reduce_fusion.2
  60.7 0.2 multiply_convert_fusion.2
  60.9 30.2 %all_to_all.68 = bf16[1,32,32,512]{3,2,0,1:T(8,128)(2,1)S(1)} all-to-all(bf16[1,32,32,512]{3,2,0,1:T(8,128)(2,1)S(1)} %bitcast.47), channel_id=1, replica_groups=mesh['img'=4,'tile'=8] {'tile'}, dimensions={1} | all-to-all | bytes 2097152 | tf_op jit(solution)/shard_map/all_to_all | solution.py:316
  91.1 4.5 %all-to-all-start.1 = ((bf16[16,256,512]{2,1,0:T(8,128)(2,1)}), bf16[16,256,512]{2,1,0:T(8,128)(2,1)}, u32[]{:S(2)}, u32[]{:S(2)}) async-start(bf16[16,256,512]{2,1,0:T(8,128)(2,1)} %bitcast.43), calls=%async_computation.1 | async-start | bytes 8388608 | tf_op jit(solution)/shard_map/all_to_all | solution.py:281
  95.7 0.1 copy.27.asked_ref
  95.8 10.6 %gather.3 = bf16[4096,512]{1,0:T(8,128)(2,1)} custom-call(s32[256,16]{1,0:T(8,128)S(1)} %copy.27.asked_ref, bf16[2048,512]{1,0:T(8,128)(2,1)S(1)} %copy-done.2), custom_call_target="tpu_custom_call" | custom-call | flops 10000000000 | bytes 10000000 | tf_op jit(solution)/shard_map/gather/pallas_call | solution.py:138
  106.4 18.3 %spread.2.weight_ref = bf16[1024,4096]{1,0:T(8,128)(2,1)} custom-call(s32[32,128]{1,0:T(8,128)S(1)} %get-tuple-element.59.own_ref, s32[32,128]{1,0:T(8,128)S(1)} %get-tuple-element.58.rank_ref, bf16[1024,128]{1,0:T(8,128)(2,1)} %collective-permute-done.1.weight_ref), custom_call_target="tpu_custom_call" | custom-call | flops 15000000512 | bytes 10000000 | tf_op jit(solution)/shard_map/spread/pallas_call | solution.py:108
  124.8 23.0 %all-to-all-done.1 = bf16[16,256,512]{2,1,0:T(8,128)(2,1)} async-done(((bf16[16,256,512]{2,1,0:T(8,128)(2,1)}), bf16[16,256,512]{2,1,0:T(8,128)(2,1)}, u32[]{:S(2)}, u32[]{:S(2)}) %all-to-all-start.1) | async-done | bytes 4194336 | tf_op jit(solution)/shard_map/all_to_all | solution.py:281
  147.7 5.9 %all-to-all-start.3 = ((bf16[16,256,512]{2,1,0:T(8,128)(2,1)}), bf16[16,256,512]{2,1,0:T(8,128)(2,1)}, u32[]{:S(2)}, u32[]{:S(2)}) async-start(bf16[16,256,512]{2,1,0:T(8,128)(2,1)} %bitcast.44), calls=%async_computation.3 | async-start | bytes 8388608 | tf_op jit(solution)/shard_map/all_to_all | solution.py:281
  153.6 0.0 copy-start.5
  153.6 8.2 %blend.2 = bf16[1024,512]{1,0:T(8,128)(2,1)S(1)} custom-call(bf16[1024,4096]{1,0:T(8,128)(2,1)} %spread.2.weight_ref, bf16[4096,512]{1,0:T(8,128)(2,1)} %bitcast.9.rows_ref), custom_call_target="tpu_custom_call" | custom-call | flops 8000000000 | bytes 10000000 | tf_op jit(solution)/shard_map/blend/pallas_call | solution.py:168
  161.8 1.0 collective-permute-start.2
  162.8 0.0 copy-done.5
  162.8 15.2 %spread.3.weight_ref = bf16[1024,4096]{1,0:T(8,128)(2,1)} custom-call(s32[32,128]{1,0:T(8,128)S(1)} %add_select_fusion.4.own_ref, s32[32,128]{1,0:T(8,128)S(1)} %get-tuple-element.31.rank_ref, bf16[1024,128]{1,0:T(8,128)(2,1)S(1)} %copy-done.5), custom_call_target="tpu_custom_call" | custom-call | flops 15000000512 | bytes 10000000 | tf_op jit(solution)/shard_map/spread/pallas_call | solution.py:108
  178.1 51.2 %collective-permute-done.2.part_ref = bf16[1024,512]{1,0:T(8,128)(2,1)S(1)} collective-permute-done((bf16[1024,512]{1,0:T(8,128)(2,1)S(1)}, bf16[1024,512]{1,0:T(8,128)(2,1)S(1)}, u32[]{:S(2)}, u32[]{:S(2)}) %collective-permute-start.2) | collective-permute-done | bytes 1048608 | tf_op jit(solution)/shard_map/ppermute | solution.py:278
  229.3 0.0 all-to-all-done.3
  229.3 9.0 %blend.3 = (bf16[1024,512]{1,0:T(8,128)(2,1)}, bf16[1024,512]{1,0:T(8,128)(2,1)S(1)}) custom-call(bf16[1024,4096]{1,0:T(8,128)(2,1)} %spread.3.weight_ref, bf16[4096,512]{1,0:T(8,128)(2,1)} %bitcast.13.rows_ref, bf16[1024,512]{1,0:T(8,128)(2,1)S(1)} %collective-permute-done.2.part_ref, bf16[1024,512]{1,0:T(8,128)(2,1)S(1)} %bitcast.35), custom_call_target="tpu_custom_call" | custom-call | flops 8000000000 | bytes 10000000 | tf_op jit(solution)/shard_map/blend/pallas_call | solution.py:168
  238.3 8.6 %terms.3 = bf16[4096,512]{1,0:T(8,128)(2,1)} custom-call(bf16[1024,4096]{1,0:T(8,128)(2,1)} %spread.3.weight_ref, bf16[1024,512]{1,0:T(8,128)(2,1)S(1)} %get-tuple-element.53.diff_ref), custom_call_target="tpu_custom_call" | custom-call | flops 8000000000 | bytes 10000000 | tf_op jit(solution)/shard_map/terms/pallas_call | solution.py:188
  246.9 4.8 %all-to-all-start.4 = ((bf16[16,256,512]{2,1,0:T(8,128)(2,1)}), bf16[16,256,512]{2,1,0:T(8,128)(2,1)}, u32[]{:S(2)}, u32[]{:S(2)}) async-start(bf16[16,256,512]{2,1,0:T(8,128)(2,1)} %bitcast.45), calls=%async_computation.4 | async-start | bytes 8388608 | tf_op jit(solution)/shard_map/all_to_all | solution.py:281
  251.7 3.0 collective-permute-start.3
  254.7 74.3 %collective-permute-done.3.diff_ref = bf16[1024,512]{1,0:T(8,128)(2,1)S(1)} collective-permute-done((bf16[1024,512]{1,0:T(8,128)(2,1)S(1)}, bf16[1024,512]{1,0:T(8,128)(2,1)S(1)}, u32[]{:S(2)}, u32[]{:S(2)}) %collective-permute-start.3) | collective-permute-done | bytes 1048608 | tf_op jit(solution)/shard_map/ppermute | solution.py:278
  328.9 8.6 %terms.2 = bf16[4096,512]{1,0:T(8,128)(2,1)} custom-call(bf16[1024,4096]{1,0:T(8,128)(2,1)} %spread.2.weight_ref, bf16[1024,512]{1,0:T(8,128)(2,1)S(1)} %collective-permute-done.3.diff_ref), custom_call_target="tpu_custom_call" | custom-call | flops 8000000000 | bytes 10000000 | tf_op jit(solution)/shard_map/terms/pallas_call | solution.py:188
  337.5 0.0 all-to-all-done.4
  337.5 4.5 %all-to-all-start.5 = ((bf16[16,256,512]{2,1,0:T(8,128)(2,1)}), bf16[16,256,512]{2,1,0:T(8,128)(2,1)}, u32[]{:S(2)}, u32[]{:S(2)}) async-start(bf16[16,256,512]{2,1,0:T(8,128)(2,1)} %bitcast.46), calls=%async_computation.5 | async-start | bytes 8388608 | tf_op jit(solution)/shard_map/all_to_all | solution.py:281
  342.0 12.6 %add_rows.2.rest_0_ = f32[2048,512]{1,0:T(8,128)} custom-call(s32[16,256]{1,0:T(8,128)S(1)} %reshape.111.asked_ref, bf16[4096,512]{1,0:T(8,128)(2,1)} %bitcast.16.terms_ref), custom_call_target="tpu_custom_call" | custom-call | flops 10000000000 | bytes 10000000 | tf_op jit(solution)/shard_map/add_rows/pallas_call | solution.py:220
  354.6 39.5 %all-to-all-done.5 = bf16[16,256,512]{2,1,0:T(8,128)(2,1)} async-done(((bf16[16,256,512]{2,1,0:T(8,128)(2,1)}), bf16[16,256,512]{2,1,0:T(8,128)(2,1)}, u32[]{:S(2)}, u32[]{:S(2)}) %all-to-all-start.5) | async-done | bytes 4194336 | tf_op jit(solution)/shard_map/all_to_all | solution.py:281
  394.1 12.9 %add_rows.3 = f32[2048,512]{1,0:T(8,128)} custom-call(s32[16,256]{1,0:T(8,128)S(1)} %reshape.109.asked_ref, bf16[4096,512]{1,0:T(8,128)(2,1)} %bitcast.18.terms_ref, f32[2048,512]{1,0:T(8,128)} %add_rows.2.rest_0_), custom_call_target="tpu_custom_call" | custom-call | flops 10000000000 | bytes 10000000 | tf_op jit(solution)/shard_map/add_rows/pallas_call | solution.py:220
  407.0 0.0 copy-done.1
  (24 shorter events, 0.2 us)
Async XLA Ops:
  0.6 58.1 %copy-start = (bf16[768,512]{1,0:T(8,128)(2,1)S(1)}, bf16[768,512]{1,0:T(8,128)(2,1)}, u32[]{:S(2)}) copy-start(bf16[768,512]{1,0:T(8,128)(2,1)} %param.22) | copy-start | bytes 2359300
  0.6 2.1 copy-start.3
  0.7 0.8 copy-start.6
  1.5 21.4 %copy-start.2 = (bf16[2048,512]{1,0:T(8,128)(2,1)S(1)}, bf16[2048,512]{1,0:T(8,128)(2,1)}, u32[]{:S(2)}) copy-start(bf16[2048,512]{1,0:T(8,128)(2,1)} %rows_ref.3) | copy-start | bytes 6291460
  3.4 19.3 %copy-start.4 = (bf16[1024,128]{1,0:T(8,128)(2,1)}, bf16[1024,128]{1,0:T(8,128)(2,1)S(1)}, u32[]{:S(2)}) copy-start(bf16[1024,128]{1,0:T(8,128)(2,1)S(1)} %weights.1.weight_ref) | copy-start | bytes 786436
  3.5 19.2 %collective-permute-start.1 = (bf16[1024,128]{1,0:T(8,128)(2,1)S(1)}, bf16[1024,128]{1,0:T(8,128)(2,1)}, u32[]{:S(2)}, u32[]{:S(2)}) collective-permute-start(bf16[1024,128]{1,0:T(8,128)(2,1)S(1)} %weights.1.weight_ref), channel_id=1, source_target_pairs={{0,6},{1,7},{2,4},{3,5},{4,2},{5,3},{6,0},{7,1},{8,14},{9,15},{10,... | collective-permute-start | bytes 786440 | tf_op jit(solution)/shard_map/ppermute | solution.py:278
  9.2 13.4 %all-to-all-start = ((s32[32,1,256]{2,1,0:T(1,128)}), s32[32,1,256]{2,1,0:T(1,128)S(1)}, u32[]{:S(2)}, u32[]{:S(2)}) async-start(s32[32,1,256]{2,1,0:T(1,128)} %copy.23), calls=%async_computation | async-start | bytes 65536 | tf_op jit(solution)/shard_map/all_to_all | solution.py:294
  12.0 10.6 %collective-permute-start = (s32[32,128]{1,0:T(8,128)S(1)}, s32[32,128]{1,0:T(8,128)S(1)}, u32[]{:S(2)}, u32[]{:S(2)}) collective-permute-start(s32[32,128]{1,0:T(8,128)S(1)} %multiply_add_fusion), channel_id=1, source_target_pairs={{0,6},{1,7},{2,4},{3,5},{4,2},{5,3},{6,0},{7,1},{8,14},{9,15},{10,... | collective-permute-start | bytes 49160 | tf_op jit(solution)/shard_map/ppermute | solution.py:278
  22.9 10.6 %copy-start.7 = (bf16[1,32,32,768]{3,2,1,0:T(8,128)(2,1)S(1)}, bf16[1,32,32,768]{3,2,1,0:T(8,128)(2,1)}, u32[]{:S(2)}) copy-start(bf16[1,32,32,768]{3,2,1,0:T(8,128)(2,1)} %param.13) | copy-start | bytes 4718596
  33.8 5.2 %copy-start.9 = (f32[3072]{0:T(1024)S(1)}, f32[3072]{0:T(1024)}, u32[]{:S(2)}) copy-start(f32[3072]{0:T(1024)} %param.17) | copy-start | bytes 36868
  33.8 5.2 %copy-start.10 = (f32[768]{0:T(1024)S(1)}, f32[768]{0:T(1024)}, u32[]{:S(2)}) copy-start(f32[768]{0:T(1024)} %param.19) | copy-start | bytes 9220
  33.8 5.2 %copy-start.11 = (f32[768]{0:T(1024)S(1)}, f32[768]{0:T(1024)}, u32[]{:S(2)}) copy-start(f32[768]{0:T(1024)} %param.15) | copy-start | bytes 9220
  33.8 5.2 %copy-start.12 = (f32[768]{0:T(1024)S(1)}, f32[768]{0:T(1024)}, u32[]{:S(2)}) copy-start(f32[768]{0:T(1024)} %param.14) | copy-start | bytes 9220
  56.3 2.8 copy-start.8
  56.3 2.8 copy-start.13
  56.3 2.8 copy-start.14
  91.1 56.6 %all-to-all-start.1 = ((bf16[16,256,512]{2,1,0:T(8,128)(2,1)}), bf16[16,256,512]{2,1,0:T(8,128)(2,1)}, u32[]{:S(2)}, u32[]{:S(2)}) async-start(bf16[16,256,512]{2,1,0:T(8,128)(2,1)} %bitcast.43), calls=%async_computation.1 | async-start | bytes 8388608 | tf_op jit(solution)/shard_map/all_to_all | solution.py:281
  147.7 81.6 %all-to-all-start.3 = ((bf16[16,256,512]{2,1,0:T(8,128)(2,1)}), bf16[16,256,512]{2,1,0:T(8,128)(2,1)}, u32[]{:S(2)}, u32[]{:S(2)}) async-start(bf16[16,256,512]{2,1,0:T(8,128)(2,1)} %bitcast.44), calls=%async_computation.3 | async-start | bytes 8388608 | tf_op jit(solution)/shard_map/all_to_all | solution.py:281
  153.6 9.2 %copy-start.5 = (bf16[1024,128]{1,0:T(8,128)(2,1)S(1)}, bf16[1024,128]{1,0:T(8,128)(2,1)}, u32[]{:S(2)}) copy-start(bf16[1024,128]{1,0:T(8,128)(2,1)} %copy-done.4) | copy-start | bytes 786436
  161.8 67.5 %collective-permute-start.2 = (bf16[1024,512]{1,0:T(8,128)(2,1)S(1)}, bf16[1024,512]{1,0:T(8,128)(2,1)S(1)}, u32[]{:S(2)}, u32[]{:S(2)}) collective-permute-start(bf16[1024,512]{1,0:T(8,128)(2,1)S(1)} %blend.2), channel_id=1, source_target_pairs={{0,6},{1,7},{2,4},{3,5},{4,2},{5,3},{6,0},{7,1},{8,14},{9,15},{10,... | collective-permute-start | bytes 3145736 | tf_op jit(solution)/shard_map/ppermute | solution.py:278
  246.9 90.6 %all-to-all-start.4 = ((bf16[16,256,512]{2,1,0:T(8,128)(2,1)}), bf16[16,256,512]{2,1,0:T(8,128)(2,1)}, u32[]{:S(2)}, u32[]{:S(2)}) async-start(bf16[16,256,512]{2,1,0:T(8,128)(2,1)} %bitcast.45), calls=%async_computation.4 | async-start | bytes 8388608 | tf_op jit(solution)/shard_map/all_to_all | solution.py:281
  251.7 77.2 %collective-permute-start.3 = (bf16[1024,512]{1,0:T(8,128)(2,1)S(1)}, bf16[1024,512]{1,0:T(8,128)(2,1)S(1)}, u32[]{:S(2)}, u32[]{:S(2)}) collective-permute-start(bf16[1024,512]{1,0:T(8,128)(2,1)S(1)} %get-tuple-element.53.diff_ref), channel_id=1, source_target_pairs={{0,6},{1,7},{2,4},{3,5},{4,2},{5,3},{6,0},{7,1},{8,14},{9,15},{10,... | collective-permute-start | bytes 3145736 | tf_op jit(solution)/shard_map/ppermute | solution.py:278
  337.5 56.6 %all-to-all-start.5 = ((bf16[16,256,512]{2,1,0:T(8,128)(2,1)}), bf16[16,256,512]{2,1,0:T(8,128)(2,1)}, u32[]{:S(2)}, u32[]{:S(2)}) async-start(bf16[16,256,512]{2,1,0:T(8,128)(2,1)} %bitcast.46), calls=%async_computation.5 | async-start | bytes 8388608 | tf_op jit(solution)/shard_map/all_to_all | solution.py:281
  394.1 12.9 %copy-start.1 = (bf16[768,512]{1,0:T(8,128)(2,1)S(1)}, bf16[768,512]{1,0:T(8,128)(2,1)}, u32[]{:S(2)}) copy-start(bf16[768,512]{1,0:T(8,128)(2,1)} %param.22) | copy-start | bytes 2359300

commit v3 on v1

v3 whole, which is shorter than its diff:
```python
import functools

import jax
import jax.numpy as jnp
from jax import lax
from jax.experimental import pallas as pl
from jax.experimental.pallas import tpu as pltpu
from jax.sharding import PartitionSpec as P

F32 = jnp.float32
BF16 = jnp.bfloat16
I32 = jnp.int32
VMEM_BYTES = 50 * 1024 * 1024
LANES = (((1,), (1,)), ((), ()))
ROWS = (((0,), (0,)), ((), ()))


def params():
    return pltpu.CompilerParams(vmem_limit_bytes=VMEM_BYTES)


def index_kernel(peers, cap, rows_held, ids_ref, req_ref, own_ref, rank_ref):
    tiles, length = ids_ref.shape
    earlier = lax.broadcasted_iota(I32, (length, length), 0)
    later = lax.broadcasted_iota(I32, (length, length), 1)
    upper = (earlier < later).astype(BF16)
    every = jnp.ones((length, length), BF16)
    peer_id = lax.broadcasted_iota(I32, (peers, length), 0)
    slot_id = lax.broadcasted_iota(I32, (cap, length), 0)
    hots = []
    for t in range(tiles):
        owner = ids_ref[t : t + 1, :] // rows_held
        own_ref[t : t + 1, :] = owner.astype(F32).astype(BF16)
        hots.append((jnp.broadcast_to(owner, (peers, length)) == peer_id).astype(F32))
    stack = jnp.concatenate(hots, 0).astype(BF16)
    within = jnp.dot(stack, upper, preferred_element_type=F32)
    totals = jnp.dot(stack, every, preferred_element_type=F32)
    offset = jnp.zeros((peers, length), F32)
    found = jnp.zeros((2 * peers, cap), F32)
    for t in range(tiles):
        own_rows = slice(t * peers, (t + 1) * peers)
        rank = jnp.sum(hots[t] * (within[own_rows] + offset), axis=0, keepdims=True).astype(I32)
        offset = offset + totals[own_rows]
        rank_ref[t : t + 1, :] = rank.astype(F32).astype(BF16)
        ids = ids_ref[t : t + 1, :]
        row = ids - (ids // rows_held) * rows_held + 1
        high = (row >> 6).astype(F32)
        low = (row & 63).astype(F32)
        digits = jnp.concatenate([hots[t] * high, hots[t] * low], 0).astype(BF16)
        slots = (jnp.broadcast_to(rank, (cap, length)) == slot_id).astype(F32).astype(BF16)
        found = found + lax.dot_general(digits, slots, LANES, preferred_element_type=F32)
    req_ref[...] = (found[:peers] * 64.0 + found[peers:]).astype(I32) - 1


def index(ids, peers, cap, rows_held):
    like = jax.ShapeDtypeStruct(ids.shape, BF16)
    return pl.pallas_call(
        functools.partial(index_kernel, peers, cap, rows_held),
        out_shape=(jax.ShapeDtypeStruct((peers, cap), I32), like, like),
        compiler_params=params(),
        cost_estimate=pl.CostEstimate(flops=10**9, bytes_accessed=10**7, transcendentals=0),
        name="index",
    )(ids)


def weights_kernel(alpha_ref, out_ref):
    alpha = alpha_ref[...]
    length = alpha.shape[1]
    logs = jnp.log1p(-alpha)
    earlier = lax.broadcasted_iota(I32, (length, length), 0)
    later = lax.broadcasted_iota(I32, (length, length), 1)
    upper = (earlier < later).astype(F32)
    before = jnp.dot(logs, upper, preferred_element_type=F32, precision=lax.Precision.HIGHEST)
    out_ref[...] = (alpha * jnp.exp(before)).astype(BF16)


def weights(alphas):
    return pl.pallas_call(
        weights_kernel,
        out_shape=jax.ShapeDtypeStruct(alphas.shape, BF16),
        compiler_params=params(),
        cost_estimate=pl.CostEstimate(flops=10**9, bytes_accessed=10**7, transcendentals=0),
        name="weights",
    )(alphas)


def spread_kernel(near, cap, base_ref, own_ref, rank_ref, weight_ref, out_ref):
    tiles, length = own_ref.shape
    cells = weight_ref.shape[0] // tiles
    slot_id = lax.broadcasted_iota(I32, (cap, length), 0)
    for t in range(tiles):
        own = own_ref[t : t + 1, :].astype(I32)
        rank = rank_ref[t : t + 1, :].astype(I32)
        here = slice(t * cells, (t + 1) * cells)
        weight = weight_ref[here, :].astype(F32)
        by_owner = [jnp.where(own == base_ref[o], weight, 0.0) for o in range(near)]
        slots = (jnp.broadcast_to(rank, (cap, length)) == slot_id).astype(F32).astype(BF16)
        moved = lax.dot_general(
            jnp.concatenate(by_owner, 0).astype(BF16), slots, LANES, preferred_element_type=F32
        ).astype(BF16)
        if cap % 128 == 0:
            for o in range(near):
                out_ref[here, o * cap : (o + 1) * cap] = moved[o * cells : (o + 1) * cells]
        else:
            out_ref[here, :] = jnp.concatenate([moved[o * cells : (o + 1) * cells] for o in range(near)], 1)


def spread(owners, own, rank, weight, cap):
    tiles, length = own.shape
    cells = weight.shape[0] // tiles
    near = owners.shape[0]
    step = 16
    lists = pl.BlockSpec((step, length), lambda t: (t, 0))
    return pl.pallas_call(
        functools.partial(spread_kernel, near, cap),
        grid=(tiles // step,),
        in_specs=[pl.BlockSpec(memory_space=pltpu.SMEM), lists, lists, pl.BlockSpec((step * cells, length), lambda t: (t, 0))],
        out_specs=pl.BlockSpec((step * cells, near * cap), lambda t: (t, 0)),
        out_shape=jax.ShapeDtypeStruct((weight.shape[0], near * cap), BF16),
        compiler_params=params(),
        cost_estimate=pl.CostEstimate(flops=7 * 10**9, bytes_accessed=10**7, transcendentals=0),
        name="spread",
    )(owners, own, rank, weight)


def gather_kernel(group, cap, asked_ref, rows_ref, out_ref):
    first = pl.program_id(0) * group
    asked = asked_ref[...]
    peer = lax.broadcasted_iota(I32, asked.shape, 1)
    held = rows_ref.shape[0]
    row_id = lax.broadcasted_iota(I32, (cap, held), 1)
    picks = []
    for q in range(group):
        column = jnp.sum(jnp.where(peer == first + q, asked, 0), axis=1, keepdims=True)
        picks.append((jnp.broadcast_to(column, (cap, held)) == row_id).astype(F32).astype(BF16))
    pick = jnp.concatenate(picks, 0)
    out_ref[...] = jnp.dot(pick, rows_ref[...], preferred_element_type=F32).astype(BF16)


def gather(asked, rows):
    near, cap = asked.shape
    held, feat = rows.shape
    group = max(1, min(near, 1024 // cap))
    return pl.pallas_call(
        functools.partial(gather_kernel, group, cap),
        grid=(near // group,),
        in_specs=[pl.BlockSpec((cap, near), lambda i: (0, 0)), pl.BlockSpec((held, feat), lambda i: (0, 0))],
        out_specs=pl.BlockSpec((group * cap, feat), lambda i: (i, 0)),
        out_shape=jax.ShapeDtypeStruct((near * cap, feat), BF16),
        compiler_params=params(),
        cost_estimate=pl.CostEstimate(flops=10**10, bytes_accessed=10**7, transcendentals=0),
        name="gather",
    )(asked.T, rows)


def blend_kernel(n_parts, weight_ref, rows_ref, *rest):
    color = jnp.dot(weight_ref[...], rows_ref[...], preferred_element_type=F32)
    for part_ref in rest[:n_parts]:
        color = color + part_ref[...].astype(F32)
    if len(rest) == n_parts + 1:
        rest[n_parts][...] = color.astype(BF16)
    else:
        target_ref, color_ref, diff_ref = rest[n_parts:]
        color_ref[...] = color.astype(BF16)
        diff_ref[...] = (color - target_ref[...].astype(F32)).astype(BF16)


def blend(weight, rows, parts=(), target=None):
    cells, slots = weight.shape
    feat = rows.shape[1]
    block = min(cells, 256)
    cell_block = pl.BlockSpec((block, feat), lambda i: (i, 0))
    out = jax.ShapeDtypeStruct((cells, feat), BF16)
    more = tuple(parts) + (() if target is None else (target,))
    return pl.pallas_call(
        functools.partial(blend_kernel, len(parts)),
        grid=(cells // block,),
        in_specs=[pl.BlockSpec((block, slots), lambda i: (i, 0)), pl.BlockSpec((slots, feat), lambda i: (0, 0))]
        + [cell_block] * len(more),
        out_specs=cell_block if target is None else (cell_block, cell_block),
        out_shape=out if target is None else (out, out),
        compiler_params=params(),
        cost_estimate=pl.CostEstimate(flops=4 * 10**9, bytes_accessed=10**7, transcendentals=0),
        name="blend",
    )(weight, rows, *more)


def terms_kernel(weight_ref, *refs):
    diff = refs[0][...]
    for more_ref in refs[1:-1]:
        diff = diff + more_ref[...]
    refs[-1][...] = lax.dot_general(weight_ref[...], diff, ROWS, preferred_element_type=F32).astype(BF16)


def terms(weight, *diffs):
    cells, slots = weight.shape
    feat = diffs[0].shape[1]
    block = min(slots, 1024)
    return pl.pallas_call(
        terms_kernel,
        grid=(slots // block,),
        in_specs=[pl.BlockSpec((cells, block), lambda i: (0, i))]
        + [pl.BlockSpec((cells, feat), lambda i: (0, 0))] * len(diffs),
        out_specs=pl.BlockSpec((block, feat), lambda i: (i, 0)),
        out_shape=jax.ShapeDtypeStruct((slots, feat), BF16),
        compiler_params=params(),
        cost_estimate=pl.CostEstimate(flops=4 * 10**9, bytes_accessed=10**7, transcendentals=0),
        name="terms",
    )(weight, *diffs)


def add_rows_kernel(count, *refs):
    out_ref = refs[-1]
    block = out_ref.shape[0]
    total = None if len(refs) == 2 * count + 1 else refs[2 * count][...]
    for n in range(count):
        asked_ref, terms_ref = refs[n], refs[count + n]
        near, cap = asked_ref.shape
        row_id = lax.broadcasted_iota(I32, (block, cap), 0) + pl.program_id(0) * block
        picks = []
        for o in range(near):
            asked = jnp.broadcast_to(asked_ref[o : o + 1, :], (block, cap))
            picks.append((asked == row_id).astype(F32).astype(BF16))
        got = jnp.dot(jnp.concatenate(picks, 1), terms_ref[...], preferred_element_type=F32)
        total = got if total is None else total + got
    out_ref[...] = total


def add_rows(askeds, arrivals, held, before=None):
    near, cap = askeds[0].shape
    feat = arrivals[0].shape[1]
    count = len(askeds)
    block = min(held, 512)
    row_block = pl.BlockSpec((block, feat), lambda i: (i, 0))
    more = before is not None
    in_specs = [pl.BlockSpec((near, cap), lambda i: (0, 0))] * count
    in_specs += [pl.BlockSpec((near * cap, feat), lambda i: (0, 0))] * count
    return pl.pallas_call(
        functools.partial(add_rows_kernel, count),
        grid=(held // block,),
        in_specs=in_specs + [row_block] * more,
        out_specs=row_block,
        out_shape=jax.ShapeDtypeStruct((held, feat), F32),
        compiler_params=params(),
        cost_estimate=pl.CostEstimate(flops=5 * count * 10**9, bytes_accessed=10**7, transcendentals=0),
        name="add_rows",
    )(*askeds, *arrivals, *((before,) if more else ()))


def layer_norm(rows, gain, bias):
    mean = jnp.mean(rows, axis=-1, keepdims=True)
    centred = rows - mean
    var = jnp.mean(centred * centred, axis=-1, keepdims=True)
    return centred * lax.rsqrt(var + 1e-05) * gain + bias


def on_device(
    patches,
    norm_gain,
    norm_bias,
    up_weight,
    up_bias,
    down_weight,
    down_bias,
    final_gain,
    final_bias,
    head_weight,
    gauss_rows,
    tile_lists,
    alphas,
):
    view_count, tiles_view, cells, width = patches.shape
    feat = head_weight.shape[1]
    n_img = lax.axis_size("img")
    n_tile = lax.axis_size("tile")
    peers = n_img * n_tile
    both = ("img", "tile")
    held = gauss_rows.shape[0]
    group_views, strip_tiles, list_len = tile_lists.shape
    tiles = group_views * strip_tiles
    cap = 2 * tiles * list_len // peers

    wide_layer = n_tile // 4
    near = n_img * wide_layer
    tile = lax.axis_index("tile")
    layer = tile // wide_layer
    low = layer < 2
    outer = (layer == 0) | (layer == 3)
    groups = [[i * n_tile + z * wide_layer + k for i in range(n_img) for k in range(wide_layer)] for z in range(4)]

    def moves(*pairs):
        return [(a * wide_layer + k, b * wide_layer + k) for a, b in pairs for k in range(wide_layer)]

    beside = moves((0, 1), (1, 0), (2, 3), (3, 2))
    middle = moves((1, 2), (2, 1))
    inwards = moves((0, 1), (3, 2))
    outwards = moves((1, 0), (2, 3))

    def move(x, pairs):
        return lax.ppermute(x, "tile", pairs)

    def exchange(x):
        return lax.all_to_all(x, both, split_axis=0, concat_axis=0, axis_index_groups=groups, tiled=True)

    request, own, rank = index(tile_lists.reshape(tiles, list_len), peers, cap, held)
    weight = weights(alphas.reshape(tiles * cells, list_len))
    packed = jnp.concatenate([weight, own, rank], 0)
    request, packed = lax.optimization_barrier((request, packed))
    from_beside = move(packed, beside)
    from_two = move(packed, moves((0, 2), (2, 0), (1, 3), (3, 1)))
    from_three = move(packed, moves((0, 3), (3, 0), (1, 2), (2, 1)))
    asked = lax.all_to_all(request, both, split_axis=0, concat_axis=0, tiled=True)
    asked = asked.reshape(n_img, 4, wide_layer, cap)
    sets = (jnp.where(low, 3, 0), jnp.where(low, 2, 1), layer ^ 1, layer)
    lists = [lax.dynamic_index_in_dim(asked, s, 1, keepdims=False).reshape(near, cap) for s in sets]
    packs = (
        jnp.where(outer, from_three, from_two),
        jnp.where(outer, from_two, from_three),
        from_beside,
        packed,
    )
    owners = (
        jnp.arange(n_img, dtype=I32)[:, None] * n_tile
        + layer * wide_layer
        + jnp.arange(wide_layer, dtype=I32)[None, :]
    ).reshape(near)

    def spread_of(pack):
        n_cells = tiles * cells
        return spread(owners, pack[n_cells : n_cells + tiles], pack[n_cells + tiles :], pack[:n_cells], cap)

    rows = []
    for n in range(4):
        looked = gather(lists[n], gauss_rows)
        if n:
            looked, rows[-1] = lax.optimization_barrier((looked, rows[-1]))
        rows.append(exchange(looked))

    wide = patches.reshape(-1, width).astype(F32)
    normed = layer_norm(wide, norm_gain, norm_bias).astype(BF16)
    inner = jnp.dot(normed, up_weight, preferred_element_type=F32) + up_bias
    act = (inner * jax.nn.sigmoid(1.702 * inner)).astype(BF16)
    block_out = wide + jnp.dot(act, down_weight, preferred_element_type=F32) + down_bias
    final = layer_norm(block_out, final_gain, final_bias).astype(BF16)
    embed = jnp.dot(final, head_weight, preferred_element_type=F32)
    scale = lax.rsqrt(jnp.mean(embed * embed, axis=-1, keepdims=True) + 1e-06)
    strips = (embed * scale).astype(BF16).reshape(n_tile, -1, feat)
    arrived = []
    for n in reversed(range(n_tile)):
        strip = lax.dynamic_index_in_dim(strips, lax.rem(tile + n, n_tile), 0, keepdims=True)
        arrived.append(lax.ppermute(strip, "tile", [(a, (a + n) % n_tile) for a in range(n_tile)]) if n else strip)
    first = lax.rem(2 * n_tile - 1 - tile, n_tile)
    target = lax.dynamic_slice_in_dim(jnp.concatenate(arrived + arrived, 0), first, n_tile, 0)
    target = target.reshape(tiles * cells, feat)

    spreads = [spread_of(pack) for pack in packs]
    part = blend(spreads[0], rows[0])
    far = move(part + move(part, inwards), middle)
    part = blend(spreads[1], rows[1])
    middle_part = move(part + move(part, inwards), middle)
    beside_part = move(blend(spreads[2], rows[2], (far,)), beside)
    color, diff = blend(spreads[3], rows[3], (beside_part, middle_part), target)

    diff_beside = move(diff, beside)
    diff_middle = move(diff, middle)
    far_middle = move(diff_beside, middle)
    diff_out = move(diff_middle, outwards)
    far_out = move(far_middle, outwards)
    back = []
    for n, diffs in ((3, (diff,)), (2, (diff_beside,)), (1, (diff_middle, diff_out)), (0, (far_middle, far_out))):
        term = terms(spreads[n], *diffs)
        if back:
            term, back[-1] = lax.optimization_barrier((term, back[-1]))
        back.append(exchange(term))
    grad = add_rows([lists[3], lists[2], lists[1]], back[:3], held)
    grad = add_rows([lists[0]], back[3:], held, grad)
    return (color.reshape(group_views, strip_tiles, cells, feat), grad)


def solution(mesh):
    placed = (
        P(("img", "tile"), None, None, None),
        P(),
        P(),
        P(),
        P(),
        P(),
        P(),
        P(),
        P(),
        P(),
        P(("img", "tile"), None),
        P("img", "tile", None),
        P("img", "tile", None, None),
    )
    return jax.shard_map(
        on_device,
        mesh=mesh,
        in_specs=placed,
        out_specs=(P("img", "tile", None, None), P(("img", "tile"), None)),
        check_vma=False,
    )
```

time: 410 us -> 388 us (0.946)
  waiting for transfers between devices: 224 us -> 142 us
  starting transfers between devices: 38.1 us -> 71.9 us
  local copies, waits for them, and re-layouts: 5.42 us -> 31.5 us
    all_to_all x4 -> x8, waiting for transfers between devices: 61.8 us -> 24.7 us  [exchange(): lax.all_to_all(x, both, split_axis=0, concat_axis=0, axis_index_groups=gr...]
    ppermute x4 -> x20, starting transfers between devices: 7.67 us -> 36.2 us  [the longest x13 28.7 us: move(): return lax.ppermute(x, 'tile', pairs)]
    ppermute x4 -> x20, waiting for transfers between devices: 140 us -> 114 us  [the longest x13 113 us: move(): return lax.ppermute(x, 'tile', pairs)]
    unnamed x24 -> x68, local copies, waits for them, and re-layouts: 1.31 us -> 22.8 us
    all_to_all x1 -> x0, waiting for transfers between devices: 15.9 us -> none  [on_device(): lax.all_to_all(target, 'tile', split_axis=1, concat_axis=0, tiled=True)]
    all_to_all x4 -> x8, starting transfers between devices: 19.4 us -> 32.8 us  [exchange(): lax.all_to_all(x, both, split_axis=0, concat_axis=0, axis_index_groups=gr...]
    pallas_call x6 -> x10, Pallas kernels: 73.2 us -> 61.3 us  [the longest x2 25.3 us: add_rows(): pl.pallas_call(functools.partial(add_rows_kernel, count), grid=(held // b...]
    pallas_call x2 -> x4, Pallas kernels: 21.2 us -> 27.6 us  [gather(): pl.pallas_call(functools.partial(gather_kernel, group, cap), grid=(near /...]
  transfers between devices with their start and end apart: 10 -> 29, of which waited for: 7 -> 10; matrix products, arithmetic and copies ran while one was open for 7% -> 12% of each run, Pallas kernels for 17% -> 23%
where the time goes in v3:
time: 388 us; the launch traced here: 383 us
  waiting for transfers between devices  142 us (37%)
  Pallas kernels  110 us (28%)
  starting transfers between devices  71.9 us (19%)
  local copies, waits for them, and re-layouts  31.5 us (8%)
  matrix products  18.3 us (5%)
  other arithmetic  7.49 us (2%)
    ppermute x13, waiting for transfers between devices, move(): return lax.ppermute(x, 'tile', pairs)  113 us
    all_to_all x8, starting transfers between devices, exchange(): lax.all_to_all(x, both, split_axis=0, concat_axis=0, axis_index_groups=gr...  32.8 us
    ppermute x13, starting transfers between devices, move(): return lax.ppermute(x, 'tile', pairs)  28.7 us
    pallas_call x4, Pallas kernels, gather(): pl.pallas_call(functools.partial(gather_kernel, group, cap), grid=(near /...  27.6 us
    pallas_call x2, Pallas kernels, add_rows(): pl.pallas_call(functools.partial(add_rows_kernel, count), grid=(held // b...  25.3 us
    all_to_all x8, waiting for transfers between devices, exchange(): lax.all_to_all(x, both, split_axis=0, concat_axis=0, axis_index_groups=gr...  24.7 us
    unnamed x68, local copies, waits for them, and re-layouts  22.8 us
    pallas_call x4, Pallas kernels, blend(): pl.pallas_call(functools.partial(blend_kernel, len(parts)), grid=(cells /...  22.2 us
  transfers between devices with their start and end apart: 29, of which 10 were waited for; matrix products, arithmetic and copies ran while one was open for 12% of the time, Pallas kernels for 23%

profile of v3, /device:TPU:0, one launch (start us, length us, event | category | flops | bytes accessed | tf_op | source)
XLA Modules:
  0.0 383.1 jit_solution(9143633301670227682)
XLA Ops:
  1.5 1.3 index.1
  3.5 5.1 %collective-permute-start.1 = (bf16[1088,128]{1,0:T(8,128)(2,1)S(1)}, bf16[1088,128]{1,0:T(8,128)(2,1)}, u32[]{:S(2)}, u32[]{:S(2)}) collective-permute-start(bf16[1088,128]{1,0:T(8,128)(2,1)S(1)} %pad_maximum_fusion), channel_id=1, source_target_pairs={{0,6},{1,7},{6,0},{7,1},{2,4},{3,5},{4,2},{5,3},{8,14},{9,15},{14,... | collective-permute-start | bytes 835592 | tf_op jit(solution)/shard_map/ppermute | solution.py:300
  10.2 2.6 copy.42
  13.0 16.7 %fusion.17 = (f32[1024]{0:T(1024)S(1)}, f32[1024,768]{0,1:T(8,128)}) fusion(f32[768]{0:T(1024)S(1)} %copy-done.21, f32[1024,768]{0,1:T(8,128)} %copy.42, bf16[3072,768]{1,0:T(8,128)(2,1)} %param.18, f32[3072]{0:T(1024)S(1)} %copy-done.20, bf16[768,3072]{1,0:T(8,128)(2,1)} %param.16, f32[768]{0:T(1024)S(1)} %copy-done.22, f32[768]{0:T(1024)S(1)} %copy-done.23, ...), kind=kOutput, calls=%fused_computation.64 | convolution fusion | flops 9692773376 | bytes 17335296 | tf_op jit(solution)/shard_map/dot_general | solution.py:343
  29.7 2.4 multiply_reduce_fusion
  32.6 1.5 multiply_reduce_fusion.2
  36.3 2.3 collective-permute-start.8
  38.6 1.4 collective-permute-start.9
  40.6 2.9 all-to-all-start
  43.8 3.3 spread.4.weight_ref
  47.1 3.7 all-to-all-done
  51.0 6.4 %gather.7 = bf16[2048,512]{1,0:T(8,128)(2,1)S(1)} custom-call(s32[256,8]{1,0:T(8,128)S(1)} %copy.41.asked_ref, bf16[2048,512]{1,0:T(8,128)(2,1)} %rows_ref.7), custom_call_target="tpu_custom_call" | custom-call | flops 10000000000 | bytes 10000000 | tf_op jit(solution)/shard_map/gather/pallas_call | solution.py:144
  57.5 1.3 copy-done.5
  58.8 3.6 all-to-all-start.1
  62.6 6.4 %gather.6 = bf16[2048,512]{1,0:T(8,128)(2,1)S(1)} custom-call(s32[256,8]{1,0:T(8,128)S(1)} %copy.39.asked_ref, bf16[2048,512]{1,0:T(8,128)(2,1)} %rows_ref.7), custom_call_target="tpu_custom_call" | custom-call | flops 10000000000 | bytes 10000000 | tf_op jit(solution)/shard_map/gather/pallas_call | solution.py:144
  69.0 1.4 copy-done.4
  70.7 7.4 %gather.5 = bf16[2048,512]{1,0:T(8,128)(2,1)} custom-call(s32[256,8]{1,0:T(8,128)S(1)} %copy.37.asked_ref, bf16[2048,512]{1,0:T(8,128)(2,1)} %rows_ref.7), custom_call_target="tpu_custom_call" | custom-call | flops 10000000000 | bytes 10000000 | tf_op jit(solution)/shard_map/gather/pallas_call | solution.py:144
  78.1 7.4 %gather.4 = bf16[2048,512]{1,0:T(8,128)(2,1)} custom-call(s32[256,8]{1,0:T(8,128)S(1)} %copy.35.asked_ref, bf16[2048,512]{1,0:T(8,128)(2,1)} %rows_ref.7), custom_call_target="tpu_custom_call" | custom-call | flops 10000000000 | bytes 10000000 | tf_op jit(solution)/shard_map/gather/pallas_call | solution.py:144
  86.6 2.4 all-to-all-done.1
  89.0 1.4 copy-done.2
  90.4 3.6 all-to-all-start.2
  95.5 2.4 collective-permute-start.13
  99.0 3.4 spread.6.weight_ref
  102.4 4.7 %blend.4 = bf16[1024,512]{1,0:T(8,128)(2,1)S(1)} custom-call(bf16[1024,2048]{1,0:T(8,128)(2,1)} %spread.6.weight_ref, bf16[2048,512]{1,0:T(8,128)(2,1)S(1)} %bitcast.53), custom_call_target="tpu_custom_call" | custom-call | flops 4000000000 | bytes 10000000 | tf_op jit(solution)/shard_map/blend/pallas_call | solution.py:175
  108.0 12.5 %all-to-all-done.2 = bf16[8,256,512]{2,1,0:T(8,128)(2,1)S(1)} async-done(((bf16[8,256,512]{2,1,0:T(8,128)(2,1)}), bf16[8,256,512]{2,1,0:T(8,128)(2,1)S(1)}, u32[]{:S(2)}, u32[]{:S(2)}) %all-to-all-start.2) | async-done | bytes 2097184 | tf_op jit(solution)/shard_map/all_to_all | solution.py:303
  120.6 4.3 %all-to-all-start.3 = ((bf16[8,256,512]{2,1,0:T(8,128)(2,1)}), bf16[8,256,512]{2,1,0:T(8,128)(2,1)}, u32[]{:S(2)}, u32[]{:S(2)}) async-start(bf16[8,256,512]{2,1,0:T(8,128)(2,1)} %bitcast.11), calls=%async_computation.3 | async-start | bytes 4194304 | tf_op jit(solution)/shard_map/all_to_all | solution.py:303
  124.9 2.5 collective-permute-start.3
  128.1 1.6 constant_dynamic-update-slice_fusion.10
  129.7 1.6 constant_dynamic-update-slice_fusion.9
  131.3 1.6 constant_dynamic-update-slice_fusion.8
  132.9 3.6 spread.7.weight_ref
  136.5 14.6 %collective-permute-done.3 = bf16[1024,512]{1,0:T(8,128)(2,1)S(1)} collective-permute-done((bf16[1024,512]{1,0:T(8,128)(2,1)}, bf16[1024,512]{1,0:T(8,128)(2,1)S(1)}, u32[]{:S(2)}, u32[]{:S(2)}) %collective-permute-start.3) | collective-permute-done | bytes 1048608 | tf_op jit(solution)/shard_map/ppermute | solution.py:300
  152.4 1.6 collective-permute-start.4
  154.0 5.5 %blend.6 = bf16[1024,512]{1,0:T(8,128)(2,1)} custom-call(bf16[1024,2048]{1,0:T(8,128)(2,1)} %spread.7.weight_ref, bf16[2048,512]{1,0:T(8,128)(2,1)S(1)} %bitcast.51), custom_call_target="tpu_custom_call" | custom-call | flops 4000000000 | bytes 10000000 | tf_op jit(solution)/shard_map/blend/pallas_call | solution.py:175
  159.5 5.1 %collective-permute-start.6 = (bf16[1024,512]{1,0:T(8,128)(2,1)}, bf16[1024,512]{1,0:T(8,128)(2,1)S(1)}, u32[]{:S(2)}, u32[]{:S(2)}) collective-permute-start(bf16[1024,512]{1,0:T(8,128)(2,1)} %blend.6), channel_id=1, source_target_pairs={{0,2},{1,3},{6,4},{7,5},{8,10},{9,11},{14,12},{15,13},{16,18},{17,... | collective-permute-start | bytes 3145736 | tf_op jit(solution)/shard_map/ppermute | solution.py:300
  165.4 1.6 dynamic-slice_dynamic-update-slice_fusion
  168.6 4.3 %all-to-all-start.4 = ((bf16[8,256,512]{2,1,0:T(8,128)(2,1)}), bf16[8,256,512]{2,1,0:T(8,128)(2,1)}, u32[]{:S(2)}, u32[]{:S(2)}) async-start(bf16[8,256,512]{2,1,0:T(8,128)(2,1)} %bitcast.13), calls=%async_computation.4 | async-start | bytes 4194304 | tf_op jit(solution)/shard_map/all_to_all | solution.py:303
  173.0 3.5 spread.5.weight_ref
  176.4 9.7 %collective-permute-done.6 = bf16[1024,512]{1,0:T(8,128)(2,1)S(1)} collective-permute-done((bf16[1024,512]{1,0:T(8,128)(2,1)}, bf16[1024,512]{1,0:T(8,128)(2,1)S(1)}, u32[]{:S(2)}, u32[]{:S(2)}) %collective-permute-start.6) | collective-permute-done | bytes 1048608 | tf_op jit(solution)/shard_map/ppermute | solution.py:300
  186.2 1.5 add.169
  188.6 5.5 %blend.5 = bf16[1024,512]{1,0:T(8,128)(2,1)S(1)} custom-call(bf16[1024,2048]{1,0:T(8,128)(2,1)} %spread.5.weight_ref, bf16[2048,512]{1,0:T(8,128)(2,1)} %bitcast.12.rows_ref, bf16[1024,512]{1,0:T(8,128)(2,1)} %collective-permute-done.4.rest_0_), custom_call_target="tpu_custom_call" | custom-call | flops 4000000000 | bytes 10000000 | tf_op jit(solution)/shard_map/blend/pallas_call | solution.py:175
  194.1 5.1 %collective-permute-start.5 = (bf16[1024,512]{1,0:T(8,128)(2,1)S(1)}, bf16[1024,512]{1,0:T(8,128)(2,1)S(1)}, u32[]{:S(2)}, u32[]{:S(2)}) collective-permute-start(bf16[1024,512]{1,0:T(8,128)(2,1)S(1)} %blend.5), channel_id=1, source_target_pairs={{0,2},{1,3},{2,0},{3,1},{4,6},{5,7},{6,4},{7,5},{8,10},{9,11},{10,... | collective-permute-start | bytes 3145736 | tf_op jit(solution)/shard_map/ppermute | solution.py:300
  204.1 16.1 %collective-permute-done.5.rest_0_ = bf16[1024,512]{1,0:T(8,128)(2,1)S(1)} collective-permute-done((bf16[1024,512]{1,0:T(8,128)(2,1)S(1)}, bf16[1024,512]{1,0:T(8,128)(2,1)S(1)}, u32[]{:S(2)}, u32[]{:S(2)}) %collective-permute-start.5) | collective-permute-done | bytes 1048608 | tf_op jit(solution)/shard_map/ppermute | solution.py:300
  220.2 6.5 %blend.7 = (bf16[1024,512]{1,0:T(8,128)(2,1)}, bf16[1024,512]{1,0:T(8,128)(2,1)S(1)}) custom-call(bf16[1024,2048]{1,0:T(8,128)(2,1)} %spread.4.weight_ref, bf16[2048,512]{1,0:T(8,128)(2,1)} %bitcast.14.rows_ref, bf16[1024,512]{1,0:T(8,128)(2,1)S(1)} %collective-permute-done.5.rest_0_, bf16[1024,512]{1,0:T(8,128)(2,1)S(1)} %collective-permute-done.7.rest_1_, ...), custom_call_target="tpu_custom_call" | custom-call | flops 4000000000 | bytes 10000000 | tf_op jit(solution)/shard_map/blend/pallas_call | solution.py:175
  226.7 4.6 %terms.7 = bf16[2048,512]{1,0:T(8,128)(2,1)S(1)} custom-call(bf16[1024,2048]{1,0:T(8,128)(2,1)} %spread.4.weight_ref, bf16[1024,512]{1,0:T(8,128)(2,1)S(1)} %get-tuple-element.33.refs_0_), custom_call_target="tpu_custom_call" | custom-call | flops 4000000000 | bytes 10000000 | tf_op jit(solution)/shard_map/terms/pallas_call | solution.py:199
  231.3 1.3 copy-done.7
  232.6 3.6 all-to-all-start.5
  236.2 1.8 collective-permute-start.15
  238.0 1.6 collective-permute-start.18
  239.6 22.2 %collective-permute-done.15.refs_0_ = bf16[1024,512]{1,0:T(8,128)(2,1)S(1)} collective-permute-done((bf16[1024,512]{1,0:T(8,128)(2,1)}, bf16[1024,512]{1,0:T(8,128)(2,1)S(1)}, u32[]{:S(2)}, u32[]{:S(2)}) %collective-permute-start.15) | collective-permute-done | bytes 1048608 | tf_op jit(solution)/shard_map/ppermute | solution.py:300
  261.9 4.2 %terms.6 = bf16[2048,512]{1,0:T(8,128)(2,1)S(1)} custom-call(bf16[1024,2048]{1,0:T(8,128)(2,1)} %spread.5.weight_ref, bf16[1024,512]{1,0:T(8,128)(2,1)S(1)} %collective-permute-done.15.refs_0_), custom_call_target="tpu_custom_call" | custom-call | flops 4000000000 | bytes 10000000 | tf_op jit(solution)/shard_map/terms/pallas_call | solution.py:199
  266.1 1.4 copy-done.6
  268.5 4.4 %all-to-all-start.6 = ((bf16[8,256,512]{2,1,0:T(8,128)(2,1)}), bf16[8,256,512]{2,1,0:T(8,128)(2,1)}, u32[]{:S(2)}, u32[]{:S(2)}) async-start(bf16[8,256,512]{2,1,0:T(8,128)(2,1)} %bitcast.56), calls=%async_computation.6 | async-start | bytes 4194304 | tf_op jit(solution)/shard_map/all_to_all | solution.py:303
  272.9 1.3 collective-permute-start.19
  274.2 1.7 collective-permute-start.16
  275.8 24.6 %collective-permute-done.19.refs_1_ = bf16[1024,512]{1,0:T(8,128)(2,1)S(1)} collective-permute-done((bf16[1024,512]{1,0:T(8,128)(2,1)}, bf16[1024,512]{1,0:T(8,128)(2,1)S(1)}, u32[]{:S(2)}, u32[]{:S(2)}) %collective-permute-start.19) | collective-permute-done | bytes 1048608 | tf_op jit(solution)/shard_map/ppermute | solution.py:300
  300.4 5.4 %terms.5 = bf16[2048,512]{1,0:T(8,128)(2,1)} custom-call(bf16[1024,2048]{1,0:T(8,128)(2,1)} %spread.7.weight_ref, bf16[1024,512]{1,0:T(8,128)(2,1)} %collective-permute-done.18.refs_0_, bf16[1024,512]{1,0:T(8,128)(2,1)S(1)} %collective-permute-done.19.refs_1_), custom_call_target="tpu_custom_call" | custom-call | flops 4000000000 | bytes 10000000 | tf_op jit(solution)/shard_map/terms/pallas_call | solution.py:199
  305.8 4.3 %all-to-all-start.7 = ((bf16[8,256,512]{2,1,0:T(8,128)(2,1)}), bf16[8,256,512]{2,1,0:T(8,128)(2,1)}, u32[]{:S(2)}, u32[]{:S(2)}) async-start(bf16[8,256,512]{2,1,0:T(8,128)(2,1)} %bitcast.70), calls=%async_computation.7 | async-start | bytes 4194304 | tf_op jit(solution)/shard_map/all_to_all | solution.py:303
  311.5 26.2 %collective-permute-done.17.refs_1_ = bf16[1024,512]{1,0:T(8,128)(2,1)S(1)} collective-permute-done((bf16[1024,512]{1,0:T(8,128)(2,1)}, bf16[1024,512]{1,0:T(8,128)(2,1)S(1)}, u32[]{:S(2)}, u32[]{:S(2)}) %collective-permute-start.17) | collective-permute-done | bytes 1048608 | tf_op jit(solution)/shard_map/ppermute | solution.py:300
  337.7 5.4 %terms.4 = bf16[2048,512]{1,0:T(8,128)(2,1)} custom-call(bf16[1024,2048]{1,0:T(8,128)(2,1)} %spread.6.weight_ref, bf16[1024,512]{1,0:T(8,128)(2,1)} %collective-permute-done.16.refs_0_, bf16[1024,512]{1,0:T(8,128)(2,1)S(1)} %collective-permute-done.17.refs_1_), custom_call_target="tpu_custom_call" | custom-call | flops 4000000000 | bytes 10000000 | tf_op jit(solution)/shard_map/terms/pallas_call | solution.py:199
  343.1 4.6 %all-to-all-start.8 = ((bf16[8,256,512]{2,1,0:T(8,128)(2,1)}), bf16[8,256,512]{2,1,0:T(8,128)(2,1)}, u32[]{:S(2)}, u32[]{:S(2)}) async-start(bf16[8,256,512]{2,1,0:T(8,128)(2,1)} %bitcast.71), calls=%async_computation.8 | async-start | bytes 4194304 | tf_op jit(solution)/shard_map/all_to_all | solution.py:303
  347.7 16.9 %add_rows.2.refs_2_ = f32[2048,512]{1,0:T(8,128)} custom-call(s32[8,256]{1,0:T(8,128)S(1)} %reshape.134.refs_0_, s32[8,256]{1,0:T(8,128)S(1)} %reshape.135.refs_1_, s32[8,256]{1,0:T(8,128)S(1)} %reshape.136.refs_2_, bf16[2048,512]{1,0:T(8,128)(2,1)S(1)} %bitcast.52, bf16[2048,512]{1,0:T(8,128)(2,1)} %bitcast.22.refs_4_, bf16[2048,512]{1,0:T(8,128)(2,1)} %bitcast.24.refs_5_), custom_call_target="tpu_custom_call" | custom-call | flops 15000000512 | bytes 10000000 | tf_op jit(solution)/shard_map/add_rows/pallas_call | solution.py:238
  364.6 9.8 %all-to-all-done.8 = bf16[8,256,512]{2,1,0:T(8,128)(2,1)} async-done(((bf16[8,256,512]{2,1,0:T(8,128)(2,1)}), bf16[8,256,512]{2,1,0:T(8,128)(2,1)}, u32[]{:S(2)}, u32[]{:S(2)}) %all-to-all-start.8) | async-done | bytes 2097184 | tf_op jit(solution)/shard_map/all_to_all | solution.py:303
  374.4 8.4 %add_rows.3 = f32[2048,512]{1,0:T(8,128)} custom-call(s32[8,256]{1,0:T(8,128)S(1)} %reshape.137.refs_0_, bf16[2048,512]{1,0:T(8,128)(2,1)} %bitcast.26.refs_1_, f32[2048,512]{1,0:T(8,128)} %add_rows.2.refs_2_), custom_call_target="tpu_custom_call" | custom-call | flops 5000000000 | bytes 10000000 | tf_op jit(solution)/shard_map/add_rows/pallas_call | solution.py:238
  (124 shorter events, 24.2 us)
Async XLA Ops:
  0.6 31.5 %copy-start = (bf16[768,512]{1,0:T(8,128)(2,1)S(1)}, bf16[768,512]{1,0:T(8,128)(2,1)}, u32[]{:S(2)}) copy-start(bf16[768,512]{1,0:T(8,128)(2,1)} %param.22) | copy-start | bytes 2359300
  0.6 2.2 copy-start.12
  0.7 0.8 copy-start.13
  2.8 6.5 %copy-start.14 = (bf16[1,32,32,768]{3,2,1,0:T(8,128)(2,1)S(1)}, bf16[1,32,32,768]{3,2,1,0:T(8,128)(2,1)}, u32[]{:S(2)}) copy-start(bf16[1,32,32,768]{3,2,1,0:T(8,128)(2,1)} %param.13) | copy-start | bytes 4718596
  3.5 91.6 %collective-permute-start.1 = (bf16[1088,128]{1,0:T(8,128)(2,1)S(1)}, bf16[1088,128]{1,0:T(8,128)(2,1)}, u32[]{:S(2)}, u32[]{:S(2)}) collective-permute-start(bf16[1088,128]{1,0:T(8,128)(2,1)S(1)} %pad_maximum_fusion), channel_id=1, source_target_pairs={{0,6},{1,7},{6,0},{7,1},{2,4},{3,5},{4,2},{5,3},{8,14},{9,15},{14,... | collective-permute-start | bytes 835592 | tf_op jit(solution)/shard_map/ppermute | solution.py:300
  8.6 86.8 %collective-permute-start.2 = (bf16[1088,128]{1,0:T(8,128)(2,1)S(1)}, bf16[1088,128]{1,0:T(8,128)(2,1)}, u32[]{:S(2)}, u32[]{:S(2)}) collective-permute-start(bf16[1088,128]{1,0:T(8,128)(2,1)S(1)} %pad_maximum_fusion), channel_id=1, source_target_pairs={{0,4},{1,5},{4,0},{5,1},{2,6},{3,7},{6,2},{7,3},{8,12},{9,13},{12,... | collective-permute-start | bytes 835592 | tf_op jit(solution)/shard_map/ppermute | solution.py:300
  8.7 158.3 %collective-permute-start = (bf16[1088,128]{1,0:T(8,128)(2,1)S(1)}, bf16[1088,128]{1,0:T(8,128)(2,1)}, u32[]{:S(2)}, u32[]{:S(2)}) collective-permute-start(bf16[1088,128]{1,0:T(8,128)(2,1)S(1)} %pad_maximum_fusion), channel_id=1, source_target_pairs={{0,2},{1,3},{2,0},{3,1},{4,6},{5,7},{6,4},{7,5},{8,10},{9,11},{10,... | collective-permute-start | bytes 835592 | tf_op jit(solution)/shard_map/ppermute | solution.py:300
  10.2 2.7 copy-start.20
  10.2 2.7 copy-start.21
  10.2 2.7 copy-start.22
  10.2 2.7 copy-start.23
  29.7 2.8 copy-start.16
  29.7 2.8 copy-start.24
  29.7 2.8 copy-start.25
  34.4 1.0 copy-start.15
  36.3 49.2 %collective-permute-start.8 = (bf16[1,128,512]{2,1,0:T(8,128)(2,1)S(1)}, bf16[1,128,512]{2,1,0:T(8,128)(2,1)S(1)}, u32[]{:S(2)}, u32[]{:S(2)}) collective-permute-start(bf16[1,128,512]{2,1,0:T(8,128)(2,1)S(1)} %get-tuple-element.46), channel_id=1, source_target_pairs={{0,7},{1,0},{2,1},{3,2},{4,3},{5,4},{6,5},{7,6},{8,15},{9,8},{10,9... | collective-permute-start | bytes 393224 | tf_op jit(solution)/shard_map/ppermute | solution.py:351
  38.6 55.4 %collective-permute-start.9 = (bf16[1,128,512]{2,1,0:T(8,128)(2,1)S(1)}, bf16[1,128,512]{2,1,0:T(8,128)(2,1)S(1)}, u32[]{:S(2)}, u32[]{:S(2)}) collective-permute-start(bf16[1,128,512]{2,1,0:T(8,128)(2,1)S(1)} %get-tuple-element.45), channel_id=1, source_target_pairs={{0,6},{1,7},{2,0},{3,1},{4,2},{5,3},{6,4},{7,5},{8,14},{9,15},{10,... | collective-permute-start | bytes 393224 | tf_op jit(solution)/shard_map/ppermute | solution.py:351
  40.6 10.1 %all-to-all-start = ((s32[32,1,256]{2,1,0:T(1,128)}), s32[32,1,256]{2,1,0:T(1,128)S(1)}, u32[]{:S(2)}, u32[]{:S(2)}) async-start(s32[32,1,256]{2,1,0:T(1,128)} %copy.33), calls=%async_computation | async-start | bytes 65536 | tf_op jit(solution)/shard_map/all_to_all | solution.py:312
  57.5 1.4 copy-start.5
  58.8 30.2 %all-to-all-start.1 = ((bf16[8,256,512]{2,1,0:T(8,128)(2,1)}), bf16[8,256,512]{2,1,0:T(8,128)(2,1)S(1)}, u32[]{:S(2)}, u32[]{:S(2)}) async-start(bf16[8,256,512]{2,1,0:T(8,128)(2,1)} %bitcast.55), calls=%async_computation.1 | async-start | bytes 4194304 | tf_op jit(solution)/shard_map/all_to_all | solution.py:303
  69.0 1.4 copy-start.4
  85.4 39.5 %collective-permute-start.10 = (bf16[1,128,512]{2,1,0:T(8,128)(2,1)}, bf16[1,128,512]{2,1,0:T(8,128)(2,1)S(1)}, u32[]{:S(2)}, u32[]{:S(2)}) collective-permute-start(bf16[1,128,512]{2,1,0:T(8,128)(2,1)} %get-tuple-element.44), channel_id=1, source_target_pairs={{0,5},{1,6},{2,7},{3,0},{4,1},{5,2},{6,3},{7,4},{8,13},{9,14},{10,... | collective-permute-start | bytes 393224 | tf_op jit(solution)/shard_map/ppermute | solution.py:351
  89.0 1.4 copy-start.2
  90.4 30.2 %all-to-all-start.2 = ((bf16[8,256,512]{2,1,0:T(8,128)(2,1)}), bf16[8,256,512]{2,1,0:T(8,128)(2,1)S(1)}, u32[]{:S(2)}, u32[]{:S(2)}) async-start(bf16[8,256,512]{2,1,0:T(8,128)(2,1)} %bitcast.54), calls=%async_computation.2 | async-start | bytes 4194304 | tf_op jit(solution)/shard_map/all_to_all | solution.py:303
  94.0 34.1 %collective-permute-start.11 = (bf16[1,128,512]{2,1,0:T(8,128)(2,1)}, bf16[1,128,512]{2,1,0:T(8,128)(2,1)}, u32[]{:S(2)}, u32[]{:S(2)}) collective-permute-start(bf16[1,128,512]{2,1,0:T(8,128)(2,1)} %get-tuple-element.43), channel_id=1, source_target_pairs={{0,4},{1,5},{2,6},{3,7},{4,0},{5,1},{6,2},{7,3},{8,12},{9,13},{10,... | collective-permute-start | bytes 393224 | tf_op jit(solution)/shard_map/ppermute | solution.py:351
  95.2 34.5 %collective-permute-start.12 = (bf16[1,128,512]{2,1,0:T(8,128)(2,1)}, bf16[1,128,512]{2,1,0:T(8,128)(2,1)}, u32[]{:S(2)}, u32[]{:S(2)}) collective-permute-start(bf16[1,128,512]{2,1,0:T(8,128)(2,1)} %get-tuple-element.42), channel_id=1, source_target_pairs={{0,3},{1,4},{2,5},{3,6},{4,7},{5,0},{6,1},{7,2},{8,11},{9,12},{10,... | collective-permute-start | bytes 393224 | tf_op jit(solution)/shard_map/ppermute | solution.py:351
  95.5 35.8 %collective-permute-start.13 = (bf16[1,128,512]{2,1,0:T(8,128)(2,1)}, bf16[1,128,512]{2,1,0:T(8,128)(2,1)}, u32[]{:S(2)}, u32[]{:S(2)}) collective-permute-start(bf16[1,128,512]{2,1,0:T(8,128)(2,1)} %get-tuple-element.41), channel_id=1, source_target_pairs={{0,2},{1,3},{2,4},{3,5},{4,6},{5,7},{6,0},{7,1},{8,10},{9,11},{10,... | collective-permute-start | bytes 393224 | tf_op jit(solution)/shard_map/ppermute | solution.py:351
  99.0 3.4 copy-start.3
  107.1 1.0 copy-start.8
  120.6 48.1 %all-to-all-start.3 = ((bf16[8,256,512]{2,1,0:T(8,128)(2,1)}), bf16[8,256,512]{2,1,0:T(8,128)(2,1)}, u32[]{:S(2)}, u32[]{:S(2)}) async-start(bf16[8,256,512]{2,1,0:T(8,128)(2,1)} %bitcast.11), calls=%async_computation.3 | async-start | bytes 4194304 | tf_op jit(solution)/shard_map/all_to_all | solution.py:303
  124.9 26.2 %collective-permute-start.3 = (bf16[1024,512]{1,0:T(8,128)(2,1)}, bf16[1024,512]{1,0:T(8,128)(2,1)S(1)}, u32[]{:S(2)}, u32[]{:S(2)}) collective-permute-start(bf16[1024,512]{1,0:T(8,128)(2,1)} %copy-done.8), channel_id=1, source_target_pairs={{0,2},{1,3},{6,4},{7,5},{8,10},{9,11},{14,12},{15,13},{16,18},{17,... | collective-permute-start | bytes 3145736 | tf_op jit(solution)/shard_map/ppermute | solution.py:300
  128.1 36.6 %collective-permute-start.14 = (bf16[1,128,512]{2,1,0:T(8,128)(2,1)}, bf16[1,128,512]{2,1,0:T(8,128)(2,1)S(1)}, u32[]{:S(2)}, u32[]{:S(2)}) collective-permute-start(bf16[1,128,512]{2,1,0:T(8,128)(2,1)} %get-tuple-element.40), channel_id=1, source_target_pairs={{0,1},{1,2},{2,3},{3,4},{4,5},{5,6},{6,7},{7,0},{8,9},{9,10},{10,1... | collective-permute-start | bytes 393224 | tf_op jit(solution)/shard_map/ppermute | solution.py:351
  132.9 18.3 %copy-start.9 = (bf16[1024,512]{1,0:T(8,128)(2,1)S(1)}, bf16[1024,512]{1,0:T(8,128)(2,1)}, u32[]{:S(2)}) copy-start(bf16[1024,512]{1,0:T(8,128)(2,1)} %copy-done.8) | copy-start | bytes 3145732
  152.4 36.1 %collective-permute-start.4 = (bf16[1024,512]{1,0:T(8,128)(2,1)}, bf16[1024,512]{1,0:T(8,128)(2,1)}, u32[]{:S(2)}, u32[]{:S(2)}) collective-permute-start(bf16[1024,512]{1,0:T(8,128)(2,1)} %add.168), channel_id=1, source_target_pairs={{2,4},{3,5},{4,2},{5,3},{10,12},{11,13},{12,10},{13,11},{18,20},{1... | collective-permute-start | bytes 3145736 | tf_op jit(solution)/shard_map/ppermute | solution.py:300
  159.5 26.6 %collective-permute-start.6 = (bf16[1024,512]{1,0:T(8,128)(2,1)}, bf16[1024,512]{1,0:T(8,128)(2,1)S(1)}, u32[]{:S(2)}, u32[]{:S(2)}) collective-permute-start(bf16[1024,512]{1,0:T(8,128)(2,1)} %blend.6), channel_id=1, source_target_pairs={{0,2},{1,3},{6,4},{7,5},{8,10},{9,11},{14,12},{15,13},{16,18},{17,... | collective-permute-start | bytes 3145736 | tf_op jit(solution)/shard_map/ppermute | solution.py:300
  164.7 2.3 copy-start.18
  168.6 51.6 %all-to-all-start.4 = ((bf16[8,256,512]{2,1,0:T(8,128)(2,1)}), bf16[8,256,512]{2,1,0:T(8,128)(2,1)}, u32[]{:S(2)}, u32[]{:S(2)}) async-start(bf16[8,256,512]{2,1,0:T(8,128)(2,1)} %bitcast.13), calls=%async_computation.4 | async-start | bytes 4194304 | tf_op jit(solution)/shard_map/all_to_all | solution.py:303
  187.7 11.6 %copy-start.17 = (bf16[16,128,512]{2,1,0:T(8,128)(2,1)S(1)}, bf16[16,128,512]{2,1,0:T(8,128)(2,1)}, u32[]{:S(2)}) copy-start(bf16[16,128,512]{2,1,0:T(8,128)(2,1)} %dynamic-slice_dynamic-update-slice_fusion) | copy-start | bytes 6291460
  187.7 14.4 %copy-start.19 = (bf16[1,128,512]{2,1,0:T(8,128)(2,1)S(1)}, bf16[1,128,512]{2,1,0:T(8,128)(2,1)}, u32[]{:S(2)}) copy-start(bf16[1,128,512]{2,1,0:T(8,128)(2,1)} %copy-done.18) | copy-start | bytes 393220
  187.7 16.4 %collective-permute-start.7 = (bf16[1024,512]{1,0:T(8,128)(2,1)S(1)}, bf16[1024,512]{1,0:T(8,128)(2,1)S(1)}, u32[]{:S(2)}, u32[]{:S(2)}) collective-permute-start(bf16[1024,512]{1,0:T(8,128)(2,1)S(1)} %add.169), channel_id=1, source_target_pairs={{2,4},{3,5},{4,2},{5,3},{10,12},{11,13},{12,10},{13,11},{18,20},{1... | collective-permute-start | bytes 3145736 | tf_op jit(solution)/shard_map/ppermute | solution.py:300
  194.1 26.1 %collective-permute-start.5 = (bf16[1024,512]{1,0:T(8,128)(2,1)S(1)}, bf16[1024,512]{1,0:T(8,128)(2,1)S(1)}, u32[]{:S(2)}, u32[]{:S(2)}) collective-permute-start(bf16[1024,512]{1,0:T(8,128)(2,1)S(1)} %blend.5), channel_id=1, source_target_pairs={{0,2},{1,3},{2,0},{3,1},{4,6},{5,7},{6,4},{7,5},{8,10},{9,11},{10,... | collective-permute-start | bytes 3145736 | tf_op jit(solution)/shard_map/ppermute | solution.py:300
  226.7 4.6 %copy-start.11 = (bf16[1024,512]{1,0:T(8,128)(2,1)}, bf16[1024,512]{1,0:T(8,128)(2,1)S(1)}, u32[]{:S(2)}) copy-start(bf16[1024,512]{1,0:T(8,128)(2,1)S(1)} %get-tuple-element.33.refs_0_) | copy-start | bytes 3145732
  231.3 1.3 copy-start.7
  232.6 35.9 %all-to-all-start.5 = ((bf16[8,256,512]{2,1,0:T(8,128)(2,1)}), bf16[8,256,512]{2,1,0:T(8,128)(2,1)S(1)}, u32[]{:S(2)}, u32[]{:S(2)}) async-start(bf16[8,256,512]{2,1,0:T(8,128)(2,1)} %bitcast.57), calls=%async_computation.5 | async-start | bytes 4194304 | tf_op jit(solution)/shard_map/all_to_all | solution.py:303
  236.2 25.7 %collective-permute-start.15 = (bf16[1024,512]{1,0:T(8,128)(2,1)}, bf16[1024,512]{1,0:T(8,128)(2,1)S(1)}, u32[]{:S(2)}, u32[]{:S(2)}) collective-permute-start(bf16[1024,512]{1,0:T(8,128)(2,1)} %copy-done.11), channel_id=1, source_target_pairs={{0,2},{1,3},{2,0},{3,1},{4,6},{5,7},{6,4},{7,5},{8,10},{9,11},{10,... | collective-permute-start | bytes 3145736 | tf_op jit(solution)/shard_map/ppermute | solution.py:300
  238.0 34.9 %collective-permute-start.18 = (bf16[1024,512]{1,0:T(8,128)(2,1)}, bf16[1024,512]{1,0:T(8,128)(2,1)}, u32[]{:S(2)}, u32[]{:S(2)}) collective-permute-start(bf16[1024,512]{1,0:T(8,128)(2,1)} %copy-done.11), channel_id=1, source_target_pairs={{2,4},{3,5},{4,2},{5,3},{10,12},{11,13},{12,10},{13,11},{18,20},{1... | collective-permute-start | bytes 3145736 | tf_op jit(solution)/shard_map/ppermute | solution.py:300
  266.1 1.4 copy-start.6
  267.5 1.0 copy-start.10
  268.5 37.3 %all-to-all-start.6 = ((bf16[8,256,512]{2,1,0:T(8,128)(2,1)}), bf16[8,256,512]{2,1,0:T(8,128)(2,1)}, u32[]{:S(2)}, u32[]{:S(2)}) async-start(bf16[8,256,512]{2,1,0:T(8,128)(2,1)} %bitcast.56), calls=%async_computation.6 | async-start | bytes 4194304 | tf_op jit(solution)/shard_map/all_to_all | solution.py:303
  272.9 27.5 %collective-permute-start.19 = (bf16[1024,512]{1,0:T(8,128)(2,1)}, bf16[1024,512]{1,0:T(8,128)(2,1)S(1)}, u32[]{:S(2)}, u32[]{:S(2)}) collective-permute-start(bf16[1024,512]{1,0:T(8,128)(2,1)} %collective-permute-done.18.refs_0_), channel_id=1, source_target_pairs={{2,0},{3,1},{4,6},{5,7},{10,8},{11,9},{12,14},{13,15},{18,16},{19,... | collective-permute-start | bytes 3145736 | tf_op jit(solution)/shard_map/ppermute | solution.py:300
  274.2 36.0 %collective-permute-start.16 = (bf16[1024,512]{1,0:T(8,128)(2,1)}, bf16[1024,512]{1,0:T(8,128)(2,1)}, u32[]{:S(2)}, u32[]{:S(2)}) collective-permute-start(bf16[1024,512]{1,0:T(8,128)(2,1)} %copy-done.10), channel_id=1, source_target_pairs={{2,4},{3,5},{4,2},{5,3},{10,12},{11,13},{12,10},{13,11},{18,20},{1... | collective-permute-start | bytes 3145736 | tf_op jit(solution)/shard_map/ppermute | solution.py:300
  305.8 37.3 %all-to-all-start.7 = ((bf16[8,256,512]{2,1,0:T(8,128)(2,1)}), bf16[8,256,512]{2,1,0:T(8,128)(2,1)}, u32[]{:S(2)}, u32[]{:S(2)}) async-start(bf16[8,256,512]{2,1,0:T(8,128)(2,1)} %bitcast.70), calls=%async_computation.7 | async-start | bytes 4194304 | tf_op jit(solution)/shard_map/all_to_all | solution.py:303
  310.2 27.5 %collective-permute-start.17 = (bf16[1024,512]{1,0:T(8,128)(2,1)}, bf16[1024,512]{1,0:T(8,128)(2,1)S(1)}, u32[]{:S(2)}, u32[]{:S(2)}) collective-permute-start(bf16[1024,512]{1,0:T(8,128)(2,1)} %collective-permute-done.16.refs_0_), channel_id=1, source_target_pairs={{2,0},{3,1},{4,6},{5,7},{10,8},{11,9},{12,14},{13,15},{18,16},{19,... | collective-permute-start | bytes 3145736 | tf_op jit(solution)/shard_map/ppermute | solution.py:300
  343.1 31.3 %all-to-all-start.8 = ((bf16[8,256,512]{2,1,0:T(8,128)(2,1)}), bf16[8,256,512]{2,1,0:T(8,128)(2,1)}, u32[]{:S(2)}, u32[]{:S(2)}) async-start(bf16[8,256,512]{2,1,0:T(8,128)(2,1)} %bitcast.71), calls=%async_computation.8 | async-start | bytes 4194304 | tf_op jit(solution)/shard_map/all_to_all | solution.py:303
  374.4 8.4 %copy-start.1 = (bf16[768,512]{1,0:T(8,128)(2,1)S(1)}, bf16[768,512]{1,0:T(8,128)(2,1)}, u32[]{:S(2)}) copy-start(bf16[768,512]{1,0:T(8,128)(2,1)} %param.22) | copy-start | bytes 2359300

commit v4 on v3

--- a/solution.py
+++ b/solution.py
@@ -157,32 +157,52 @@
     color = jnp.dot(weight_ref[...], rows_ref[...], preferred_element_type=F32)
     for part_ref in rest[:n_parts]:
         color = color + part_ref[...].astype(F32)
-    if len(rest) == n_parts + 1:
-        rest[n_parts][...] = color.astype(BF16)
-    else:
-        target_ref, color_ref, diff_ref = rest[n_parts:]
-        color_ref[...] = color.astype(BF16)
-        diff_ref[...] = (color - target_ref[...].astype(F32)).astype(BF16)
-
-
-def blend(weight, rows, parts=(), target=None):
+    rest[n_parts][...] = color.astype(BF16)
+
+
+def last_blend_kernel(n_parts, first_ref, weight_ref, rows_ref, *rest):
+    parts, strips = rest[:n_parts], rest[n_parts:-2]
+    color_ref, diff_ref = rest[-2:]
+    color = jnp.dot(weight_ref[...], rows_ref[...], preferred_element_type=F32)
+    for part_ref in parts:
+        color = color + part_ref[...].astype(F32)
+    color_ref[...] = color.astype(BF16)
+    cells = strips[0].shape[0]
+    per_step = color.shape[0] // cells
+    for k in range(per_step):
+        at = lax.rem(first_ref[0] + pl.program_id(0) * per_step + k, len(strips))
+        here = slice(k * cells, (k + 1) * cells)
+        for n in range(len(strips)):
+
+            @pl.when(at == n)
+            def _(n=n):
+                diff_ref[here, :] = (color[here] - strips[n][...].astype(F32)).astype(BF16)
+
+
+def blend(weight, rows, parts=(), first=None, strips=()):
     cells, slots = weight.shape
     feat = rows.shape[1]
     block = min(cells, 256)
     cell_block = pl.BlockSpec((block, feat), lambda i: (i, 0))
     out = jax.ShapeDtypeStruct((cells, feat), BF16)
-    more = tuple(parts) + (() if target is None else (target,))
-    return pl.pallas_call(
-        functools.partial(blend_kernel, len(parts)),
+    last = first is not None
+    in_specs = [pl.BlockSpec((block, slots), lambda i: (i, 0)), pl.BlockSpec((slots, feat), lambda i: (0, 0))]
+    in_specs += [cell_block] * len(parts)
+    args = [weight, rows, *parts]
+    if last:
+        in_specs = [pl.BlockSpec(memory_space=pltpu.SMEM)] + in_specs
+        in_specs += [pl.BlockSpec(strip.shape, lambda i: (0, 0)) for strip in strips]
+        args = [first, *args, *strips]
+    return pl.pallas_call(
+        functools.partial(last_blend_kernel if last else blend_kernel, len(parts)),
         grid=(cells // block,),
-        in_specs=[pl.BlockSpec((block, slots), lambda i: (i, 0)), pl.BlockSpec((slots, feat), lambda i: (0, 0))]
-        + [cell_block] * len(more),
-        out_specs=cell_block if target is None else (cell_block, cell_block),
-        out_shape=out if target is None else (out, out),
+        in_specs=in_specs,
+        out_specs=(cell_block, cell_block) if last else cell_block,
+        out_shape=(out, out) if last else out,
         compiler_params=params(),
         cost_estimate=pl.CostEstimate(flops=4 * 10**9, bytes_accessed=10**7, transcendentals=0),
         name="blend",
-    )(weight, rows, *more)
+    )(*args)
 
 
 def terms_kernel(weight_ref, *refs):
@@ -303,38 +323,35 @@
         return lax.all_to_all(x, both, split_axis=0, concat_axis=0, axis_index_groups=groups, tiled=True)
 
     request, own, rank = index(tile_lists.reshape(tiles, list_len), peers, cap, held)
-    weight = weights(alphas.reshape(tiles * cells, list_len))
-    packed = jnp.concatenate([weight, own, rank], 0)
-    request, packed = lax.optimization_barrier((request, packed))
-    from_beside = move(packed, beside)
-    from_two = move(packed, moves((0, 2), (2, 0), (1, 3), (3, 1)))
-    from_three = move(packed, moves((0, 3), (3, 0), (1, 2), (2, 1)))
     asked = lax.all_to_all(request, both, split_axis=0, concat_axis=0, tiled=True)
     asked = asked.reshape(n_img, 4, wide_layer, cap)
     sets = (jnp.where(low, 3, 0), jnp.where(low, 2, 1), layer ^ 1, layer)
     lists = [lax.dynamic_index_in_dim(asked, s, 1, keepdims=False).reshape(near, cap) for s in sets]
+    owners = (
+        jnp.arange(n_img, dtype=I32)[:, None] * n_tile
+        + layer * wide_layer
+        + jnp.arange(wide_layer, dtype=I32)[None, :]
+    ).reshape(near)
+
+    def spread_of(pack):
+        n_cells = tiles * cells
+        return spread(owners, pack[n_cells : n_cells + tiles], pack[n_cells + tiles :], pack[:n_cells], cap)
+
+    looked = gather(lists[0], gauss_rows)
+    looked, patches, alphas = lax.optimization_barrier((looked, patches, alphas))
+    rows = [exchange(looked)]
+    weight = weights(alphas.reshape(tiles * cells, list_len))
+    packed = jnp.concatenate([weight, own, rank], 0)
+    from_beside = move(packed, beside)
+    from_two = move(packed, moves((0, 2), (2, 0), (1, 3), (3, 1)))
+    from_three = move(packed, moves((0, 3), (3, 0), (1, 2), (2, 1)))
     packs = (
         jnp.where(outer, from_three, from_two),
         jnp.where(outer, from_two, from_three),
         from_beside,
         packed,
     )
-    owners = (
-        jnp.arange(n_img, dtype=I32)[:, None] * n_tile
-        + layer * wide_layer
-        + jnp.arange(wide_layer, dtype=I32)[None, :]
-    ).reshape(near)
-
-    def spread_of(pack):
-        n_cells = tiles * cells
-        return spread(owners, pack[n_cells : n_cells + tiles], pack[n_cells + tiles :], pack[:n_cells], cap)
-
-    rows = []
-    for n in range(4):
-        looked = gather(lists[n], gauss_rows)
-        if n:
-            looked, rows[-1] = lax.optimization_barrier((looked, rows[-1]))
-        rows.append(exchange(looked))
+    spreads = [spread_of(pack) for pack in packs]
 
     wide = patches.reshape(-1, width).astype(F32)
     normed = layer_norm(wide, norm_gain, norm_bias).astype(BF16)
@@ -344,22 +361,28 @@
     final = layer_norm(block_out, final_gain, final_bias).astype(BF16)
     embed = jnp.dot(final, head_weight, preferred_element_type=F32)
     scale = lax.rsqrt(jnp.mean(embed * embed, axis=-1, keepdims=True) + 1e-06)
-    strips = (embed * scale).astype(BF16).reshape(n_tile, -1, feat)
-    arrived = []
+    target = (embed * scale).astype(BF16).reshape(n_tile, -1, feat)
+
+    looked, rows[0] = lax.optimization_barrier((gather(lists[1], gauss_rows), rows[0]))
+    rows.append(exchange(looked))
+    part = blend(spreads[0], rows[0])
+    moved = move(part, inwards)
+    looked, rows[1], part, moved = lax.optimization_barrier((gather(lists[2], gauss_rows), rows[1], part, moved))
+    rows.append(exchange(looked))
+    far = move(part + moved, middle)
+    part = blend(spreads[1], rows[1])
+    moved = move(part, inwards)
+    looked, rows[2], far = lax.optimization_barrier((gather(lists[3], gauss_rows), rows[2], far))
+    rows.append(exchange(looked))
+    middle_part = move(part + moved, middle)
+    beside_part = move(blend(spreads[2], rows[2], (far,)), beside)
+
+    strips = []
     for n in reversed(range(n_tile)):
-        strip = lax.dynamic_index_in_dim(strips, lax.rem(tile + n, n_tile), 0, keepdims=True)
-        arrived.append(lax.ppermute(strip, "tile", [(a, (a + n) % n_tile) for a in range(n_tile)]) if n else strip)
-    first = lax.rem(2 * n_tile - 1 - tile, n_tile)
-    target = lax.dynamic_slice_in_dim(jnp.concatenate(arrived + arrived, 0), first, n_tile, 0)
-    target = target.reshape(tiles * cells, feat)
-
-    spreads = [spread_of(pack) for pack in packs]
-    part = blend(spreads[0], rows[0])
-    far = move(part + move(part, inwards), middle)
-    part = blend(spreads[1], rows[1])
-    middle_part = move(part + move(part, inwards), middle)
-    beside_part = move(blend(spreads[2], rows[2], (far,)), beside)
-    color, diff = blend(spreads[3], rows[3], (beside_part, middle_part), target)
+        strip = lax.dynamic_index_in_dim(target, lax.rem(tile + n, n_tile), 0, keepdims=False)
+        strips.append(lax.ppermute(strip, "tile", [(a, (a + n) % n_tile) for a in range(n_tile)]) if n else strip)
+    first = lax.rem(2 * n_tile - 1 - tile, n_tile).astype(I32).reshape(1)
+    color, diff = blend(spreads[3], rows[3], (beside_part, middle_part), first, strips)
 
     diff_beside = move(diff, beside)
     diff_middle = move(diff, middle)

time: 388 us -> 386 us (level)
  local copies, waits for them, and re-layouts: 31.5 us -> 10.7 us
  waiting for transfers between devices: 142 us -> 152 us
  Pallas kernels: 110 us -> 115 us
    ppermute x7, waiting for transfers between devices: 0.02 us -> 34.6 us  [on_device(): lax.ppermute(strip, 'tile', [(a, (a + n) % n_tile) for a in range(n_tile)])]
    unnamed x68 -> x43, local copies, waits for them, and re-layouts: 22.8 us -> 5.42 us
    ppermute x13, waiting for transfers between devices: 113 us -> 98.3 us  [move(): return lax.ppermute(x, 'tile', pairs)]
    all_to_all x8, waiting for transfers between devices: 24.7 us -> 12.2 us  [exchange(): lax.all_to_all(x, both, split_axis=0, concat_axis=0, axis_index_groups=gr...]
    all_to_all x1, starting transfers between devices: 2.87 us -> 7.3 us  [on_device(): lax.all_to_all(request, both, split_axis=0, concat_axis=0, tiled=True)]
    ppermute x7, starting transfers between devices: 7.5 us -> 3.47 us  [on_device(): lax.ppermute(strip, 'tile', [(a, (a + n) % n_tile) for a in range(n_tile)])]
  transfers between devices with their start and end apart: 29 -> 29, of which waited for: 10 -> 12; matrix products, arithmetic and copies ran while one was open for 12% -> 8% of each run, Pallas kernels for 23% -> 23%
where the time goes in v4:
time: 386 us; the launch traced here: 379 us
  waiting for transfers between devices  152 us (39%)
  Pallas kernels  115 us (30%)
  starting transfers between devices  70.9 us (18%)
  matrix products  20.4 us (5%)
  local copies, waits for them, and re-layouts  10.7 us (3%)
  other arithmetic  8.43 us (2%)
    ppermute x13, waiting for transfers between devices, move(): return lax.ppermute(x, 'tile', pairs)  98.3 us
    ppermute x7, waiting for transfers between devices, on_device(): lax.ppermute(strip, 'tile', [(a, (a + n) % n_tile) for a in range(n_tile)])  34.6 us
    all_to_all x8, starting transfers between devices, exchange(): lax.all_to_all(x, both, split_axis=0, concat_axis=0, axis_index_groups=gr...  33.4 us
    pallas_call x4, Pallas kernels, gather(): pl.pallas_call(functools.partial(gather_kernel, group, cap), grid=(near /...  30.3 us
    ppermute x13, starting transfers between devices, move(): return lax.ppermute(x, 'tile', pairs)  26.8 us
    pallas_call x2, Pallas kernels, add_rows(): pl.pallas_call(functools.partial(add_rows_kernel, count), grid=(held // b...  25.3 us
    pallas_call x4, Pallas kernels, blend(): pl.pallas_call(functools.partial(last_blend_kernel if last else blend_ker...  23.9 us
    pallas_call x4, Pallas kernels, terms(): pl.pallas_call(terms_kernel, grid=(slots // block,), in_specs=[pl.BlockSp...  19.6 us
  transfers between devices with their start and end apart: 29, of which 12 were waited for; matrix products, arithmetic and copies ran while one was open for 8% of the time, Pallas kernels for 23%

profile of v4, /device:TPU:0, one launch (start us, length us, event | category | flops | bytes accessed | tf_op | source)
XLA Modules:
  0.0 379.2 jit_solution(10907193493710815311)
XLA Ops:
  0.7 0.8 copy-done.9
  1.4 1.3 index.1
  3.4 7.3 %all-to-all-start = ((s32[32,1,256]{2,1,0:T(1,128)}), s32[32,1,256]{2,1,0:T(1,128)S(1)}, u32[]{:S(2)}, u32[]{:S(2)}) async-start(s32[32,1,256]{2,1,0:T(1,128)} %copy.33), calls=%async_computation | async-start | bytes 65536 | tf_op jit(solution)/shard_map/all_to_all | solution.py:326
  10.9 7.1 %all-to-all-done = s32[32,1,256]{2,1,0:T(1,128)S(1)} async-done(((s32[32,1,256]{2,1,0:T(1,128)}), s32[32,1,256]{2,1,0:T(1,128)S(1)}, u32[]{:S(2)}, u32[]{:S(2)}) %all-to-all-start) | async-done | bytes 32800 | tf_op jit(solution)/shard_map/all_to_all | solution.py:326
  18.3 7.5 %gather.4 = bf16[2048,512]{1,0:T(8,128)(2,1)} custom-call(s32[256,8]{1,0:T(8,128)S(1)} %copy.35.asked_ref, bf16[2048,512]{1,0:T(8,128)(2,1)} %rows_ref.7), custom_call_target="tpu_custom_call" | custom-call | flops 10000000000 | bytes 10000000 | tf_op jit(solution)/shard_map/gather/pallas_call | solution.py:144
  28.8 1.4 collective-permute-start.1
  30.2 2.4 collective-permute-start.4
  32.6 2.1 copy.42
  34.8 3.6 all-to-all-start.1
  38.6 7.6 %gather.7 = bf16[2048,512]{1,0:T(8,128)(2,1)} custom-call(s32[256,8]{1,0:T(8,128)S(1)} %copy.41.asked_ref, bf16[2048,512]{1,0:T(8,128)(2,1)} %rows_ref.7), custom_call_target="tpu_custom_call" | custom-call | flops 10000000000 | bytes 10000000 | tf_op jit(solution)/shard_map/gather/pallas_call | solution.py:144
  46.5 17.2 %fusion.16 = (f32[1024]{0:T(1024)S(1)}, f32[1024,768]{0,1:T(8,128)}) fusion(f32[768]{0:T(1024)S(1)} %copy-done.16, f32[1024,768]{0,1:T(8,128)} %copy.42, bf16[3072,768]{1,0:T(8,128)(2,1)} %param.18, f32[3072]{0:T(1024)S(1)} %copy-done.15, bf16[768,3072]{1,0:T(8,128)(2,1)} %param.16, f32[768]{0:T(1024)S(1)} %copy-done.17, f32[768]{0:T(1024)S(1)} %copy-done.18, ...), kind=kOutput, calls=%fused_computation.47 | convolution fusion | flops 9692773376 | bytes 17335296 | tf_op jit(solution)/shard_map/dot_general | solution.py:360
  63.7 7.7 %gather.6 = bf16[2048,512]{1,0:T(8,128)(2,1)} custom-call(s32[256,8]{1,0:T(8,128)S(1)} %copy.39.asked_ref, bf16[2048,512]{1,0:T(8,128)(2,1)} %rows_ref.7), custom_call_target="tpu_custom_call" | custom-call | flops 10000000000 | bytes 10000000 | tf_op jit(solution)/shard_map/gather/pallas_call | solution.py:144
  71.8 1.1 broadcast_select_fusion
  73.6 4.3 %all-to-all-start.2 = ((bf16[8,256,512]{2,1,0:T(8,128)(2,1)}), bf16[8,256,512]{2,1,0:T(8,128)(2,1)}, u32[]{:S(2)}, u32[]{:S(2)}) async-start(bf16[8,256,512]{2,1,0:T(8,128)(2,1)} %bitcast.10), calls=%async_computation.2 | async-start | bytes 4194304 | tf_op jit(solution)/shard_map/all_to_all | solution.py:323
  78.0 3.4 spread.5.weight_ref
  81.4 5.5 %blend.4 = bf16[1024,512]{1,0:T(8,128)(2,1)} custom-call(bf16[1024,2048]{1,0:T(8,128)(2,1)} %spread.5.weight_ref, bf16[2048,512]{1,0:T(8,128)(2,1)S(1)} %bitcast.68), custom_call_target="tpu_custom_call" | custom-call | flops 4000000000 | bytes 10000000 | tf_op jit(solution)/shard_map/blend/pallas_call | solution.py:196
  86.9 2.0 collective-permute-start.2
  89.0 7.4 %gather.5 = bf16[2048,512]{1,0:T(8,128)(2,1)} custom-call(s32[256,8]{1,0:T(8,128)S(1)} %copy.37.asked_ref, bf16[2048,512]{1,0:T(8,128)(2,1)} %rows_ref.7), custom_call_target="tpu_custom_call" | custom-call | flops 10000000000 | bytes 10000000 | tf_op jit(solution)/shard_map/gather/pallas_call | solution.py:144
  96.4 15.6 %collective-permute-done.2 = bf16[1024,512]{1,0:T(8,128)(2,1)S(1)} collective-permute-done((bf16[1024,512]{1,0:T(8,128)(2,1)}, bf16[1024,512]{1,0:T(8,128)(2,1)S(1)}, u32[]{:S(2)}, u32[]{:S(2)}) %collective-permute-start.2) | collective-permute-done | bytes 1048608 | tf_op jit(solution)/shard_map/ppermute | solution.py:320
  112.0 4.4 %all-to-all-start.3 = ((bf16[8,256,512]{2,1,0:T(8,128)(2,1)}), bf16[8,256,512]{2,1,0:T(8,128)(2,1)}, u32[]{:S(2)}, u32[]{:S(2)}) async-start(bf16[8,256,512]{2,1,0:T(8,128)(2,1)} %bitcast.12), calls=%async_computation.3 | async-start | bytes 4194304 | tf_op jit(solution)/shard_map/all_to_all | solution.py:323
  116.4 3.2 multiply_reduce_fusion.2
  119.7 1.5 add.165
  121.9 3.4 spread.7.weight_ref
  125.4 5.4 %blend.6 = bf16[1024,512]{1,0:T(8,128)(2,1)S(1)} custom-call(bf16[1024,2048]{1,0:T(8,128)(2,1)} %spread.7.weight_ref, bf16[2048,512]{1,0:T(8,128)(2,1)} %bitcast.11.rows_ref), custom_call_target="tpu_custom_call" | custom-call | flops 4000000000 | bytes 10000000 | tf_op jit(solution)/shard_map/blend/pallas_call | solution.py:196
  130.8 7.0 %collective-permute-start.6 = (bf16[1024,512]{1,0:T(8,128)(2,1)S(1)}, bf16[1024,512]{1,0:T(8,128)(2,1)}, u32[]{:S(2)}, u32[]{:S(2)}) collective-permute-start(bf16[1024,512]{1,0:T(8,128)(2,1)S(1)} %blend.6), channel_id=1, source_target_pairs={{0,2},{1,3},{6,4},{7,5},{8,10},{9,11},{14,12},{15,13},{16,18},{17,... | collective-permute-start | bytes 3145736 | tf_op jit(solution)/shard_map/ppermute | solution.py:320
  137.8 1.2 multiply_convert_fusion.2
  138.9 1.0 slice.41.weight_ref
  140.6 2.4 all-to-all-done.3
  143.0 4.3 %all-to-all-start.4 = ((bf16[8,256,512]{2,1,0:T(8,128)(2,1)}), bf16[8,256,512]{2,1,0:T(8,128)(2,1)}, u32[]{:S(2)}, u32[]{:S(2)}) async-start(bf16[8,256,512]{2,1,0:T(8,128)(2,1)} %bitcast.14), calls=%async_computation.4 | async-start | bytes 4194304 | tf_op jit(solution)/shard_map/all_to_all | solution.py:323
  147.4 3.4 spread.6.weight_ref
  150.8 8.6 %collective-permute-done.6 = bf16[1024,512]{1,0:T(8,128)(2,1)} collective-permute-done((bf16[1024,512]{1,0:T(8,128)(2,1)S(1)}, bf16[1024,512]{1,0:T(8,128)(2,1)}, u32[]{:S(2)}, u32[]{:S(2)}) %collective-permute-start.6) | collective-permute-done | bytes 1048608 | tf_op jit(solution)/shard_map/ppermute | solution.py:320
  159.4 2.5 add.166
  161.9 1.8 collective-permute-start.7
  163.7 6.2 %blend.5 = bf16[1024,512]{1,0:T(8,128)(2,1)} custom-call(bf16[1024,2048]{1,0:T(8,128)(2,1)} %spread.6.weight_ref, bf16[2048,512]{1,0:T(8,128)(2,1)} %bitcast.13.rows_ref, bf16[1024,512]{1,0:T(8,128)(2,1)S(1)} %collective-permute-done.3.rest_0_), custom_call_target="tpu_custom_call" | custom-call | flops 4000000000 | bytes 10000000 | tf_op jit(solution)/shard_map/blend/pallas_call | solution.py:196
  169.9 4.3 %collective-permute-start.5 = (bf16[1024,512]{1,0:T(8,128)(2,1)}, bf16[1024,512]{1,0:T(8,128)(2,1)S(1)}, u32[]{:S(2)}, u32[]{:S(2)}) collective-permute-start(bf16[1024,512]{1,0:T(8,128)(2,1)} %blend.5), channel_id=1, source_target_pairs={{0,2},{1,3},{2,0},{3,1},{4,6},{5,7},{6,4},{7,5},{8,10},{9,11},{10,... | collective-permute-start | bytes 3145736 | tf_op jit(solution)/shard_map/ppermute | solution.py:320
  174.4 1.2 collective-permute-start.11
  176.1 27.2 %collective-permute-done.10.rest_4_ = bf16[128,512]{1,0:T(8,128)(2,1)S(1)} collective-permute-done((bf16[128,512]{1,0:T(8,128)(2,1)S(1)}, bf16[128,512]{1,0:T(8,128)(2,1)S(1)}, u32[]{:S(2)}, u32[]{:S(2)}) %collective-permute-start.10) | collective-permute-done | bytes 131104 | tf_op jit(solution)/shard_map/ppermute | solution.py:383
  203.3 1.9 collective-permute-done.12.rest_6_
  205.2 1.7 collective-permute-start.8
  206.9 4.1 %collective-permute-done.13.rest_7_ = bf16[128,512]{1,0:T(8,128)(2,1)S(1)} collective-permute-done((bf16[128,512]{1,0:T(8,128)(2,1)S(1)}, bf16[128,512]{1,0:T(8,128)(2,1)S(1)}, u32[]{:S(2)}, u32[]{:S(2)}) %collective-permute-start.13) | collective-permute-done | bytes 131104 | tf_op jit(solution)/shard_map/ppermute | solution.py:383
  211.0 3.6 spread.4.weight_ref
  214.6 1.4 collective-permute-done.9.rest_3_
  216.0 6.8 %blend.7 = (bf16[1024,512]{1,0:T(8,128)(2,1)}, bf16[1024,512]{1,0:T(8,128)(2,1)S(1)}) custom-call(s32[1]{0:T(128)} %bitcast.first_ref, bf16[1024,2048]{1,0:T(8,128)(2,1)} %spread.4.weight_ref, bf16[2048,512]{1,0:T(8,128)(2,1)} %bitcast.15.rows_ref, bf16[1024,512]{1,0:T(8,128)(2,1)S(1)} %collective-permute-done.5.rest_0_, ...), custom_call_target="tpu_custom_call" | custom-call | flops 4000000000 | bytes 10000000 | tf_op jit(solution)/shard_map/blend/pallas_call | solution.py:196
  222.8 4.6 %terms.7 = bf16[2048,512]{1,0:T(8,128)(2,1)S(1)} custom-call(bf16[1024,2048]{1,0:T(8,128)(2,1)} %spread.4.weight_ref, bf16[1024,512]{1,0:T(8,128)(2,1)S(1)} %get-tuple-element.41.refs_0_), custom_call_target="tpu_custom_call" | custom-call | flops 4000000000 | bytes 10000000 | tf_op jit(solution)/shard_map/terms/pallas_call | solution.py:219
  227.4 1.3 copy-done.3
  228.7 3.6 all-to-all-start.5
  233.1 1.6 collective-permute-start.18
  234.7 23.3 %collective-permute-done.15.refs_0_ = bf16[1024,512]{1,0:T(8,128)(2,1)S(1)} collective-permute-done((bf16[1024,512]{1,0:T(8,128)(2,1)}, bf16[1024,512]{1,0:T(8,128)(2,1)S(1)}, u32[]{:S(2)}, u32[]{:S(2)}) %collective-permute-start.15) | collective-permute-done | bytes 1048608 | tf_op jit(solution)/shard_map/ppermute | solution.py:320
  258.0 4.2 %terms.6 = bf16[2048,512]{1,0:T(8,128)(2,1)S(1)} custom-call(bf16[1024,2048]{1,0:T(8,128)(2,1)} %spread.6.weight_ref, bf16[1024,512]{1,0:T(8,128)(2,1)S(1)} %collective-permute-done.15.refs_0_), custom_call_target="tpu_custom_call" | custom-call | flops 4000000000 | bytes 10000000 | tf_op jit(solution)/shard_map/terms/pallas_call | solution.py:219
  262.2 1.4 copy-done.2
  263.7 1.0 copy-done.6
  264.7 4.4 %all-to-all-start.6 = ((bf16[8,256,512]{2,1,0:T(8,128)(2,1)}), bf16[8,256,512]{2,1,0:T(8,128)(2,1)}, u32[]{:S(2)}, u32[]{:S(2)}) async-start(bf16[8,256,512]{2,1,0:T(8,128)(2,1)} %bitcast.69), calls=%async_computation.6 | async-start | bytes 4194304 | tf_op jit(solution)/shard_map/all_to_all | solution.py:323
  269.1 1.3 collective-permute-start.19
  270.4 1.7 collective-permute-start.16
  272.0 24.6 %collective-permute-done.19.refs_1_ = bf16[1024,512]{1,0:T(8,128)(2,1)S(1)} collective-permute-done((bf16[1024,512]{1,0:T(8,128)(2,1)}, bf16[1024,512]{1,0:T(8,128)(2,1)S(1)}, u32[]{:S(2)}, u32[]{:S(2)}) %collective-permute-start.19) | collective-permute-done | bytes 1048608 | tf_op jit(solution)/shard_map/ppermute | solution.py:320
  296.6 5.4 %terms.5 = bf16[2048,512]{1,0:T(8,128)(2,1)} custom-call(bf16[1024,2048]{1,0:T(8,128)(2,1)} %spread.7.weight_ref, bf16[1024,512]{1,0:T(8,128)(2,1)} %collective-permute-done.18.refs_0_, bf16[1024,512]{1,0:T(8,128)(2,1)S(1)} %collective-permute-done.19.refs_1_), custom_call_target="tpu_custom_call" | custom-call | flops 4000000000 | bytes 10000000 | tf_op jit(solution)/shard_map/terms/pallas_call | solution.py:219
  302.0 4.4 %all-to-all-start.7 = ((bf16[8,256,512]{2,1,0:T(8,128)(2,1)}), bf16[8,256,512]{2,1,0:T(8,128)(2,1)}, u32[]{:S(2)}, u32[]{:S(2)}) async-start(bf16[8,256,512]{2,1,0:T(8,128)(2,1)} %bitcast.81), calls=%async_computation.7 | async-start | bytes 4194304 | tf_op jit(solution)/shard_map/all_to_all | solution.py:323
  306.4 1.3 collective-permute-start.17
  307.7 26.2 %collective-permute-done.17.refs_1_ = bf16[1024,512]{1,0:T(8,128)(2,1)S(1)} collective-permute-done((bf16[1024,512]{1,0:T(8,128)(2,1)}, bf16[1024,512]{1,0:T(8,128)(2,1)S(1)}, u32[]{:S(2)}, u32[]{:S(2)}) %collective-permute-start.17) | collective-permute-done | bytes 1048608 | tf_op jit(solution)/shard_map/ppermute | solution.py:320
  333.9 5.4 %terms.4 = bf16[2048,512]{1,0:T(8,128)(2,1)} custom-call(bf16[1024,2048]{1,0:T(8,128)(2,1)} %spread.5.weight_ref, bf16[1024,512]{1,0:T(8,128)(2,1)} %collective-permute-done.16.refs_0_, bf16[1024,512]{1,0:T(8,128)(2,1)S(1)} %collective-permute-done.17.refs_1_), custom_call_target="tpu_custom_call" | custom-call | flops 4000000000 | bytes 10000000 | tf_op jit(solution)/shard_map/terms/pallas_call | solution.py:219
  339.3 4.4 %all-to-all-start.8 = ((bf16[8,256,512]{2,1,0:T(8,128)(2,1)}), bf16[8,256,512]{2,1,0:T(8,128)(2,1)}, u32[]{:S(2)}, u32[]{:S(2)}) async-start(bf16[8,256,512]{2,1,0:T(8,128)(2,1)} %bitcast.82), calls=%async_computation.8 | async-start | bytes 4194304 | tf_op jit(solution)/shard_map/all_to_all | solution.py:323
  343.7 16.9 %add_rows.2.refs_2_ = f32[2048,512]{1,0:T(8,128)} custom-call(s32[8,256]{1,0:T(8,128)S(1)} %reshape.136.refs_0_, s32[8,256]{1,0:T(8,128)S(1)} %reshape.137.refs_1_, s32[8,256]{1,0:T(8,128)S(1)} %reshape.138.refs_2_, bf16[2048,512]{1,0:T(8,128)(2,1)S(1)} %bitcast.67, bf16[2048,512]{1,0:T(8,128)(2,1)} %bitcast.30.refs_4_, bf16[2048,512]{1,0:T(8,128)(2,1)} %bitcast.32.refs_5_), custom_call_target="tpu_custom_call" | custom-call | flops 15000000512 | bytes 10000000 | tf_op jit(solution)/shard_map/add_rows/pallas_call | solution.py:258
  360.6 9.8 %all-to-all-done.8 = bf16[8,256,512]{2,1,0:T(8,128)(2,1)} async-done(((bf16[8,256,512]{2,1,0:T(8,128)(2,1)}), bf16[8,256,512]{2,1,0:T(8,128)(2,1)}, u32[]{:S(2)}, u32[]{:S(2)}) %all-to-all-start.8) | async-done | bytes 2097184 | tf_op jit(solution)/shard_map/all_to_all | solution.py:323
  370.4 8.4 %add_rows.3 = f32[2048,512]{1,0:T(8,128)} custom-call(s32[8,256]{1,0:T(8,128)S(1)} %copy-done.5, bf16[2048,512]{1,0:T(8,128)(2,1)} %bitcast.34.refs_1_, f32[2048,512]{1,0:T(8,128)} %add_rows.2.refs_2_), custom_call_target="tpu_custom_call" | custom-call | flops 5000000000 | bytes 10000000 | tf_op jit(solution)/shard_map/add_rows/pallas_call | solution.py:258
  (95 shorter events, 8.6 us)
Async XLA Ops:
  0.6 115.8 %copy-start = (bf16[768,512]{1,0:T(8,128)(2,1)S(1)}, bf16[768,512]{1,0:T(8,128)(2,1)}, u32[]{:S(2)}) copy-start(bf16[768,512]{1,0:T(8,128)(2,1)} %param.22) | copy-start | bytes 2359300
  0.6 0.8 copy-start.9
  3.4 14.5 %all-to-all-start = ((s32[32,1,256]{2,1,0:T(1,128)}), s32[32,1,256]{2,1,0:T(1,128)S(1)}, u32[]{:S(2)}, u32[]{:S(2)}) async-start(s32[32,1,256]{2,1,0:T(1,128)} %copy.33), calls=%async_computation | async-start | bytes 65536 | tf_op jit(solution)/shard_map/all_to_all | solution.py:326
  18.1 7.7 %copy-start.4 = (s32[8,256]{1,0:T(8,128)}, s32[8,256]{1,0:T(8,128)S(1)}, u32[]{:S(2)}) copy-start(s32[8,256]{1,0:T(8,128)S(1)} %reshape.134.refs_0_) | copy-start | bytes 24580
  18.2 7.6 %copy-start.10 = (bf16[1,32,32,768]{3,2,1,0:T(8,128)(2,1)S(1)}, bf16[1,32,32,768]{3,2,1,0:T(8,128)(2,1)}, u32[]{:S(2)}) copy-start(bf16[1,32,32,768]{3,2,1,0:T(8,128)(2,1)} %param.13) | copy-start | bytes 4718596
  25.8 1.0 copy-start.8
  28.2 43.5 %collective-permute-start = (bf16[1088,128]{1,0:T(8,128)(2,1)}, bf16[1088,128]{1,0:T(8,128)(2,1)}, u32[]{:S(2)}, u32[]{:S(2)}) collective-permute-start(bf16[1088,128]{1,0:T(8,128)(2,1)} %pad_maximum_fusion), channel_id=1, source_target_pairs={{0,6},{1,7},{6,0},{7,1},{2,4},{3,5},{4,2},{5,3},{8,14},{9,15},{14,... | collective-permute-start | bytes 835592 | tf_op jit(solution)/shard_map/ppermute | solution.py:320
  28.8 43.0 %collective-permute-start.1 = (bf16[1088,128]{1,0:T(8,128)(2,1)}, bf16[1088,128]{1,0:T(8,128)(2,1)}, u32[]{:S(2)}, u32[]{:S(2)}) collective-permute-start(bf16[1088,128]{1,0:T(8,128)(2,1)} %pad_maximum_fusion), channel_id=1, source_target_pairs={{0,4},{1,5},{4,0},{5,1},{2,6},{3,7},{6,2},{7,3},{8,12},{9,13},{12,... | collective-permute-start | bytes 835592 | tf_op jit(solution)/shard_map/ppermute | solution.py:320
  30.2 108.7 %collective-permute-start.4 = (bf16[1088,128]{1,0:T(8,128)(2,1)}, bf16[1088,128]{1,0:T(8,128)(2,1)}, u32[]{:S(2)}, u32[]{:S(2)}) collective-permute-start(bf16[1088,128]{1,0:T(8,128)(2,1)} %pad_maximum_fusion), channel_id=1, source_target_pairs={{0,2},{1,3},{2,0},{3,1},{4,6},{5,7},{6,4},{7,5},{8,10},{9,11},{10,... | collective-permute-start | bytes 835592 | tf_op jit(solution)/shard_map/ppermute | solution.py:320
  34.8 38.8 %all-to-all-start.1 = ((bf16[8,256,512]{2,1,0:T(8,128)(2,1)}), bf16[8,256,512]{2,1,0:T(8,128)(2,1)S(1)}, u32[]{:S(2)}, u32[]{:S(2)}) async-start(bf16[8,256,512]{2,1,0:T(8,128)(2,1)} %bitcast.8), calls=%async_computation.1 | async-start | bytes 4194304 | tf_op jit(solution)/shard_map/all_to_all | solution.py:323
  38.6 7.8 %copy-start.15 = (f32[3072]{0:T(1024)S(1)}, f32[3072]{0:T(1024)}, u32[]{:S(2)}) copy-start(f32[3072]{0:T(1024)} %param.17) | copy-start | bytes 36868
  38.6 7.8 %copy-start.16 = (f32[768]{0:T(1024)S(1)}, f32[768]{0:T(1024)}, u32[]{:S(2)}) copy-start(f32[768]{0:T(1024)} %param.19) | copy-start | bytes 9220
  38.6 7.8 %copy-start.17 = (f32[768]{0:T(1024)S(1)}, f32[768]{0:T(1024)}, u32[]{:S(2)}) copy-start(f32[768]{0:T(1024)} %param.15) | copy-start | bytes 9220
  38.6 7.8 %copy-start.18 = (f32[768]{0:T(1024)S(1)}, f32[768]{0:T(1024)}, u32[]{:S(2)}) copy-start(f32[768]{0:T(1024)} %param.14) | copy-start | bytes 9220
  63.7 7.7 %copy-start.12 = (f32[1024,768]{0,1:T(8,128)S(1)}, f32[1024,768]{0,1:T(8,128)}, u32[]{:S(2)}) copy-start(f32[1024,768]{0,1:T(8,128)} %get-tuple-element.69) | copy-start | bytes 9437188
  72.9 0.7 copy-start.13
  73.6 38.4 %all-to-all-start.2 = ((bf16[8,256,512]{2,1,0:T(8,128)(2,1)}), bf16[8,256,512]{2,1,0:T(8,128)(2,1)}, u32[]{:S(2)}, u32[]{:S(2)}) async-start(bf16[8,256,512]{2,1,0:T(8,128)(2,1)} %bitcast.10), calls=%async_computation.2 | async-start | bytes 4194304 | tf_op jit(solution)/shard_map/all_to_all | solution.py:323
  86.9 25.1 %collective-permute-start.2 = (bf16[1024,512]{1,0:T(8,128)(2,1)}, bf16[1024,512]{1,0:T(8,128)(2,1)S(1)}, u32[]{:S(2)}, u32[]{:S(2)}) collective-permute-start(bf16[1024,512]{1,0:T(8,128)(2,1)} %blend.4), channel_id=1, source_target_pairs={{0,2},{1,3},{6,4},{7,5},{8,10},{9,11},{14,12},{15,13},{16,18},{17,... | collective-permute-start | bytes 3145736 | tf_op jit(solution)/shard_map/ppermute | solution.py:320
  96.4 20.0 %copy-start.19 = (f32[768]{0:T(1024)S(1)}, f32[768]{0:T(1024)}, u32[]{:S(2)}) copy-start(f32[768]{0:T(1024)} %param.21) | copy-start | bytes 9220
  96.4 20.0 %copy-start.20 = (f32[768]{0:T(1024)S(1)}, f32[768]{0:T(1024)}, u32[]{:S(2)}) copy-start(f32[768]{0:T(1024)} %param.20) | copy-start | bytes 9220
  112.0 31.0 %all-to-all-start.3 = ((bf16[8,256,512]{2,1,0:T(8,128)(2,1)}), bf16[8,256,512]{2,1,0:T(8,128)(2,1)}, u32[]{:S(2)}, u32[]{:S(2)}) async-start(bf16[8,256,512]{2,1,0:T(8,128)(2,1)} %bitcast.12), calls=%async_computation.3 | async-start | bytes 4194304 | tf_op jit(solution)/shard_map/all_to_all | solution.py:323
  116.4 3.2 copy-start.14
  121.2 19.4 %collective-permute-start.3 = (bf16[1024,512]{1,0:T(8,128)(2,1)S(1)}, bf16[1024,512]{1,0:T(8,128)(2,1)S(1)}, u32[]{:S(2)}, u32[]{:S(2)}) collective-permute-start(bf16[1024,512]{1,0:T(8,128)(2,1)S(1)} %add.165), channel_id=1, source_target_pairs={{2,4},{3,5},{4,2},{5,3},{10,12},{11,13},{12,10},{13,11},{18,20},{1... | collective-permute-start | bytes 3145736 | tf_op jit(solution)/shard_map/ppermute | solution.py:320
  130.8 28.7 %collective-permute-start.6 = (bf16[1024,512]{1,0:T(8,128)(2,1)S(1)}, bf16[1024,512]{1,0:T(8,128)(2,1)}, u32[]{:S(2)}, u32[]{:S(2)}) collective-permute-start(bf16[1024,512]{1,0:T(8,128)(2,1)S(1)} %blend.6), channel_id=1, source_target_pairs={{0,2},{1,3},{6,4},{7,5},{8,10},{9,11},{14,12},{15,13},{16,18},{17,... | collective-permute-start | bytes 3145736 | tf_op jit(solution)/shard_map/ppermute | solution.py:320
  143.0 73.0 %all-to-all-start.4 = ((bf16[8,256,512]{2,1,0:T(8,128)(2,1)}), bf16[8,256,512]{2,1,0:T(8,128)(2,1)}, u32[]{:S(2)}, u32[]{:S(2)}) async-start(bf16[8,256,512]{2,1,0:T(8,128)(2,1)} %bitcast.14), calls=%async_computation.4 | async-start | bytes 4194304 | tf_op jit(solution)/shard_map/all_to_all | solution.py:323
  161.9 12.3 %copy-start.11 = (bf16[1024,512]{1,0:T(8,128)(2,1)S(1)}, bf16[1024,512]{1,0:T(8,128)(2,1)}, u32[]{:S(2)}) copy-start(bf16[1024,512]{1,0:T(8,128)(2,1)} %multiply_convert_fusion.2) | copy-start | bytes 3145732
  161.9 54.1 %collective-permute-start.7 = (bf16[1024,512]{1,0:T(8,128)(2,1)}, bf16[1024,512]{1,0:T(8,128)(2,1)}, u32[]{:S(2)}, u32[]{:S(2)}) collective-permute-start(bf16[1024,512]{1,0:T(8,128)(2,1)} %add.166), channel_id=1, source_target_pairs={{2,4},{3,5},{4,2},{5,3},{10,12},{11,13},{12,10},{13,11},{18,20},{1... | collective-permute-start | bytes 3145736 | tf_op jit(solution)/shard_map/ppermute | solution.py:320
  169.9 46.1 %collective-permute-start.5 = (bf16[1024,512]{1,0:T(8,128)(2,1)}, bf16[1024,512]{1,0:T(8,128)(2,1)S(1)}, u32[]{:S(2)}, u32[]{:S(2)}) collective-permute-start(bf16[1024,512]{1,0:T(8,128)(2,1)} %blend.5), channel_id=1, source_target_pairs={{0,2},{1,3},{2,0},{3,1},{4,6},{5,7},{6,4},{7,5},{8,10},{9,11},{10,... | collective-permute-start | bytes 3145736 | tf_op jit(solution)/shard_map/ppermute | solution.py:320
  174.3 29.0 %collective-permute-start.10 = (bf16[128,512]{1,0:T(8,128)(2,1)S(1)}, bf16[128,512]{1,0:T(8,128)(2,1)S(1)}, u32[]{:S(2)}, u32[]{:S(2)}) collective-permute-start(bf16[128,512]{1,0:T(8,128)(2,1)S(1)} %get-tuple-element.53), channel_id=1, source_target_pairs={{0,5},{1,6},{2,7},{3,0},{4,1},{5,2},{6,3},{7,4},{8,13},{9,14},{10,... | collective-permute-start | bytes 393224 | tf_op jit(solution)/shard_map/ppermute | solution.py:383
  174.4 29.0 %collective-permute-start.11 = (bf16[128,512]{1,0:T(8,128)(2,1)S(1)}, bf16[128,512]{1,0:T(8,128)(2,1)S(1)}, u32[]{:S(2)}, u32[]{:S(2)}) collective-permute-start(bf16[128,512]{1,0:T(8,128)(2,1)S(1)} %get-tuple-element.52), channel_id=1, source_target_pairs={{0,4},{1,5},{2,6},{3,7},{4,0},{5,1},{6,2},{7,3},{8,12},{9,13},{10,... | collective-permute-start | bytes 393224 | tf_op jit(solution)/shard_map/ppermute | solution.py:383
  175.6 29.7 %collective-permute-start.12 = (bf16[128,512]{1,0:T(8,128)(2,1)S(1)}, bf16[128,512]{1,0:T(8,128)(2,1)S(1)}, u32[]{:S(2)}, u32[]{:S(2)}) collective-permute-start(bf16[128,512]{1,0:T(8,128)(2,1)S(1)} %get-tuple-element.51), channel_id=1, source_target_pairs={{0,3},{1,4},{2,5},{3,6},{4,7},{5,0},{6,1},{7,2},{8,11},{9,12},{10,... | collective-permute-start | bytes 393224 | tf_op jit(solution)/shard_map/ppermute | solution.py:383
  203.3 7.7 %collective-permute-start.13 = (bf16[128,512]{1,0:T(8,128)(2,1)S(1)}, bf16[128,512]{1,0:T(8,128)(2,1)S(1)}, u32[]{:S(2)}, u32[]{:S(2)}) collective-permute-start(bf16[128,512]{1,0:T(8,128)(2,1)S(1)} %get-tuple-element.50), channel_id=1, source_target_pairs={{0,2},{1,3},{2,4},{3,5},{4,6},{5,7},{6,0},{7,1},{8,10},{9,11},{10,... | collective-permute-start | bytes 393224 | tf_op jit(solution)/shard_map/ppermute | solution.py:383
  203.3 11.3 %collective-permute-start.14 = (bf16[128,512]{1,0:T(8,128)(2,1)S(1)}, bf16[128,512]{1,0:T(8,128)(2,1)S(1)}, u32[]{:S(2)}, u32[]{:S(2)}) collective-permute-start(bf16[128,512]{1,0:T(8,128)(2,1)S(1)} %get-tuple-element.49), channel_id=1, source_target_pairs={{0,1},{1,2},{2,3},{3,4},{4,5},{5,6},{6,7},{7,0},{8,9},{9,10},{10,1... | collective-permute-start | bytes 393224 | tf_op jit(solution)/shard_map/ppermute | solution.py:383
  205.2 9.4 %collective-permute-start.8 = (bf16[128,512]{1,0:T(8,128)(2,1)S(1)}, bf16[128,512]{1,0:T(8,128)(2,1)S(1)}, u32[]{:S(2)}, u32[]{:S(2)}) collective-permute-start(bf16[128,512]{1,0:T(8,128)(2,1)S(1)} %get-tuple-element.55), channel_id=1, source_target_pairs={{0,7},{1,0},{2,1},{3,2},{4,3},{5,4},{6,5},{7,6},{8,15},{9,8},{10,9... | collective-permute-start | bytes 393224 | tf_op jit(solution)/shard_map/ppermute | solution.py:383
  211.0 5.0 %collective-permute-start.9 = (bf16[128,512]{1,0:T(8,128)(2,1)S(1)}, bf16[128,512]{1,0:T(8,128)(2,1)S(1)}, u32[]{:S(2)}, u32[]{:S(2)}) collective-permute-start(bf16[128,512]{1,0:T(8,128)(2,1)S(1)} %get-tuple-element.54), channel_id=1, source_target_pairs={{0,6},{1,7},{2,0},{3,1},{4,2},{5,3},{6,4},{7,5},{8,14},{9,15},{10,... | collective-permute-start | bytes 393224 | tf_op jit(solution)/shard_map/ppermute | solution.py:383
  222.8 4.6 %copy-start.7 = (bf16[1024,512]{1,0:T(8,128)(2,1)}, bf16[1024,512]{1,0:T(8,128)(2,1)S(1)}, u32[]{:S(2)}) copy-start(bf16[1024,512]{1,0:T(8,128)(2,1)S(1)} %get-tuple-element.41.refs_0_) | copy-start | bytes 3145732
  227.4 1.3 copy-start.3
  228.7 35.9 %all-to-all-start.5 = ((bf16[8,256,512]{2,1,0:T(8,128)(2,1)}), bf16[8,256,512]{2,1,0:T(8,128)(2,1)S(1)}, u32[]{:S(2)}, u32[]{:S(2)}) async-start(bf16[8,256,512]{2,1,0:T(8,128)(2,1)} %bitcast.70), calls=%async_computation.5 | async-start | bytes 4194304 | tf_op jit(solution)/shard_map/all_to_all | solution.py:323
  232.4 25.7 %collective-permute-start.15 = (bf16[1024,512]{1,0:T(8,128)(2,1)}, bf16[1024,512]{1,0:T(8,128)(2,1)S(1)}, u32[]{:S(2)}, u32[]{:S(2)}) collective-permute-start(bf16[1024,512]{1,0:T(8,128)(2,1)} %copy-done.7), channel_id=1, source_target_pairs={{0,2},{1,3},{2,0},{3,1},{4,6},{5,7},{6,4},{7,5},{8,10},{9,11},{10,... | collective-permute-start | bytes 3145736 | tf_op jit(solution)/shard_map/ppermute | solution.py:320
  233.1 36.0 %collective-permute-start.18 = (bf16[1024,512]{1,0:T(8,128)(2,1)}, bf16[1024,512]{1,0:T(8,128)(2,1)}, u32[]{:S(2)}, u32[]{:S(2)}) collective-permute-start(bf16[1024,512]{1,0:T(8,128)(2,1)} %copy-done.7), channel_id=1, source_target_pairs={{2,4},{3,5},{4,2},{5,3},{10,12},{11,13},{12,10},{13,11},{18,20},{1... | collective-permute-start | bytes 3145736 | tf_op jit(solution)/shard_map/ppermute | solution.py:320
  262.2 1.4 copy-start.2
  263.6 1.0 copy-start.6
  264.7 37.3 %all-to-all-start.6 = ((bf16[8,256,512]{2,1,0:T(8,128)(2,1)}), bf16[8,256,512]{2,1,0:T(8,128)(2,1)}, u32[]{:S(2)}, u32[]{:S(2)}) async-start(bf16[8,256,512]{2,1,0:T(8,128)(2,1)} %bitcast.69), calls=%async_computation.6 | async-start | bytes 4194304 | tf_op jit(solution)/shard_map/all_to_all | solution.py:323
  269.1 27.5 %collective-permute-start.19 = (bf16[1024,512]{1,0:T(8,128)(2,1)}, bf16[1024,512]{1,0:T(8,128)(2,1)S(1)}, u32[]{:S(2)}, u32[]{:S(2)}) collective-permute-start(bf16[1024,512]{1,0:T(8,128)(2,1)} %collective-permute-done.18.refs_0_), channel_id=1, source_target_pairs={{2,0},{3,1},{4,6},{5,7},{10,8},{11,9},{12,14},{13,15},{18,16},{19,... | collective-permute-start | bytes 3145736 | tf_op jit(solution)/shard_map/ppermute | solution.py:320
  270.4 36.0 %collective-permute-start.16 = (bf16[1024,512]{1,0:T(8,128)(2,1)}, bf16[1024,512]{1,0:T(8,128)(2,1)}, u32[]{:S(2)}, u32[]{:S(2)}) collective-permute-start(bf16[1024,512]{1,0:T(8,128)(2,1)} %copy-done.6), channel_id=1, source_target_pairs={{2,4},{3,5},{4,2},{5,3},{10,12},{11,13},{12,10},{13,11},{18,20},{1... | collective-permute-start | bytes 3145736 | tf_op jit(solution)/shard_map/ppermute | solution.py:320
  302.0 37.3 %all-to-all-start.7 = ((bf16[8,256,512]{2,1,0:T(8,128)(2,1)}), bf16[8,256,512]{2,1,0:T(8,128)(2,1)}, u32[]{:S(2)}, u32[]{:S(2)}) async-start(bf16[8,256,512]{2,1,0:T(8,128)(2,1)} %bitcast.81), calls=%async_computation.7 | async-start | bytes 4194304 | tf_op jit(solution)/shard_map/all_to_all | solution.py:323
  306.4 27.5 %collective-permute-start.17 = (bf16[1024,512]{1,0:T(8,128)(2,1)}, bf16[1024,512]{1,0:T(8,128)(2,1)S(1)}, u32[]{:S(2)}, u32[]{:S(2)}) collective-permute-start(bf16[1024,512]{1,0:T(8,128)(2,1)} %collective-permute-done.16.refs_0_), channel_id=1, source_target_pairs={{2,0},{3,1},{4,6},{5,7},{10,8},{11,9},{12,14},{13,15},{18,16},{19,... | collective-permute-start | bytes 3145736 | tf_op jit(solution)/shard_map/ppermute | solution.py:320
  339.3 31.0 %all-to-all-start.8 = ((bf16[8,256,512]{2,1,0:T(8,128)(2,1)}), bf16[8,256,512]{2,1,0:T(8,128)(2,1)}, u32[]{:S(2)}, u32[]{:S(2)}) async-start(bf16[8,256,512]{2,1,0:T(8,128)(2,1)} %bitcast.82), calls=%async_computation.8 | async-start | bytes 4194304 | tf_op jit(solution)/shard_map/all_to_all | solution.py:323
  343.7 26.7 %copy-start.5 = (s32[8,256]{1,0:T(8,128)S(1)}, s32[8,256]{1,0:T(8,128)}, u32[]{:S(2)}) copy-start(s32[8,256]{1,0:T(8,128)} %copy-done.4) | copy-start | bytes 24580
  370.4 8.4 %copy-start.1 = (bf16[768,512]{1,0:T(8,128)(2,1)S(1)}, bf16[768,512]{1,0:T(8,128)(2,1)}, u32[]{:S(2)}) copy-start(bf16[768,512]{1,0:T(8,128)(2,1)} %param.22) | copy-start | bytes 2359300
